TPU v7x, 512 devices: a whole 4x8x8 slice. The times are simulated.
512 devices in a mesh: exp: 64 (over y, z), ten: 8 (over x, core).
Axes of the slice: x: 4, y: 8, z: 8, core: 2. Of those that a mesh axis runs over, the one named last changes fastest.
Arguments:
- tokens: bfloat16 [12288, 4096], P('exp', 'ten'), may hold values from -6 to 6
- output_grad: bfloat16 [12288, 4096], P('exp', 'ten'), may hold values from -3 to 3
- gate_weight: bfloat16 [64, 4096, 1024], P('exp', None, 'ten'), may hold values from -0.09375 to 0.09375
- up_weight: bfloat16 [64, 4096, 1024], P('exp', None, 'ten'), may hold values from -0.09375 to 0.09375
- down_weight: bfloat16 [64, 1024, 4096], P('exp', 'ten'), may hold values from -0.0625 to 0.0625
- chosen: int32 [8, 384], replicated, may hold values from 0 to 12287, as said below
- gate_values: float32 [8, 384], replicated, may hold values from 0.1 to 1
Outputs:
- grad_tokens: bfloat16 [12288, 4096], P('exp', 'ten')
- gate_grad: float32 [8, 384], replicated
Inputs may be any that keep to these rules, and one draw needn't show every extreme that they name: `chosen`: each row names 384 different tokens. Of the block of 192 tokens held by one index of exp, a row names at most 8, and in every row exactly 8 for some index.
All inputs are finite; a program needn't handle non-finite values.
Results may differ from a plain program's by a relative error of at most 0.019.
Values may be sent and summed in bfloat16 or wider, within the bound.
No kernel may reach another device: no remote copies, remote signals or barrier semaphores. Data moves between devices by JAX's collectives and lax.ppermute only.
A program may use at most 64 MiB of HBM per device.

v0:
```python
import jax
import jax.numpy as jnp
from jax import lax
from jax.sharding import PartitionSpec as P


def silu_parts(values):
    sig = jax.nn.sigmoid(values)
    return (values * sig, sig * (1.0 + values * (1.0 - sig)))


def on_device(tokens, output_grad, gate_weight, up_weight, down_weight, chosen, gate_values):
    exp_count = lax.axis_size("exp")
    exp_index = lax.axis_index("exp")
    expert_count, capacity = chosen.shape
    group_size = exp_count // expert_count
    expert = exp_index // group_size
    token_rows = tokens.shape[0]
    share_mean = capacity // exp_count
    slot_count = share_mean + share_mean // 3
    all_slots = exp_count * slot_count
    gate_local = gate_weight[0]
    up_local = up_weight[0]
    down_local = down_weight[0]
    contract = (((1,), (1,)), ((), ()))
    source = chosen // token_rows
    peer_ids = jnp.arange(exp_count, dtype=jnp.int32)
    peer_hits = (source[:, :, None] == peer_ids[None, None, :]).astype(jnp.int32)
    running = jnp.cumsum(peer_hits, axis=1)
    slot_rank = jnp.sum(running * peer_hits, axis=2) - 1
    slot_ids = jnp.arange(slot_count, dtype=jnp.int32)
    mine_mask = (source == exp_index)[:, None, :] & (
        slot_rank[:, None, :] == slot_ids[None, :, None]
    )
    local_rows = chosen - exp_index * token_rows
    send_row = jnp.sum(jnp.where(mine_mask, local_rows[:, None, :], 0), axis=2)
    send_live = jnp.any(mine_mask, axis=2)
    send_row_all = jnp.repeat(send_row, group_size, axis=0).reshape(-1)
    send_live_all = jnp.repeat(send_live, group_size, axis=0).reshape(-1)
    full_tokens, full_grads = (
        lax.all_gather(tokens, "ten", axis=1, tiled=True),
        lax.all_gather(output_grad, "ten", axis=1, tiled=True),
    )
    picked_rows = jnp.where(
        send_live_all[:, None], full_tokens[send_row_all], jnp.zeros((), tokens.dtype)
    )
    picked_grads = jnp.where(
        send_live_all[:, None], full_grads[send_row_all], jnp.zeros((), output_grad.dtype)
    )
    got_rows, got_grads = (
        lax.all_to_all(picked_rows, "exp", split_axis=0, concat_axis=0, tiled=True),
        lax.all_to_all(picked_grads, "exp", split_axis=0, concat_axis=0, tiled=True),
    )
    my_source = lax.dynamic_index_in_dim(source, expert, 0, keepdims=False)
    my_rank = lax.dynamic_index_in_dim(slot_rank, expert, 0, keepdims=False)
    my_gates = lax.dynamic_index_in_dim(gate_values, expert, 0, keepdims=False)
    position = my_source * slot_count + my_rank
    row_gate = jnp.zeros((all_slots,), jnp.float32).at[position].set(my_gates)
    pre_gate = jnp.dot(got_rows, gate_local, preferred_element_type=jnp.float32)
    pre_up = jnp.dot(got_rows, up_local, preferred_element_type=jnp.float32)
    back = lax.dot_general(got_grads, down_local, contract, preferred_element_type=jnp.float32)
    active, slope = silu_parts(pre_gate)
    gate_part = jnp.sum(active * pre_up * back, axis=1)
    scaled = row_gate[:, None] * back
    gate_delta = (scaled * pre_up * slope).astype(jnp.bfloat16)
    up_delta = (scaled * active).astype(jnp.bfloat16)
    gate_rows_sum = gate_part[position]
    gate_table = jnp.zeros((expert_count, capacity), jnp.float32)
    gate_table = lax.dynamic_update_slice_in_dim(gate_table, gate_rows_sum[None, :], expert, 0)
    gate_grad = lax.psum(gate_table, ("exp", "ten"))
    token_ids = jnp.arange(token_rows, dtype=jnp.int32)
    owner_onehot = (send_row_all[:, None] == token_ids[None, :]) & send_live_all[:, None]
    column_sum = lax.dot_general(
        gate_local, gate_delta, contract, preferred_element_type=jnp.float32
    )
    summed = lax.psum_scatter(
        (
            column_sum
            + lax.dot_general(up_local, up_delta, contract, preferred_element_type=jnp.float32)
        ).astype(jnp.bfloat16),
        "ten",
        scatter_dimension=0,
        tiled=True,
    ).astype(jnp.float32)
    back_sums = lax.all_to_all(
        summed.astype(jnp.bfloat16), "exp", split_axis=1, concat_axis=1, tiled=True
    ).astype(summed.dtype)
    grad_tokens = lax.dot_general(
        owner_onehot.astype(jnp.float32),
        back_sums,
        (((0,), (1,)), ((), ())),
        precision=lax.Precision.HIGHEST,
        preferred_element_type=jnp.float32,
    )
    return (grad_tokens.astype(jnp.bfloat16), gate_grad)


def solution(mesh):
    in_specs = (
        P("exp", "ten"),
        P("exp", "ten"),
        P("exp", None, "ten"),
        P("exp", None, "ten"),
        P("exp", "ten", None),
        P(),
        P(),
    )
    out_specs = (P("exp", "ten"), P())
    return jax.shard_map(
        on_device, mesh=mesh, in_specs=in_specs, out_specs=out_specs, check_vma=False
    )
```

profile of v0, /device:TPU:1, one launch (start us, length us, event | category | flops | bytes accessed | tf_op | source)
XLA Modules:
  0.0 527.9 jit_solution(6173108992639356255)
XLA Ops:
  7.2 0.0 copy-start
  7.2 0.0 copy-start.3
  7.2 0.0 all-gather.5.cloned.1.call-start
  7.2 0.7 all-gather.5.cloned.1.call-update
  7.9 0.0 all-gather.3.cloned.1.call-start
  8.0 0.7 all-gather.3.cloned.1.call-update
  8.7 0.7 broadcast_compare_fusion
  9.4 0.1 fusion.15
  9.5 7.2 %reduce-window.6 = s32[8,64,3,128]{3,1,2,0:T(8,128)S(1)} reduce-window(s32[8,64,3,128]{3,1,2,0:T(8,128)S(1)} %fusion.15, s32[]{:T(128)} %constant.52.clone.1), window={size=1x1x1x128 pad=0_0x0_0x0_0x127_0}, to_apply=%region_0.1 | reduce-window | flops 24969216 | bytes 1572868 | tf_op jit(solution)/shard_map/reduce-window
  16.7 0.3 slice.14
  16.9 0.3 copy.15
  17.2 0.1 fusion.28
  17.3 0.3 fusion.14
  17.6 0.0 copy-done.3
  17.7 0.2 select_reduce_fusion
  17.9 0.1 reshape_reshape.3
  18.0 0.2 fusion.26
  18.2 27.5 %all-gather.5.cloned.1.call-done = bf16[192,4096]{1,0:T(8,128)(2,1)} async-done(((bf16[192,512]{1,0:T(8,128)(2,1)}), bf16[192,4096]{1,0:T(8,128)(2,1)}) %all-gather.5.cloned.1.call-update) | async-done | bytes 1572880 | tf_op jit(solution)/shard_map/all_gather | solution.py:41
  45.7 10.2 %gather_fusion.1 = bf16[512,4096]{1,0:T(8,128)(2,1)} fusion(bf16[192,4096]{1,0:T(8,128)(2,1)} %all-gather.5.cloned.1.call-done, s32[1024]{0:T(1024)S(1)} %pad_clamp_fusion.1), kind=kCustom, calls=%fused_computation.1 | custom fusion | bytes 8390656 | tf_op jit(solution)/shard_map/gather | solution.py:45
  56.0 22.0 %all-gather.3.cloned.1.call-done = bf16[192,4096]{1,0:T(8,128)(2,1)} async-done(((bf16[192,512]{1,0:T(8,128)(2,1)}), bf16[192,4096]{1,0:T(8,128)(2,1)}) %all-gather.3.cloned.1.call-update) | async-done | bytes 1572880 | tf_op jit(solution)/shard_map/all_gather | solution.py:42
  78.0 10.2 %gather_fusion = bf16[512,4096]{1,0:T(8,128)(2,1)} fusion(bf16[192,4096]{1,0:T(8,128)(2,1)} %all-gather.3.cloned.1.call-done, s32[1024]{0:T(1024)S(1)} %pad_clamp_fusion.1), kind=kCustom, calls=%fused_computation | custom fusion | bytes 8390656 | tf_op jit(solution)/shard_map/gather | solution.py:48
  88.2 5.1 bitcast_select_fusion.1
  93.3 110.9 %all_to_all.30 = bf16[64,8,4096]{2,1,0:T(8,128)(2,1)} all-to-all(bf16[64,8,4096]{2,1,0:T(8,128)(2,1)S(1)} %get-tuple-element.5), channel_id=1, replica_groups=mesh['exp'=64,'ten'=8] {'exp'}, dimensions={0} | all-to-all | bytes 8388608 | tf_op jit(solution)/shard_map/all_to_all | solution.py:51
  204.2 24.8 %all-to-all-start = ((bf16[64,8,4096]{2,1,0:T(8,128)(2,1)}), bf16[64,8,4096]{2,1,0:T(8,128)(2,1)}, u32[]{:S(2)}, u32[]{:S(2)}) async-start(bf16[64,8,4096]{2,1,0:T(8,128)(2,1)} %get-tuple-element.4), calls=%async_computation | async-start | bytes 8388608 | tf_op jit(solution)/shard_map/all_to_all | solution.py:52
  229.0 0.0 copy-start.2
  229.0 0.2 reduce-scatter.2.cloned.1.call-start
  229.3 0.8 dynamic-slice_reduce_fusion
  230.1 2.9 scatter_custom_fusion
  233.0 0.0 copy-done
  233.0 0.0 copy-start.1
  233.0 3.8 fusion.1
  236.9 0.0 copy-done.2
  236.9 0.0 copy-done.1
  236.9 1.5 fusion.3
  238.4 107.0 %all-to-all-done = bf16[64,8,4096]{2,1,0:T(8,128)(2,1)} async-done(((bf16[64,8,4096]{2,1,0:T(8,128)(2,1)}), bf16[64,8,4096]{2,1,0:T(8,128)(2,1)}, u32[]{:S(2)}, u32[]{:S(2)}) %all-to-all-start) | async-done | bytes 4194336 | tf_op jit(solution)/shard_map/all_to_all | solution.py:52
  345.5 4.0 multiply_reduce_fusion
  349.5 1.3 fusion.7
  350.9 3.3 fusion
  354.1 0.0 reduce-scatter.2.cloned.1.call-update
  354.2 49.5 %reduce-scatter.2.cloned.1.call-done = bf16[512,512]{0,1:T(8,128)(2,1)} async-done(((bf16[4096,512]{0,1:T(8,128)(2,1)}), bf16[512,512]{0,1:T(8,128)(2,1)}) %reduce-scatter.2.cloned.1.call-update) | async-done | bytes 524304 | tf_op jit(solution)/shard_map/reduce_scatter | solution.py:76
  403.6 12.3 %all-to-all-start.2 = ((bf16[512,64,8]{0,2,1:T(8,128)(2,1)}), bf16[512,64,8]{0,2,1:T(8,128)(2,1)S(1)}, u32[]{:S(2)}, u32[]{:S(2)}) async-start(bf16[512,64,8]{0,2,1:T(8,128)(2,1)} %bitcast.60), calls=%async_computation.3 | async-start | bytes 1048576 | tf_op jit(solution)/shard_map/all_to_all | solution.py:85
  415.9 0.1 eq.69
  416.0 0.1 and.31
  416.1 2.8 gather_fusion.2
  418.9 0.1 dynamic_update_slice.3
  419.0 101.1 %psum.7 = f32[8,384]{1,0:T(8,128)} all-reduce(f32[8,384]{1,0:T(8,128)S(1)} %dynamic_update_slice.3), channel_id=1, replica_groups=mesh['exp'=64,'ten'=8] {'exp','ten'}, use_global_device_ids=true, to_apply=%region_8.9 | all-reduce | flops 3072 | bytes 24576 | tf_op jit(solution)/shard_map/psum | solution.py:70
  520.1 0.0 all-to-all-done.2
  520.1 1.2 convolution_convert_fusion
  (13 shorter events, 0.1 us)
Async XLA Ops:
  7.2 225.9 %copy-start = (bf16[1,4096,128]{2,1,0:T(8,128)(2,1)S(1)}, bf16[1,4096,128]{2,1,0:T(8,128)(2,1)}, u32[]{:S(2)}) copy-start(bf16[1,4096,128]{2,1,0:T(8,128)(2,1)} %param.9) | copy-start | bytes 3145732
  7.2 10.5 %copy-start.3 = (s32[8,384]{1,0:T(8,128)S(1)}, s32[8,384]{1,0:T(8,128)}, u32[]{:S(2)}) copy-start(s32[8,384]{1,0:T(8,128)} %param.12) | copy-start | bytes 36868
  7.2 38.5 %all-gather.5.cloned.1.call-start = ((), (), s32[]{:S(2)}) async-start(), calls=%async_computation.5 | async-start | bytes 1769472 | tf_op jit(solution)/shard_map/all_gather | solution.py:41
  7.9 70.1 %all-gather.3.cloned.1.call-start = ((), (), s32[]{:S(2)}) async-start(), calls=%async_computation.4 | async-start | bytes 1769472 | tf_op jit(solution)/shard_map/all_gather | solution.py:42
  204.2 141.3 %all-to-all-start = ((bf16[64,8,4096]{2,1,0:T(8,128)(2,1)}), bf16[64,8,4096]{2,1,0:T(8,128)(2,1)}, u32[]{:S(2)}, u32[]{:S(2)}) async-start(bf16[64,8,4096]{2,1,0:T(8,128)(2,1)} %get-tuple-element.4), calls=%async_computation | async-start | bytes 8388608 | tf_op jit(solution)/shard_map/all_to_all | solution.py:52
  229.0 7.9 %copy-start.2 = (bf16[1,4096,128]{2,1,0:T(8,128)(2,1)S(1)}, bf16[1,4096,128]{2,1,0:T(8,128)(2,1)}, u32[]{:S(2)}) copy-start(bf16[1,4096,128]{2,1,0:T(8,128)(2,1)} %param.10) | copy-start | bytes 3145732
  229.0 174.6 %reduce-scatter.2.cloned.1.call-start = ((), (), s32[]{:S(2)}) async-start(), calls=%async_computation.6 | async-start | bytes 4718592 | tf_op jit(solution)/shard_map/reduce_scatter | solution.py:76
  233.0 3.9 copy-start.1
  403.6 116.5 %all-to-all-start.2 = ((bf16[512,64,8]{0,2,1:T(8,128)(2,1)}), bf16[512,64,8]{0,2,1:T(8,128)(2,1)S(1)}, u32[]{:S(2)}, u32[]{:S(2)}) async-start(bf16[512,64,8]{0,2,1:T(8,128)(2,1)} %bitcast.60), calls=%async_computation.3 | async-start | bytes 1048576 | tf_op jit(solution)/shard_map/all_to_all | solution.py:85
Sparse Core Ops, SparseCore 0:
  10.2 35.5 all-gather.4
  47.9 30.0 all-gather.2
  354.3 49.3 reduce-scatter.1
where the time goes:
time: 528 us
  blocking collectives  212 us (40%)
  waiting for transfers between devices  207 us (39%)
  starting transfers between devices  37.4 us (7%)
  local copies, waits for them, and re-layouts  27.8 us (5%)
  matrix products  15.2 us (3%)
  between operations  14 us (3%)
  other arithmetic  13.9 us (3%)
    all_to_all x1, blocking collectives, on_device(): lax.all_to_all(picked_rows, 'exp', split_axis=0, concat_axis=0, tiled=True)  111 us
    all_to_all x1, waiting for transfers between devices, on_device(): lax.all_to_all(picked_grads, 'exp', split_axis=0, concat_axis=0, tiled=True)  107 us
    psum x1, blocking collectives, on_device(): gate_grad = lax.psum(gate_table, ('exp', 'ten'))  101 us
    reduce_scatter x1, waiting for transfers between devices, on_device(): lax.psum_scatter((column_sum + lax.dot_general(up_local, up_delta, contra...  49.5 us
    all_gather x1, waiting for transfers between devices, on_device(): lax.all_gather(tokens, 'ten', axis=1, tiled=True)  27.5 us
    all_to_all x1, starting transfers between devices, on_device(): lax.all_to_all(picked_grads, 'exp', split_axis=0, concat_axis=0, tiled=True)  24.8 us
    all_gather x1, waiting for transfers between devices, on_device(): lax.all_gather(output_grad, 'ten', axis=1, tiled=True)  22 us
    all_to_all x1, starting transfers between devices, on_device(): lax.all_to_all(summed.astype(jnp.bfloat16), 'exp', split_axis=1, concat_a...  12.3 us
  transfers between devices with their start and end apart: 5, of which 4 were waited for; matrix products, arithmetic and copies ran while one was open for 6% of the time, Pallas kernels for 0%

commit v1 on v0

v1 whole, which is shorter than its diff:
```python
import jax
import jax.numpy as jnp
import numpy as np
from jax import lax
from jax.sharding import Mesh
from jax.sharding import PartitionSpec as P

NY, NZ, NX, NC = 8, 8, 4, 2
SLOTS = 8
BF = jnp.bfloat16
F32 = jnp.float32


def silu_parts(values):
    sig = jax.nn.sigmoid(values)
    return (values * sig, sig * (1.0 + values * (1.0 - sig)))


def swap_cores(a):
    return lax.ppermute(a, "c", [(0, 1), (1, 0)])


def shift_x(a, k):
    return lax.ppermute(a, "x", [(j, (j + k) % NX) for j in range(NX)])


def hi_lo(values):
    hi = values.astype(BF)
    lo = (values - hi.astype(F32)).astype(BF)
    return hi, lo


def on_device(tokens, output_grad, gate_weight, up_weight, down_weight, chosen, gate_values):
    expert = lax.axis_index("y")
    exp_index = expert * NZ + lax.axis_index("z")
    x_index = lax.axis_index("x")
    c_index = lax.axis_index("c")
    expert_count, capacity = chosen.shape
    token_rows, feat = tokens.shape
    hid = gate_weight.shape[2]
    peers = NY * NZ
    all_slots = peers * SLOTS
    wide = NC * feat

    source = chosen // token_rows
    local_rows = chosen - exp_index * token_rows
    mine = source == exp_index
    order = jnp.arange(capacity, dtype=jnp.int32)
    earlier = (order[:, None] < order[None, :]).astype(BF)
    rank = jnp.dot(mine.astype(BF), earlier, preferred_element_type=F32).astype(jnp.int32)
    slot_ids = jnp.arange(SLOTS, dtype=jnp.int32)
    hit = mine[:, None, :] & (rank[:, None, :] == slot_ids[None, :, None])
    send_row = jnp.sum(jnp.where(hit, local_rows[:, None, :] + 1, 0), axis=2) - 1
    token_ids = jnp.arange(token_rows, dtype=jnp.int32)
    pick = (send_row.reshape(-1)[:, None] == token_ids[None, :]).astype(BF)
    both = jnp.concatenate([tokens, output_grad], axis=1)
    picked = jnp.dot(pick, both, preferred_element_type=F32).astype(BF)
    outgoing = jnp.broadcast_to(
        picked.reshape(expert_count, 1, SLOTS, 2 * feat), (expert_count, NZ, SLOTS, 2 * feat)
    ).reshape(all_slots, 2 * feat)
    got = lax.all_to_all(outgoing, ("y", "z"), split_axis=0, concat_axis=0, tiled=True)

    gate_local = gate_weight[0]
    up_local = up_weight[0]
    down_local = down_weight[0]
    gu_all = jnp.zeros((NX, wide, 2 * hid), BF)
    down_all = jnp.zeros((NX, hid, wide), BF)
    for k in (1, 3, 2, 0):
        dest = (x_index + k) % NX
        g = lax.dynamic_slice_in_dim(gate_local, dest * wide, wide, 0)
        u = lax.dynamic_slice_in_dim(up_local, dest * wide, wide, 0)
        d = lax.dynamic_slice_in_dim(down_local, dest * wide, wide, 1)
        gu = jnp.concatenate([g, u], axis=1)
        if k:
            gu, d = shift_x(gu, k), shift_x(d, k)
        origin = (x_index - k) % NX
        gu_all = lax.dynamic_update_slice_in_dim(gu_all, gu[None], origin, 0)
        down_all = lax.dynamic_update_slice_in_dim(down_all, d[None], origin, 0)
    gu_cat = gu_all.transpose(1, 0, 2).reshape(wide, NX * 2 * hid)
    down_cat = down_all.reshape(NX * hid, wide)

    my_source = lax.dynamic_index_in_dim(source, expert, 0, keepdims=False)
    my_gates = lax.dynamic_index_in_dim(gate_values, expert, 0, keepdims=False)
    same = (my_source[:, None] == my_source[None, :]) & (order[None, :] < order[:, None])
    my_rank = jnp.sum(same.astype(jnp.int32), axis=1)
    my_slot = my_source * SLOTS + my_rank
    place = (my_slot[:, None] == jnp.arange(all_slots, dtype=jnp.int32)[None, :]).astype(BF)
    own = jnp.dot(place, got, preferred_element_type=F32).astype(BF)
    other = swap_cores(own)
    first = c_index == 0
    low, high = jnp.where(first, own, other), jnp.where(first, other, own)
    rows_in = jnp.concatenate([low[:, :feat], high[:, :feat]], axis=1)
    grads_in = jnp.concatenate([low[:, feat:], high[:, feat:]], axis=1)

    contract = (((1,), (1,)), ((), ()))
    pre_gu = jnp.dot(rows_in, gu_cat, preferred_element_type=F32).astype(BF)
    back = lax.dot_general(grads_in, down_cat, contract, preferred_element_type=F32).astype(BF)
    parts = jnp.stack(
        [
            jnp.concatenate(
                [pre_gu[:, j * 2 * hid : (j + 1) * 2 * hid], back[:, j * hid : (j + 1) * hid]], axis=1
            )
            for j in range(NX)
        ]
    )
    parts = lax.all_to_all(parts, "x", split_axis=0, concat_axis=0, tiled=True)
    sums = jnp.sum(parts.astype(F32), axis=0)
    pre_gate, pre_up, back = sums[:, :hid], sums[:, hid : 2 * hid], sums[:, 2 * hid :]
    active, slope = silu_parts(pre_gate)
    gate_part = jnp.sum(active * pre_up * back, axis=1)
    scaled = my_gates[:, None] * back
    gate_delta = (scaled * pre_up * slope).astype(BF)
    up_delta = (scaled * active).astype(BF)
    hi, lo = hi_lo(gate_part)
    extra = jnp.concatenate([hi, lo, jnp.zeros((16 * 2 * hid - 2 * capacity,), BF)]).reshape(16, 2 * hid)
    deltas = jnp.concatenate([jnp.concatenate([gate_delta, up_delta], axis=1), extra], axis=0)
    deltas = lax.all_gather(deltas, "x", axis=0, tiled=False)
    gate_rows = deltas[:, capacity:].reshape(NX, -1).astype(F32)
    gate_sum = jnp.sum(gate_rows[:, :capacity] + gate_rows[:, capacity : 2 * capacity], axis=0)
    delta_cat = deltas[:, :capacity].transpose(1, 0, 2).reshape(capacity, NX * 2 * hid)
    term = lax.dot_general(delta_cat, gu_cat, contract, preferred_element_type=F32)
    hi, lo = hi_lo(gate_sum)
    extra = jnp.concatenate([hi, lo, jnp.zeros((16 * feat - 2 * capacity,), BF)]).reshape(16, feat)
    keep, give = jnp.where(first, term[:, :feat], term[:, feat:]), jnp.where(first, term[:, feat:], term[:, :feat])
    came = swap_cores(jnp.concatenate([give.astype(BF), extra], axis=0))
    term = (keep + came[:capacity].astype(F32)).astype(BF)
    came_gate = came[capacity:].reshape(-1).astype(F32)
    gate_sum = (hi.astype(F32) + lo.astype(F32)) + (came_gate[:capacity] + came_gate[capacity : 2 * capacity])
    hi, lo = hi_lo(gate_sum)
    gate_block = jnp.concatenate([hi, lo, jnp.zeros((SLOTS * 128 - 2 * capacity,), BF)]).reshape(1, SLOTS, 128)
    gate_block = jnp.broadcast_to(gate_block, (peers, SLOTS, 128)).reshape(all_slots, 128)
    spread = lax.dot_general(place, term, (((0,), (0,)), ((), ())), preferred_element_type=F32).astype(BF)
    home = lax.all_to_all(
        jnp.concatenate([spread, gate_block], axis=1), ("y", "z"), split_axis=0, concat_axis=0, tiled=True
    )
    owner = jnp.broadcast_to(
        pick.reshape(expert_count, 1, SLOTS, token_rows), (expert_count, NZ, SLOTS, token_rows)
    ).reshape(all_slots, token_rows)
    grad_tokens = lax.dot_general(
        owner, home[:, :feat], (((0,), (0,)), ((), ())), preferred_element_type=F32
    ).astype(BF)
    gates = jnp.sum(home[:, feat:].reshape(expert_count, NZ, SLOTS * 128).astype(F32), axis=1)
    gate_grad = gates[:, :capacity] + gates[:, capacity : 2 * capacity]
    return grad_tokens, gate_grad


def solution(mesh):
    grid = Mesh(np.asarray(mesh.devices).reshape(NY, NZ, NX, NC), ("y", "z", "x", "c"))
    exp, ten = ("y", "z"), ("x", "c")
    in_specs = (
        P(exp, ten),
        P(exp, ten),
        P(exp, None, ten),
        P(exp, None, ten),
        P(exp, ten, None),
        P(),
        P(),
    )
    out_specs = (P(exp, ten), P())
    return jax.shard_map(on_device, mesh=grid, in_specs=in_specs, out_specs=out_specs, check_vma=False)
```

time: 528 us -> 167 us (0.32)
  the two profiles are of different devices: /device:TPU:1 before, /device:TPU:16 now
where the time goes in v1:
time: 167 us; the launch traced here: 166 us
  starting transfers between devices  57.5 us (34%)
  waiting for transfers between devices  56.4 us (34%)
  local copies, waits for them, and re-layouts  17.1 us (10%)
  blocking collectives  14 us (8%)
  matrix products  9.89 us (6%)
  other arithmetic  9.57 us (6%)
    all_to_all x1, waiting for transfers between devices, on_device(): lax.all_to_all(jnp.concatenate([spread, gate_block], axis=1), ('y', 'z'),...  22.4 us
    ppermute x6, starting transfers between devices, shift_x(): return lax.ppermute(a, 'x', [(j, (j + k) % NX) for j in range(NX)])  21 us
    all_to_all x1, waiting for transfers between devices, on_device(): parts = lax.all_to_all(parts, 'x', split_axis=0, concat_axis=0, tiled=True)  17.4 us
    all_to_all x1, starting transfers between devices, on_device(): lax.all_to_all(outgoing, ('y', 'z'), split_axis=0, concat_axis=0, tiled=T...  16.5 us
    ppermute x6, waiting for transfers between devices, shift_x(): return lax.ppermute(a, 'x', [(j, (j + k) % NX) for j in range(NX)])  15 us
    all_gather x1, blocking collectives, on_device(): deltas = lax.all_gather(deltas, 'x', axis=0, tiled=False)  14 us
    all_to_all x1, starting transfers between devices, on_device(): lax.all_to_all(jnp.concatenate([spread, gate_block], axis=1), ('y', 'z'),...  12.7 us
    dynamic_update_slice x4, local copies, waits for them, and re-layouts, on_device(): down_all = lax.dynamic_update_slice_in_dim(down_all, d[None], origin, 0)  4.81 us
  transfers between devices with their start and end apart: 11, of which 5 were waited for; matrix products, arithmetic and copies ran while one was open for 11% of the time, Pallas kernels for 0%

profile of v1, /device:TPU:16, one launch (start us, length us, event | category | flops | bytes accessed | tf_op | source)
XLA Modules:
  0.0 165.9 jit_solution(18436199860719075838)
XLA Ops:
  0.7 0.7 broadcast_compare_fusion
  1.4 0.1 convolution_convert_fusion.6
  1.5 0.8 subtract_add_fusion
  2.3 0.2 select_reduce_fusion
  2.5 0.1 sub.43
  2.6 1.3 fusion.6
  3.9 1.1 broadcast_in_dim.86
  5.0 16.5 %all-to-all-start = ((bf16[64,8,1024]{2,1,0:T(8,128)(2,1)}), bf16[64,8,1024]{2,1,0:T(8,128)(2,1)S(1)}, u32[]{:S(2)}, u32[]{:S(2)}) async-start(bf16[64,8,1024]{2,1,0:T(8,128)(2,1)} %bitcast.2), calls=%async_computation | async-start | bytes 2097152 | tf_op jit(solution)/shard_map/all_to_all | solution.py:61
  21.5 1.3 constant_dynamic-slice_fusion
  22.8 1.1 copy.18
  24.0 1.1 copy.19
  25.1 0.8 pad_maximum_fusion.2
  25.9 3.4 %collective-permute-start.1 = (bf16[1024,256]{0,1:T(8,128)(2,1)}, bf16[1024,256]{0,1:T(8,128)(2,1)}, u32[]{:S(2)}, u32[]{:S(2)}) collective-permute-start(bf16[1024,256]{0,1:T(8,128)(2,1)} %pad_maximum_fusion.2), channel_id=1, source_target_pairs={{0,2},{2,4},{4,6},{6,0},{1,3},{3,5},{5,7},{7,1},{8,10},{10,12},{12... | collective-permute-start | bytes 1572872 | tf_op jit(solution)/shard_map/ppermute | solution.py:24
  29.3 0.1 copy.20
  29.5 0.1 copy.21
  29.7 0.8 pad_maximum_fusion.3
  30.5 3.6 %collective-permute-start.2 = (bf16[1024,256]{0,1:T(8,128)(2,1)}, bf16[1024,256]{0,1:T(8,128)(2,1)}, u32[]{:S(2)}, u32[]{:S(2)}) collective-permute-start(bf16[1024,256]{0,1:T(8,128)(2,1)} %pad_maximum_fusion.3), channel_id=1, source_target_pairs={{0,6},{2,0},{4,2},{6,4},{1,7},{3,1},{5,3},{7,5},{8,14},{10,8},{12,... | collective-permute-start | bytes 1572872 | tf_op jit(solution)/shard_map/ppermute | solution.py:24
  34.2 0.1 copy.22
  34.3 0.1 copy.23
  34.5 0.8 pad_maximum_fusion.4
  35.3 3.7 %collective-permute-start.3 = (bf16[1024,256]{0,1:T(8,128)(2,1)}, bf16[1024,256]{0,1:T(8,128)(2,1)}, u32[]{:S(2)}, u32[]{:S(2)}) collective-permute-start(bf16[1024,256]{0,1:T(8,128)(2,1)} %pad_maximum_fusion.4), channel_id=1, source_target_pairs={{0,4},{2,6},{4,0},{6,2},{1,5},{3,7},{5,1},{7,3},{8,12},{10,14},{12... | collective-permute-start | bytes 1572872 | tf_op jit(solution)/shard_map/ppermute | solution.py:24
  39.0 0.8 dynamic-slice_bitcast_fusion
  39.8 2.5 %collective-permute-start.4 = (bf16[128,1024]{1,0:T(8,128)(2,1)}, bf16[128,1024]{1,0:T(8,128)(2,1)}, u32[]{:S(2)}, u32[]{:S(2)}) collective-permute-start(bf16[128,1024]{1,0:T(8,128)(2,1)} %get-tuple-element.20), channel_id=1, source_target_pairs={{0,2},{2,4},{4,6},{6,0},{1,3},{3,5},{5,7},{7,1},{8,10},{10,12},{12... | collective-permute-start | bytes 786440 | tf_op jit(solution)/shard_map/ppermute | solution.py:24
  42.3 4.6 %collective-permute-start.5 = (bf16[128,1024]{1,0:T(8,128)(2,1)S(1)}, bf16[128,1024]{1,0:T(8,128)(2,1)}, u32[]{:S(2)}, u32[]{:S(2)}) collective-permute-start(bf16[128,1024]{1,0:T(8,128)(2,1)S(1)} %get-tuple-element.19), channel_id=1, source_target_pairs={{0,6},{2,0},{4,2},{6,4},{1,7},{3,1},{5,3},{7,5},{8,14},{10,8},{12,... | collective-permute-start | bytes 786440 | tf_op jit(solution)/shard_map/ppermute | solution.py:24
  46.9 0.2 convert_reduce_fusion.1
  47.2 0.1 copy.24
  47.4 0.9 copy.25
  48.3 11.5 %collective-permute-done.4 = bf16[128,1024]{1,0:T(8,128)(2,1)} collective-permute-done((bf16[128,1024]{1,0:T(8,128)(2,1)}, bf16[128,1024]{1,0:T(8,128)(2,1)}, u32[]{:S(2)}, u32[]{:S(2)}) %collective-permute-start.4) | collective-permute-done | bytes 262176 | tf_op jit(solution)/shard_map/ppermute | solution.py:24
  59.8 3.2 %collective-permute-start.6 = (bf16[128,1024]{1,0:T(8,128)(2,1)S(1)}, bf16[128,1024]{1,0:T(8,128)(2,1)S(1)}, u32[]{:S(2)}, u32[]{:S(2)}) collective-permute-start(bf16[128,1024]{1,0:T(8,128)(2,1)S(1)} %get-tuple-element.18), channel_id=1, source_target_pairs={{0,4},{2,6},{4,0},{6,2},{1,5},{3,7},{5,1},{7,3},{8,12},{10,14},{12... | collective-permute-start | bytes 786440 | tf_op jit(solution)/shard_map/ppermute | solution.py:24
  63.0 1.1 broadcast_in_dim.92
  64.1 1.7 %bitcast_dynamic-update-slice_fusion.5 = bf16[4,128,1024]{2,1,0:T(8,128)(2,1)} fusion(bf16[4,128,1024]{2,1,0:T(8,128)(2,1)} %broadcast_in_dim.92, s32[]{:T(128)S(6)} %select_n.118, bf16[128,1024]{1,0:T(8,128)(2,1)} %collective-permute-done.4), kind=kLoop, calls=%fused_computation.55 | loop fusion | bytes 524292 | tf_op jit(solution)/shard_map/dynamic_update_slice | solution.py:78
  65.8 1.7 %bitcast_dynamic-update-slice_fusion.4 = bf16[4,128,1024]{2,1,0:T(8,128)(2,1)} fusion(bf16[4,128,1024]{2,1,0:T(8,128)(2,1)} %bitcast_dynamic-update-slice_fusion.5, s32[]{:T(128)S(6)} %select_n.122, bf16[128,1024]{1,0:T(8,128)(2,1)} %collective-permute-done.5), kind=kLoop, calls=%fused_computation.54 | loop fusion | bytes 524292 | tf_op jit(solution)/shard_map/dynamic_update_slice | solution.py:78
  67.5 3.4 %collective-permute-done.6 = bf16[128,1024]{1,0:T(8,128)(2,1)S(1)} collective-permute-done((bf16[128,1024]{1,0:T(8,128)(2,1)S(1)}, bf16[128,1024]{1,0:T(8,128)(2,1)S(1)}, u32[]{:S(2)}, u32[]{:S(2)}) %collective-permute-start.6) | collective-permute-done | bytes 262176 | tf_op jit(solution)/shard_map/ppermute | solution.py:24
  70.9 0.7 bitcast_dynamic-update-slice_fusion.3
  71.6 0.7 dynamic-slice_dynamic-update-slice_fusion
  72.4 0.6 convolution_convert_fusion
  73.0 1.9 %collective-permute-start = (bf16[384,1024]{1,0:T(8,128)(2,1)S(1)}, bf16[384,1024]{1,0:T(8,128)(2,1)S(1)}, u32[]{:S(2)}, u32[]{:S(2)}) collective-permute-start(bf16[384,1024]{1,0:T(8,128)(2,1)S(1)} %convolution_convert_fusion), channel_id=1, source_target_pairs={{0,1},{1,0},{2,3},{3,2},{4,5},{5,4},{6,7},{7,6},{8,9},{9,8},{10,11... | collective-permute-start | bytes 2359304 | tf_op jit(solution)/shard_map/ppermute | solution.py:20
  74.9 0.3 broadcast_in_dim.87
  75.2 1.1 bitcast_dynamic-update-slice_fusion.2
  76.3 1.1 bitcast_dynamic-update-slice_fusion.1
  77.4 1.1 bitcast_dynamic-update-slice_fusion
  78.6 0.1 broadcast_select_fusion.1
  78.7 0.1 fusion.40
  78.8 1.0 convolution_convert_fusion.1
  79.9 1.8 %convolution_convert_fusion.3 = bf16[384,512]{1,0:T(8,128)(2,1)S(1)} fusion(bf16[512,1024]{1,0:T(8,128)(2,1)} %bitcast.24, bf16[384,512]{1,0:T(8,128)(2,1)S(1)} %get-tuple-element.42, bf16[384,512]{1,0:T(8,128)(2,1)S(1)} %get-tuple-element.26), kind=kOutput, calls=%fused_computation.7 | convolution fusion | flops 404422656 | bytes 2228224 | tf_op jit(solution)/shard_map/dot_general | solution.py:97
  81.8 0.1 fusion.42
  82.0 1.2 pad_maximum_fusion
  83.2 3.5 %all-to-all-start.1 = ((bf16[4,384,384]{2,1,0:T(8,128)(2,1)}), bf16[4,384,384]{2,1,0:T(8,128)(2,1)S(1)}, u32[]{:S(2)}, u32[]{:S(2)}) async-start(bf16[4,384,384]{2,1,0:T(8,128)(2,1)} %pad_maximum_fusion), calls=%async_computation.1 | async-start | bytes 2359296 | tf_op jit(solution)/shard_map/all_to_all | solution.py:106
  86.8 17.4 %all-to-all-done.1 = bf16[4,384,384]{2,1,0:T(8,128)(2,1)S(1)} async-done(((bf16[4,384,384]{2,1,0:T(8,128)(2,1)}), bf16[4,384,384]{2,1,0:T(8,128)(2,1)S(1)}, u32[]{:S(2)}, u32[]{:S(2)}) %all-to-all-start.1) | async-done | bytes 1179680 | tf_op jit(solution)/shard_map/all_to_all | solution.py:106
  104.1 0.2 convert_reduce_fusion
  104.3 0.2 multiply_convert_fusion.1
  104.6 14.0 %all-gather = bf16[1600,256]{1,0:T(8,128)(2,1)S(1)} all-gather(bf16[400,256]{1,0:T(8,128)(2,1)S(1)} %pad_maximum_fusion.6), channel_id=2, replica_groups=mesh['y'=8,'z'=8,'x'=4,'c'=2] {'x'}, dimensions={0}, use_global_device_ids=true | all-gather | bytes 1024000 | tf_op jit(solution)/shard_map/all_gather | solution.py:117
  118.6 2.1 %fusion.2 = f32[384,1024]{1,0:T(8,128)} fusion(bf16[4,1024,256]{1,2,0:T(8,128)(2,1)S(1)} %fusion.16, bf16[4,400,256]{2,1,0:T(8,128)(2,1)S(1)} %bitcast.85), kind=kOutput, calls=%fused_computation.3 | convolution fusion | flops 805306368 | bytes 4456448 | tf_op jit(solution)/shard_map/dot_general | solution.py:121
  120.8 1.4 select_convert_fusion
  122.4 1.9 %collective-permute-start.7 = (bf16[400,512]{1,0:T(8,128)(2,1)S(1)}, bf16[400,512]{1,0:T(8,128)(2,1)S(1)}, u32[]{:S(2)}, u32[]{:S(2)}) collective-permute-start(bf16[400,512]{1,0:T(8,128)(2,1)S(1)} %pad_maximum_fusion.5), channel_id=1, source_target_pairs={{0,1},{1,0},{2,3},{3,2},{4,5},{5,4},{6,7},{7,6},{8,9},{9,8},{10,11... | collective-permute-start | bytes 1228808 | tf_op jit(solution)/shard_map/ppermute | solution.py:20
  124.4 1.7 %collective-permute-done.7 = bf16[400,512]{1,0:T(8,128)(2,1)S(1)} collective-permute-done((bf16[400,512]{1,0:T(8,128)(2,1)S(1)}, bf16[400,512]{1,0:T(8,128)(2,1)S(1)}, u32[]{:S(2)}, u32[]{:S(2)}) %collective-permute-start.7) | collective-permute-done | bytes 409632 | tf_op jit(solution)/shard_map/ppermute | solution.py:20
  126.1 1.9 %fusion.5 = bf16[64,8,512]{2,1,0:T(8,128)(2,1)S(1)} fusion(f32[384,1024]{1,0:T(8,128)} %fusion.2, bf16[400,512]{1,0:T(8,128)(2,1)S(1)} %collective-permute-done.7, s32[384]{0:T(512)S(1)} %copy-done.11, pred[]{:T(512)S(6)} %eq.94), kind=kOutput, calls=%fused_computation.8 | convolution fusion | flops 202571776 | bytes 2492417 | tf_op jit(solution)/shard_map/dot_general | solution.py:132
  128.1 0.9 pad_maximum_fusion.1
  129.0 12.7 %all-to-all-start.2 = ((bf16[64,8,640]{2,1,0:T(8,128)(2,1)}), bf16[64,8,640]{2,1,0:T(8,128)(2,1)S(1)}, u32[]{:S(2)}, u32[]{:S(2)}) async-start(bf16[64,8,640]{2,1,0:T(8,128)(2,1)} %pad_maximum_fusion.1), calls=%async_computation.2 | async-start | bytes 1310720 | tf_op jit(solution)/shard_map/all_to_all | solution.py:133
  141.7 0.1 fusion.26
  141.8 22.4 %all-to-all-done.2 = bf16[64,8,640]{2,1,0:T(8,128)(2,1)S(1)} async-done(((bf16[64,8,640]{2,1,0:T(8,128)(2,1)}), bf16[64,8,640]{2,1,0:T(8,128)(2,1)S(1)}, u32[]{:S(2)}, u32[]{:S(2)}) %all-to-all-start.2) | async-done | bytes 655392 | tf_op jit(solution)/shard_map/all_to_all | solution.py:133
  164.3 0.1 reduce_sum.59
  164.3 0.6 slice_add_fusion
  165.0 1.0 convolution_convert_fusion.4
  (62 shorter events, 0.7 us)
Async XLA Ops:
  0.6 86.1 %copy-start = (f32[8,384]{1,0:T(8,128)S(1)}, f32[8,384]{1,0:T(8,128)}, u32[]{:S(2)}) copy-start(f32[8,384]{1,0:T(8,128)} %param.13) | copy-start | bytes 36868
  3.8 17.7 %copy-start.3 = (bf16[1,4096,128]{2,1,0:T(8,128)(2,1)S(1)}, bf16[1,4096,128]{2,1,0:T(8,128)(2,1)}, u32[]{:S(2)}) copy-start(bf16[1,4096,128]{2,1,0:T(8,128)(2,1)} %param.10) | copy-start | bytes 3145732
  3.8 17.7 %copy-start.4 = (bf16[1,4096,128]{2,1,0:T(8,128)(2,1)S(1)}, bf16[1,4096,128]{2,1,0:T(8,128)(2,1)}, u32[]{:S(2)}) copy-start(bf16[1,4096,128]{2,1,0:T(8,128)(2,1)} %param.9) | copy-start | bytes 3145732
  5.0 67.4 %all-to-all-start = ((bf16[64,8,1024]{2,1,0:T(8,128)(2,1)}), bf16[64,8,1024]{2,1,0:T(8,128)(2,1)S(1)}, u32[]{:S(2)}, u32[]{:S(2)}) async-start(bf16[64,8,1024]{2,1,0:T(8,128)(2,1)} %bitcast.2), calls=%async_computation | async-start | bytes 2097152 | tf_op jit(solution)/shard_map/all_to_all | solution.py:61
  22.8 6.5 %copy-start.9 = (bf16[1,1024,128]{2,1,0:T(8,128)(2,1)S(1)}, bf16[1,1024,128]{2,1,0:T(8,128)(2,1)}, u32[]{:S(2)}) copy-start(bf16[1,1024,128]{2,1,0:T(8,128)(2,1)} %get-tuple-element.40) | copy-start | bytes 786436
  22.8 6.7 %copy-start.8 = (bf16[1,1024,128]{2,1,0:T(8,128)(2,1)S(1)}, bf16[1,1024,128]{2,1,0:T(8,128)(2,1)}, u32[]{:S(2)}) copy-start(bf16[1,1024,128]{2,1,0:T(8,128)(2,1)} %get-tuple-element.15) | copy-start | bytes 786436
  25.1 9.1 %copy-start.7 = (bf16[1,1024,128]{2,1,0:T(8,128)(2,1)S(1)}, bf16[1,1024,128]{2,1,0:T(8,128)(2,1)}, u32[]{:S(2)}) copy-start(bf16[1,1024,128]{2,1,0:T(8,128)(2,1)} %get-tuple-element.38) | copy-start | bytes 786436
  25.9 49.0 %collective-permute-start.1 = (bf16[1024,256]{0,1:T(8,128)(2,1)}, bf16[1024,256]{0,1:T(8,128)(2,1)}, u32[]{:S(2)}, u32[]{:S(2)}) collective-permute-start(bf16[1024,256]{0,1:T(8,128)(2,1)} %pad_maximum_fusion.2), channel_id=1, source_target_pairs={{0,2},{2,4},{4,6},{6,0},{1,3},{3,5},{5,7},{7,1},{8,10},{10,12},{12... | collective-permute-start | bytes 1572872 | tf_op jit(solution)/shard_map/ppermute | solution.py:24
  29.6 9.4 %copy-start.1 = (bf16[1,128,4096]{2,1,0:T(8,128)(2,1)S(1)}, bf16[1,128,4096]{2,1,0:T(8,128)(2,1)}, u32[]{:S(2)}) copy-start(bf16[1,128,4096]{2,1,0:T(8,128)(2,1)} %param.11) | copy-start | bytes 3145732
  30.5 45.8 %collective-permute-start.2 = (bf16[1024,256]{0,1:T(8,128)(2,1)}, bf16[1024,256]{0,1:T(8,128)(2,1)}, u32[]{:S(2)}, u32[]{:S(2)}) collective-permute-start(bf16[1024,256]{0,1:T(8,128)(2,1)} %pad_maximum_fusion.3), channel_id=1, source_target_pairs={{0,6},{2,0},{4,2},{6,4},{1,7},{3,1},{5,3},{7,5},{8,14},{10,8},{12,... | collective-permute-start | bytes 1572872 | tf_op jit(solution)/shard_map/ppermute | solution.py:24
  34.3 12.9 %copy-start.6 = (bf16[1,1024,128]{2,1,0:T(8,128)(2,1)S(1)}, bf16[1,1024,128]{2,1,0:T(8,128)(2,1)}, u32[]{:S(2)}) copy-start(bf16[1,1024,128]{2,1,0:T(8,128)(2,1)} %get-tuple-element.41) | copy-start | bytes 786436
  34.5 12.9 %copy-start.5 = (bf16[1,1024,128]{2,1,0:T(8,128)(2,1)S(1)}, bf16[1,1024,128]{2,1,0:T(8,128)(2,1)}, u32[]{:S(2)}) copy-start(bf16[1,1024,128]{2,1,0:T(8,128)(2,1)} %get-tuple-element.14) | copy-start | bytes 786436
  35.3 42.1 %collective-permute-start.3 = (bf16[1024,256]{0,1:T(8,128)(2,1)}, bf16[1024,256]{0,1:T(8,128)(2,1)}, u32[]{:S(2)}, u32[]{:S(2)}) collective-permute-start(bf16[1024,256]{0,1:T(8,128)(2,1)} %pad_maximum_fusion.4), channel_id=1, source_target_pairs={{0,4},{2,6},{4,0},{6,2},{1,5},{3,7},{5,1},{7,3},{8,12},{10,14},{12... | collective-permute-start | bytes 1572872 | tf_op jit(solution)/shard_map/ppermute | solution.py:24
  39.8 20.0 %collective-permute-start.4 = (bf16[128,1024]{1,0:T(8,128)(2,1)}, bf16[128,1024]{1,0:T(8,128)(2,1)}, u32[]{:S(2)}, u32[]{:S(2)}) collective-permute-start(bf16[128,1024]{1,0:T(8,128)(2,1)} %get-tuple-element.20), channel_id=1, source_target_pairs={{0,2},{2,4},{4,6},{6,0},{1,3},{3,5},{5,7},{7,1},{8,10},{10,12},{12... | collective-permute-start | bytes 786440 | tf_op jit(solution)/shard_map/ppermute | solution.py:24
  42.3 23.5 %collective-permute-start.5 = (bf16[128,1024]{1,0:T(8,128)(2,1)S(1)}, bf16[128,1024]{1,0:T(8,128)(2,1)}, u32[]{:S(2)}, u32[]{:S(2)}) collective-permute-start(bf16[128,1024]{1,0:T(8,128)(2,1)S(1)} %get-tuple-element.19), channel_id=1, source_target_pairs={{0,6},{2,0},{4,2},{6,4},{1,7},{3,1},{5,3},{7,5},{8,14},{10,8},{12,... | collective-permute-start | bytes 786440 | tf_op jit(solution)/shard_map/ppermute | solution.py:24
  47.1 25.2 %copy-start.10 = (s32[384]{0:T(512)}, s32[384]{0:T(512)S(1)}, u32[]{:S(2)}) copy-start(s32[384]{0:T(512)S(1)} %multiply_add_fusion) | copy-start | bytes 4612
  59.8 11.1 %collective-permute-start.6 = (bf16[128,1024]{1,0:T(8,128)(2,1)S(1)}, bf16[128,1024]{1,0:T(8,128)(2,1)S(1)}, u32[]{:S(2)}, u32[]{:S(2)}) collective-permute-start(bf16[128,1024]{1,0:T(8,128)(2,1)S(1)} %get-tuple-element.18), channel_id=1, source_target_pairs={{0,4},{2,6},{4,0},{6,2},{1,5},{3,7},{5,1},{7,3},{8,12},{10,14},{12... | collective-permute-start | bytes 786440 | tf_op jit(solution)/shard_map/ppermute | solution.py:24
  73.0 5.6 %collective-permute-start = (bf16[384,1024]{1,0:T(8,128)(2,1)S(1)}, bf16[384,1024]{1,0:T(8,128)(2,1)S(1)}, u32[]{:S(2)}, u32[]{:S(2)}) collective-permute-start(bf16[384,1024]{1,0:T(8,128)(2,1)S(1)} %convolution_convert_fusion), channel_id=1, source_target_pairs={{0,1},{1,0},{2,3},{3,2},{4,5},{5,4},{6,7},{7,6},{8,9},{9,8},{10,11... | collective-permute-start | bytes 2359304 | tf_op jit(solution)/shard_map/ppermute | solution.py:20
  75.2 3.3 %copy-start.2 = (bf16[1,1024,128]{1,2,0:T(8,128)(2,1)S(1)}, bf16[1,1024,128]{1,2,0:T(8,128)(2,1)}, u32[]{:S(2)}) copy-start(bf16[1,1024,128]{1,2,0:T(8,128)(2,1)} %copy.25) | copy-start | bytes 786436
  83.2 20.9 %all-to-all-start.1 = ((bf16[4,384,384]{2,1,0:T(8,128)(2,1)}), bf16[4,384,384]{2,1,0:T(8,128)(2,1)S(1)}, u32[]{:S(2)}, u32[]{:S(2)}) async-start(bf16[4,384,384]{2,1,0:T(8,128)(2,1)} %pad_maximum_fusion), calls=%async_computation.1 | async-start | bytes 2359296 | tf_op jit(solution)/shard_map/all_to_all | solution.py:106
  120.8 5.3 %copy-start.11 = (s32[384]{0:T(512)S(1)}, s32[384]{0:T(512)}, u32[]{:S(2)}) copy-start(s32[384]{0:T(512)} %copy-done.10) | copy-start | bytes 4612
  122.4 3.6 %collective-permute-start.7 = (bf16[400,512]{1,0:T(8,128)(2,1)S(1)}, bf16[400,512]{1,0:T(8,128)(2,1)S(1)}, u32[]{:S(2)}, u32[]{:S(2)}) collective-permute-start(bf16[400,512]{1,0:T(8,128)(2,1)S(1)} %pad_maximum_fusion.5), channel_id=1, source_target_pairs={{0,1},{1,0},{2,3},{3,2},{4,5},{5,4},{6,7},{7,6},{8,9},{9,8},{10,11... | collective-permute-start | bytes 1228808 | tf_op jit(solution)/shard_map/ppermute | solution.py:20
  129.0 35.2 %all-to-all-start.2 = ((bf16[64,8,640]{2,1,0:T(8,128)(2,1)}), bf16[64,8,640]{2,1,0:T(8,128)(2,1)S(1)}, u32[]{:S(2)}, u32[]{:S(2)}) async-start(bf16[64,8,640]{2,1,0:T(8,128)(2,1)} %pad_maximum_fusion.1), calls=%async_computation.2 | async-start | bytes 1310720 | tf_op jit(solution)/shard_map/all_to_all | solution.py:133

commit v2 on v1

v2 whole, which is shorter than its diff:
```python
import jax
import jax.numpy as jnp
import numpy as np
from jax import lax
from jax.experimental import pallas as pl
from jax.experimental.pallas import tpu as pltpu
from jax.sharding import Mesh
from jax.sharding import PartitionSpec as P

NY, NZ, NX, NC = 8, 8, 4, 2
SLOTS = 8
BF = jnp.bfloat16
F32 = jnp.float32
VMEM = 12 * 1024 * 1024
CONTRACT = (((1,), (1,)), ((), ()))


def silu_parts(values):
    sig = jax.nn.sigmoid(values)
    return (values * sig, sig * (1.0 + values * (1.0 - sig)))


def swap_cores(a):
    return lax.ppermute(a, "c", [(0, 1), (1, 0)])


def shift_x(a, k):
    return lax.ppermute(a, "x", [(j, (j + k) % NX) for j in range(NX)])


def hi_lo(values):
    hi = values.astype(BF)
    lo = (values - hi.astype(F32)).astype(BF)
    return hi, lo


def pack_kernel(where_ref, gate_ref, up_ref, down_ref, out_ref, sems):
    hid = gate_ref.shape[1]
    half = out_ref.shape[0] // 3
    chunk = out_ref.shape[1]
    copies = []
    for h in range(NC):
        start = pl.multiple_of(where_ref[h], half)
        rows = pl.ds(h * half, half)
        copies.append((gate_ref.at[pl.ds(start, half), :], out_ref.at[rows, pl.ds(0, hid)]))
        copies.append((up_ref.at[pl.ds(start, half), :], out_ref.at[rows, pl.ds(hid, hid)]))
        for q in range(half // chunk):
            begin = pl.multiple_of(start + q * chunk, chunk)
            low = NC * half + (h * (half // chunk) + q) * hid
            copies.append((down_ref.at[:, pl.ds(begin, chunk)], out_ref.at[pl.ds(low, hid), :]))
    started = []
    for i, (src, dst) in enumerate(copies):
        copy = pltpu.make_async_copy(src, dst, sems.at[i])
        copy.start()
        started.append(copy)
    for copy in started:
        copy.wait()


def pack(gate, up, down, where, feat):
    hid = gate.shape[1]
    chunk = 2 * hid
    rows = NC * feat + NC * (feat // chunk) * hid
    n = NC * (2 + feat // chunk)
    anywhere = pl.BlockSpec(memory_space=pltpu.HBM)
    return pl.pallas_call(
        pack_kernel,
        out_shape=jax.ShapeDtypeStruct((rows, chunk), BF),
        in_specs=[pl.BlockSpec(memory_space=pltpu.SMEM), anywhere, anywhere, anywhere],
        scratch_shapes=[pltpu.SemaphoreType.DMA((n,))],
        compiler_params=pltpu.CompilerParams(vmem_limit_bytes=VMEM),
        name="pack_weights",
    )(where, gate, up, down)


def pre_kernel(own_ref, other_ref, w_ref, out_ref):
    feat = own_ref.shape[1] // 2
    chunk = w_ref.shape[1]
    hid = chunk // 2
    gu = None
    back = None
    for h, rows in enumerate((own_ref, other_ref)):
        term = jnp.dot(rows[:, :feat], w_ref[h * feat : (h + 1) * feat, :], preferred_element_type=F32)
        gu = term if gu is None else gu + term
        for q in range(feat // chunk):
            low = NC * feat + (h * (feat // chunk) + q) * hid
            term = lax.dot_general(
                rows[:, feat + q * chunk : feat + (q + 1) * chunk],
                w_ref[low : low + hid, :],
                CONTRACT,
                preferred_element_type=F32,
            )
            back = term if back is None else back + term
    out_ref[:, :chunk] = gu.astype(BF)
    out_ref[:, chunk:] = back.astype(BF)


def pre_part(own, other, w):
    rows = own.shape[0]
    return pl.pallas_call(
        pre_kernel,
        out_shape=jax.ShapeDtypeStruct((rows, w.shape[1] // 2 * 3), BF),
        compiler_params=pltpu.CompilerParams(vmem_limit_bytes=VMEM),
        name="pre_part",
    )(own, other, w)


def give_kernel(from_ref, d_ref, w0, w1, w2, w3, extra_ref, give_ref, keep_ref):
    rows, feat = keep_ref.shape
    for h in (1, 0):
        total = None
        for k, w in enumerate((w0, w1, w2, w3)):
            term = lax.dot_general(
                d_ref[from_ref[k], :rows, :],
                w[h * feat : (h + 1) * feat, :],
                CONTRACT,
                preferred_element_type=F32,
            )
            total = term if total is None else total + term
        if h:
            give_ref[:rows, :] = total.astype(BF)
            give_ref[rows:, :] = extra_ref[...]
        else:
            keep_ref[...] = total


def give_keep(origin, deltas, weights, extra, rows, feat):
    vmem = pl.BlockSpec(memory_space=pltpu.VMEM)
    return pl.pallas_call(
        give_kernel,
        out_shape=(
            jax.ShapeDtypeStruct((rows + extra.shape[0], feat), BF),
            jax.ShapeDtypeStruct((rows, feat), F32),
        ),
        in_specs=[pl.BlockSpec(memory_space=pltpu.SMEM)] + [vmem] * 6,
        compiler_params=pltpu.CompilerParams(vmem_limit_bytes=VMEM),
        name="input_grads",
    )(origin, deltas, *weights, extra)


def spread_kernel(keep_ref, came_ref, place_ref, gate_ref, out_ref):
    rows, feat = keep_ref.shape
    term = (keep_ref[...] + came_ref[:rows, :].astype(F32)).astype(BF)
    out_ref[:, :feat] = jnp.dot(place_ref[...], term, preferred_element_type=F32).astype(BF)
    block = gate_ref[...]
    slots = out_ref.shape[0]
    block = jnp.broadcast_to(block[None], (slots // SLOTS, SLOTS, 128)).reshape(slots, 128)
    out_ref[:, feat:] = block.astype(BF)


def spread_out(keep, came, place_t, gate_block):
    slots, feat = place_t.shape[0], keep.shape[1]
    return pl.pallas_call(
        spread_kernel,
        out_shape=jax.ShapeDtypeStruct((slots, feat + 128), BF),
        compiler_params=pltpu.CompilerParams(vmem_limit_bytes=VMEM),
        name="rows_to_slots",
    )(keep, came, place_t, gate_block)


def on_device(tokens, output_grad, gate_weight, up_weight, down_weight, chosen, gate_values):
    expert = lax.axis_index("y")
    exp_index = expert * NZ + lax.axis_index("z")
    x_index = lax.axis_index("x")
    c_index = lax.axis_index("c")
    expert_count, capacity = chosen.shape
    token_rows, feat = tokens.shape
    hid = gate_weight.shape[2]
    peers = NY * NZ
    all_slots = peers * SLOTS
    wide = NC * feat

    packed = {}
    for k in (2, 1, 3, 0):
        dest = (x_index + k) % NX
        where = jnp.stack([dest * wide + c_index * feat, dest * wide + (1 - c_index) * feat])
        packed[k] = pack(gate_weight[0], up_weight[0], down_weight[0], where, feat)
    weights = {0: packed[0]}
    for k in (2, 1, 3):
        weights[k] = shift_x(packed[k], k)

    source = chosen // token_rows
    local_rows = chosen - exp_index * token_rows
    mine = source == exp_index
    order = jnp.arange(capacity, dtype=jnp.int32)
    earlier = (order[:, None] < order[None, :]).astype(BF)
    rank = jnp.dot(mine.astype(BF), earlier, preferred_element_type=F32).astype(jnp.int32)
    slot_ids = jnp.arange(SLOTS, dtype=jnp.int32)
    hit = mine[:, None, :] & (rank[:, None, :] == slot_ids[None, :, None])
    send_row = jnp.sum(jnp.where(hit, local_rows[:, None, :] + 1, 0), axis=2) - 1
    token_ids = jnp.arange(token_rows, dtype=jnp.int32)
    pick = (send_row.reshape(-1)[:, None] == token_ids[None, :]).astype(BF)
    both = jnp.concatenate([tokens, output_grad], axis=1)
    picked = jnp.dot(pick, both, preferred_element_type=F32).astype(BF)
    outgoing = jnp.broadcast_to(
        picked.reshape(expert_count, 1, SLOTS, 2 * feat), (expert_count, NZ, SLOTS, 2 * feat)
    ).reshape(all_slots, 2 * feat)
    got = lax.all_to_all(outgoing, ("y", "z"), split_axis=0, concat_axis=0, tiled=True)
    got, weights[2], weights[1] = lax.optimization_barrier((got, weights[2], weights[1]))

    my_source = lax.dynamic_index_in_dim(source, expert, 0, keepdims=False)
    my_gates = lax.dynamic_index_in_dim(gate_values, expert, 0, keepdims=False)
    same = (my_source[:, None] == my_source[None, :]) & (order[None, :] < order[:, None])
    my_rank = jnp.sum(same.astype(jnp.int32), axis=1)
    my_slot = my_source * SLOTS + my_rank
    slot_order = jnp.arange(all_slots, dtype=jnp.int32)
    place = (my_slot[:, None] == slot_order[None, :]).astype(BF)
    place_t = (my_slot[None, :] == slot_order[:, None]).astype(BF)
    own = jnp.dot(place, got, preferred_element_type=F32).astype(BF)
    other = swap_cores(own)
    other, weights[3] = lax.optimization_barrier((other, weights[3]))

    sums = None
    for k in (2, 1, 3, 0):
        part = pre_part(own, other, weights[(NX - k) % NX])
        part = (shift_x(part, k) if k else part).astype(F32)
        sums = part if sums is None else sums + part
    pre_gate, pre_up, back = sums[:, :hid], sums[:, hid : 2 * hid], sums[:, 2 * hid :]
    active, slope = silu_parts(pre_gate)
    gate_part = jnp.sum(active * pre_up * back, axis=1)
    scaled = my_gates[:, None] * back
    gate_delta = (scaled * pre_up * slope).astype(BF)
    up_delta = (scaled * active).astype(BF)
    hi, lo = hi_lo(gate_part)
    extra = jnp.concatenate([hi, lo, jnp.zeros((16 * 2 * hid - 2 * capacity,), BF)]).reshape(16, 2 * hid)
    delta = jnp.concatenate([jnp.concatenate([gate_delta, up_delta], axis=1), extra], axis=0)
    deltas = lax.all_gather(delta, "x", axis=0, tiled=False)
    gate_rows = deltas[:, capacity:].reshape(NX, -1).astype(F32)
    gate_sum = jnp.sum(gate_rows[:, :capacity] + gate_rows[:, capacity : 2 * capacity], axis=0)
    origin = (x_index - jnp.arange(NX, dtype=jnp.int32)) % NX
    hi, lo = hi_lo(gate_sum)
    extra = jnp.concatenate([hi, lo, jnp.zeros((16 * feat - 2 * capacity,), BF)]).reshape(16, feat)
    give, keep = give_keep(
        origin, deltas, [weights[k] for k in range(NX)], extra, capacity, feat
    )
    came = swap_cores(give)
    came_gate = came[capacity:].reshape(-1).astype(F32)
    gate_sum = (hi.astype(F32) + lo.astype(F32)) + (came_gate[:capacity] + came_gate[capacity : 2 * capacity])
    hi, lo = hi_lo(gate_sum)
    gate_block = jnp.concatenate([hi, lo, jnp.zeros((SLOTS * 128 - 2 * capacity,), BF)])
    gate_block = gate_block.astype(F32).reshape(SLOTS, 128)
    home = lax.all_to_all(
        spread_out(keep, came, place_t, gate_block), ("y", "z"), split_axis=0, concat_axis=0, tiled=True
    )
    owner = jnp.broadcast_to(
        pick.reshape(expert_count, 1, SLOTS, token_rows), (expert_count, NZ, SLOTS, token_rows)
    ).reshape(all_slots, token_rows)
    grad_tokens = lax.dot_general(
        owner, home[:, :feat], (((0,), (0,)), ((), ())), preferred_element_type=F32
    ).astype(BF)
    gates = jnp.sum(home[:, feat:].reshape(expert_count, NZ, SLOTS * 128).astype(F32), axis=1)
    gate_grad = gates[:, :capacity] + gates[:, capacity : 2 * capacity]
    return grad_tokens, gate_grad


def solution(mesh):
    grid = Mesh(np.asarray(mesh.devices).reshape(NY, NZ, NX, NC), ("y", "z", "x", "c"))
    exp, ten = ("y", "z"), ("x", "c")
    in_specs = (
        P(exp, ten),
        P(exp, ten),
        P(exp, None, ten),
        P(exp, None, ten),
        P(exp, ten, None),
        P(),
        P(),
    )
    out_specs = (P(exp, ten), P())
    return jax.shard_map(on_device, mesh=grid, in_specs=in_specs, out_specs=out_specs, check_vma=False)
```

time: 167 us -> 156 us (0.934)
  the two profiles are of different devices: /device:TPU:16 before, /device:TPU:18 now
where the time goes in v2:
time: 156 us; the launch traced here: 155 us
  waiting for transfers between devices  57.5 us (37%)
  starting transfers between devices  52.4 us (34%)
  Pallas kernels  17.1 us (11%)
  blocking collectives  15.9 us (10%)
  other arithmetic  4.74 us (3%)
  matrix products  4.18 us (3%)
  local copies, waits for them, and re-layouts  2.01 us (1%)
    ppermute x6, waiting for transfers between devices, shift_x(): return lax.ppermute(a, 'x', [(j, (j + k) % NX) for j in range(NX)])  31.2 us
    all_to_all x1, waiting for transfers between devices, on_device(): lax.all_to_all(spread_out(keep, came, place_t, gate_block), ('y', 'z'), s...  22.4 us
    ppermute x6, starting transfers between devices, shift_x(): return lax.ppermute(a, 'x', [(j, (j + k) % NX) for j in range(NX)])  19.1 us
    all_to_all x1, starting transfers between devices, on_device(): lax.all_to_all(outgoing, ('y', 'z'), split_axis=0, concat_axis=0, tiled=T...  16.8 us
    all_gather x1, blocking collectives, on_device(): deltas = lax.all_gather(delta, 'x', axis=0, tiled=False)  15.9 us
    all_to_all x1, starting transfers between devices, on_device(): lax.all_to_all(spread_out(keep, came, place_t, gate_block), ('y', 'z'), s...  12.7 us
    pallas_call x4, Pallas kernels, pre_part(): pl.pallas_call(pre_kernel, out_shape=jax.ShapeDtypeStruct((rows, w.shape[...  7.41 us
    pallas_call x4, Pallas kernels, pack(): pl.pallas_call(pack_kernel, out_shape=jax.ShapeDtypeStruct((rows, chunk),...  5.8 us
  transfers between devices with their start and end apart: 10, of which 7 were waited for; matrix products, arithmetic and copies ran while one was open for 2% of the time, Pallas kernels for 7%

profile of v2, /device:TPU:18, one launch (start us, length us, event | category | flops | bytes accessed | tf_op | source)
XLA Modules:
  0.0 155.0 jit_solution(2961443098506151123)
XLA Ops:
  0.6 0.0 copy-start
  0.7 0.7 broadcast_compare_fusion
  1.4 0.1 convolution_convert_fusion.3
  1.5 0.8 subtract_add_fusion
  2.3 0.2 select_reduce_fusion
  2.5 0.1 sub.48
  2.6 1.3 fusion
  3.8 0.0 copy-start.3
  3.8 1.1 broadcast_in_dim.28
  5.0 16.8 %all-to-all-start = ((bf16[64,8,1024]{2,1,0:T(8,128)(2,1)}), bf16[64,8,1024]{2,1,0:T(8,128)(2,1)}, u32[]{:S(2)}, u32[]{:S(2)}) async-start(bf16[64,8,1024]{2,1,0:T(8,128)(2,1)} %bitcast.47), calls=%async_computation | async-start | bytes 2097152 | tf_op jit(solution)/shard_map/all_to_all | solution.py:198
  21.8 0.1 pad_add_fusion.where_ref
  21.9 0.0 copy-done.3
  21.9 0.0 copy-done.1
  21.9 0.0 copy-done.2
  21.9 1.7 %pack_weights.4 = bf16[1536,256]{1,0:T(8,128)(2,1)} custom-call(s32[2]{0:T(128)S(1)} %pad_add_fusion.where_ref, bf16[4096,128]{1,0:T(8,128)(2,1)S(1)} %bitcast.33, bf16[4096,128]{1,0:T(8,128)(2,1)S(1)} %bitcast.37, bf16[128,4096]{1,0:T(8,128)(2,1)S(1)} %bitcast.41), custom_call_target="tpu_custom_call" | custom-call | tf_op jit(solution)/shard_map/pack_weights/pallas_call | solution.py:66
  23.6 4.0 %collective-permute-start = (bf16[1536,256]{1,0:T(8,128)(2,1)}, bf16[1536,256]{1,0:T(8,128)(2,1)}, u32[]{:S(2)}, u32[]{:S(2)}) collective-permute-start(bf16[1536,256]{1,0:T(8,128)(2,1)} %pack_weights.4), channel_id=1, source_target_pairs={{0,4},{2,6},{4,0},{6,2},{1,5},{3,7},{5,1},{7,3},{8,12},{10,14},{12... | collective-permute-start | bytes 2359304 | tf_op jit(solution)/shard_map/ppermute | solution.py:28
  27.7 0.1 pad_add_fusion.1.where_ref
  27.7 1.7 %pack_weights.5 = bf16[1536,256]{1,0:T(8,128)(2,1)} custom-call(s32[2]{0:T(128)S(1)} %pad_add_fusion.1.where_ref, bf16[4096,128]{1,0:T(8,128)(2,1)S(1)} %bitcast.34, bf16[4096,128]{1,0:T(8,128)(2,1)S(1)} %bitcast.38, bf16[128,4096]{1,0:T(8,128)(2,1)S(1)} %bitcast.42), custom_call_target="tpu_custom_call" | custom-call | tf_op jit(solution)/shard_map/pack_weights/pallas_call | solution.py:66
  29.4 1.9 %collective-permute-start.1 = (bf16[1536,256]{1,0:T(8,128)(2,1)}, bf16[1536,256]{1,0:T(8,128)(2,1)}, u32[]{:S(2)}, u32[]{:S(2)}) collective-permute-start(bf16[1536,256]{1,0:T(8,128)(2,1)} %pack_weights.5), channel_id=1, source_target_pairs={{0,2},{2,4},{4,6},{6,0},{1,3},{3,5},{5,7},{7,1},{8,10},{10,12},{12... | collective-permute-start | bytes 2359304 | tf_op jit(solution)/shard_map/ppermute | solution.py:28
  31.4 0.1 pad_add_fusion.2.where_ref
  31.4 1.7 %pack_weights.6 = bf16[1536,256]{1,0:T(8,128)(2,1)} custom-call(s32[2]{0:T(128)S(1)} %pad_add_fusion.2.where_ref, bf16[4096,128]{1,0:T(8,128)(2,1)S(1)} %bitcast.35, bf16[4096,128]{1,0:T(8,128)(2,1)S(1)} %bitcast.39, bf16[128,4096]{1,0:T(8,128)(2,1)S(1)} %bitcast.43), custom_call_target="tpu_custom_call" | custom-call | tf_op jit(solution)/shard_map/pack_weights/pallas_call | solution.py:66
  33.1 3.9 %collective-permute-start.3 = (bf16[1536,256]{1,0:T(8,128)(2,1)}, bf16[1536,256]{1,0:T(8,128)(2,1)}, u32[]{:S(2)}, u32[]{:S(2)}) collective-permute-start(bf16[1536,256]{1,0:T(8,128)(2,1)} %pack_weights.6), channel_id=1, source_target_pairs={{0,6},{2,0},{4,2},{6,4},{1,7},{3,1},{5,3},{7,5},{8,14},{10,8},{12,... | collective-permute-start | bytes 2359304 | tf_op jit(solution)/shard_map/ppermute | solution.py:28
  37.1 0.2 convert_reduce_fusion
  37.3 10.5 %collective-permute-done.w_ref.w2 = bf16[1536,256]{1,0:T(8,128)(2,1)} collective-permute-done((bf16[1536,256]{1,0:T(8,128)(2,1)}, bf16[1536,256]{1,0:T(8,128)(2,1)}, u32[]{:S(2)}, u32[]{:S(2)}) %collective-permute-start) | collective-permute-done | bytes 786464 | tf_op jit(solution)/shard_map/ppermute | solution.py:28
  47.8 15.1 %collective-permute-done.1.w_ref.w1 = bf16[1536,256]{1,0:T(8,128)(2,1)} collective-permute-done((bf16[1536,256]{1,0:T(8,128)(2,1)}, bf16[1536,256]{1,0:T(8,128)(2,1)}, u32[]{:S(2)}, u32[]{:S(2)}) %collective-permute-start.1) | collective-permute-done | bytes 786464 | tf_op jit(solution)/shard_map/ppermute | solution.py:28
  63.0 0.0 all-to-all-done
  63.0 1.8 %convolution_convert_fusion.own_ref = bf16[384,1024]{1,0:T(8,128)(2,1)S(1)} fusion(bf16[512,1024]{1,0:T(8,128)(2,1)} %bitcast.3, s32[384]{0:T(512)S(1)} %multiply_add_fusion), kind=kOutput, calls=%fused_computation | convolution fusion | flops 403243008 | bytes 1836544 | tf_op jit(solution)/shard_map/dot_general | solution.py:209
  64.8 0.0 copy-start.4
  64.8 1.9 %collective-permute-start.2 = (bf16[384,1024]{1,0:T(8,128)(2,1)S(1)}, bf16[384,1024]{1,0:T(8,128)(2,1)S(1)}, u32[]{:S(2)}, u32[]{:S(2)}) collective-permute-start(bf16[384,1024]{1,0:T(8,128)(2,1)S(1)} %convolution_convert_fusion.own_ref), channel_id=1, source_target_pairs={{0,1},{1,0},{2,3},{3,2},{4,5},{5,4},{6,7},{7,6},{8,9},{9,8},{10,11... | collective-permute-start | bytes 2359304 | tf_op jit(solution)/shard_map/ppermute | solution.py:24
  66.7 0.0 collective-permute-done.3.w_ref.w3
  66.8 2.2 %collective-permute-done.2.other_ref = bf16[384,1024]{1,0:T(8,128)(2,1)S(1)} collective-permute-done((bf16[384,1024]{1,0:T(8,128)(2,1)S(1)}, bf16[384,1024]{1,0:T(8,128)(2,1)S(1)}, u32[]{:S(2)}, u32[]{:S(2)}) %collective-permute-start.2) | collective-permute-done | bytes 786464 | tf_op jit(solution)/shard_map/ppermute | solution.py:24
  69.0 2.0 %pre_part.4 = bf16[384,384]{1,0:T(8,128)(2,1)S(1)} custom-call(bf16[384,1024]{1,0:T(8,128)(2,1)S(1)} %convolution_convert_fusion.own_ref, bf16[384,1024]{1,0:T(8,128)(2,1)S(1)} %collective-permute-done.2.other_ref, bf16[1536,256]{1,0:T(8,128)(2,1)} %collective-permute-done.w_ref.w2), custom_call_target="tpu_custom_call" | custom-call | tf_op jit(solution)/shard_map/pre_part/pallas_call | solution.py:100
  71.0 1.9 %collective-permute-start.4 = (bf16[384,384]{1,0:T(8,128)(2,1)S(1)}, bf16[384,384]{1,0:T(8,128)(2,1)}, u32[]{:S(2)}, u32[]{:S(2)}) collective-permute-start(bf16[384,384]{1,0:T(8,128)(2,1)S(1)} %pre_part.4), channel_id=1, source_target_pairs={{0,4},{2,6},{4,0},{6,2},{1,5},{3,7},{5,1},{7,3},{8,12},{10,14},{12... | collective-permute-start | bytes 884744 | tf_op jit(solution)/shard_map/ppermute | solution.py:28
  72.9 2.4 %pre_part.5 = bf16[384,384]{1,0:T(8,128)(2,1)} custom-call(bf16[384,1024]{1,0:T(8,128)(2,1)S(1)} %convolution_convert_fusion.own_ref, bf16[384,1024]{1,0:T(8,128)(2,1)S(1)} %collective-permute-done.2.other_ref, bf16[1536,256]{1,0:T(8,128)(2,1)} %collective-permute-done.3.w_ref.w3), custom_call_target="tpu_custom_call" | custom-call | tf_op jit(solution)/shard_map/pre_part/pallas_call | solution.py:100
  75.4 3.8 %collective-permute-start.5 = (bf16[384,384]{1,0:T(8,128)(2,1)}, bf16[384,384]{1,0:T(8,128)(2,1)}, u32[]{:S(2)}, u32[]{:S(2)}) collective-permute-start(bf16[384,384]{1,0:T(8,128)(2,1)} %pre_part.5), channel_id=1, source_target_pairs={{0,2},{2,4},{4,6},{6,0},{1,3},{3,5},{5,7},{7,1},{8,10},{10,12},{12... | collective-permute-start | bytes 884744 | tf_op jit(solution)/shard_map/ppermute | solution.py:28
  79.2 0.0 copy-done.4
  79.2 0.0 copy-done.6
  79.2 2.4 %pre_part.6 = bf16[384,384]{1,0:T(8,128)(2,1)} custom-call(bf16[384,1024]{1,0:T(8,128)(2,1)S(1)} %convolution_convert_fusion.own_ref, bf16[384,1024]{1,0:T(8,128)(2,1)S(1)} %collective-permute-done.2.other_ref, bf16[1536,256]{1,0:T(8,128)(2,1)} %collective-permute-done.1.w_ref.w1), custom_call_target="tpu_custom_call" | custom-call | tf_op jit(solution)/shard_map/pre_part/pallas_call | solution.py:100
  81.6 3.5 %collective-permute-start.6 = (bf16[384,384]{1,0:T(8,128)(2,1)}, bf16[384,384]{1,0:T(8,128)(2,1)}, u32[]{:S(2)}, u32[]{:S(2)}) collective-permute-start(bf16[384,384]{1,0:T(8,128)(2,1)} %pre_part.6), channel_id=1, source_target_pairs={{0,6},{2,0},{4,2},{6,4},{1,7},{3,1},{5,3},{7,5},{8,14},{10,8},{12,... | collective-permute-start | bytes 884744 | tf_op jit(solution)/shard_map/ppermute | solution.py:28
  85.1 0.1 pad_add_fusion.3.where_ref
  85.2 0.8 pack_weights.7.w_ref.w0
  86.0 0.0 copy-done
  86.0 0.0 copy-start.8
  86.0 0.3 copy-done.5
  86.3 0.2 copy-done.7
  86.6 0.6 pre_part.7
  87.1 0.0 copy-done.8
  87.2 0.0 collective-permute-done.4
  87.2 2.7 %collective-permute-done.5 = bf16[384,384]{1,0:T(8,128)(2,1)} collective-permute-done((bf16[384,384]{1,0:T(8,128)(2,1)}, bf16[384,384]{1,0:T(8,128)(2,1)}, u32[]{:S(2)}, u32[]{:S(2)}) %collective-permute-start.5) | collective-permute-done | bytes 294944 | tf_op jit(solution)/shard_map/ppermute | solution.py:28
  89.9 2.9 %collective-permute-done.6 = bf16[384,384]{1,0:T(8,128)(2,1)} collective-permute-done((bf16[384,384]{1,0:T(8,128)(2,1)}, bf16[384,384]{1,0:T(8,128)(2,1)}, u32[]{:S(2)}, u32[]{:S(2)}) %collective-permute-start.6) | collective-permute-done | bytes 294944 | tf_op jit(solution)/shard_map/ppermute | solution.py:28
  92.7 1.3 convert_add_fusion
  94.0 0.2 multiply_convert_fusion.1
  94.3 15.9 %all-gather = bf16[1600,256]{1,0:T(8,128)(2,1)S(1)} all-gather(bf16[400,256]{1,0:T(8,128)(2,1)S(1)} %pad_maximum_fusion), channel_id=2, replica_groups=mesh['y'=8,'z'=8,'x'=4,'c'=2] {'x'}, dimensions={0}, use_global_device_ids=true | all-gather | bytes 1024000 | tf_op jit(solution)/shard_map/all_gather | solution.py:227
  110.4 2.6 %input_grads.1 = (bf16[400,512]{1,0:T(8,128)(2,1)S(1)}, f32[384,512]{1,0:T(8,128)S(1)}) custom-call(s32[4]{0:T(128)S(1)} %and_select_fusion.from_ref, bf16[4,400,256]{2,1,0:T(8,128)(2,1)S(1)} %bitcast.46, bf16[1536,256]{1,0:T(8,128)(2,1)S(1)} %copy-done.9, bf16[1536,256]{1,0:T(8,128)(2,1)} %collective-permute-done.1.w_ref.w1, ...), custom_call_target="tpu_custom_call" | custom-call | tf_op jit(solution)/shard_map/input_grads/pallas_call | solution.py:129
  113.0 1.9 %collective-permute-start.7 = (bf16[400,512]{1,0:T(8,128)(2,1)S(1)}, bf16[400,512]{1,0:T(8,128)(2,1)S(1)}, u32[]{:S(2)}, u32[]{:S(2)}) collective-permute-start(bf16[400,512]{1,0:T(8,128)(2,1)S(1)} %get-tuple-element.15), channel_id=1, source_target_pairs={{0,1},{1,0},{2,3},{3,2},{4,5},{5,4},{6,7},{7,6},{8,9},{9,8},{10,11... | collective-permute-start | bytes 1228808 | tf_op jit(solution)/shard_map/ppermute | solution.py:24
  115.0 0.1 fusion.1.place_ref
  115.1 1.6 %collective-permute-done.7.came_ref = bf16[400,512]{1,0:T(8,128)(2,1)S(1)} collective-permute-done((bf16[400,512]{1,0:T(8,128)(2,1)S(1)}, bf16[400,512]{1,0:T(8,128)(2,1)S(1)}, u32[]{:S(2)}, u32[]{:S(2)}) %collective-permute-start.7) | collective-permute-done | bytes 409632 | tf_op jit(solution)/shard_map/ppermute | solution.py:24
  116.7 1.3 rows_to_slots.1
  118.0 12.7 %all-to-all-start.1 = ((bf16[64,8,640]{2,1,0:T(8,128)(2,1)}), bf16[64,8,640]{2,1,0:T(8,128)(2,1)S(1)}, u32[]{:S(2)}, u32[]{:S(2)}) async-start(bf16[64,8,640]{2,1,0:T(8,128)(2,1)} %bitcast.17), calls=%async_computation.1 | async-start | bytes 1310720 | tf_op jit(solution)/shard_map/all_to_all | solution.py:242
  130.7 0.1 fusion.10
  130.8 22.4 %all-to-all-done.1 = bf16[64,8,640]{2,1,0:T(8,128)(2,1)S(1)} async-done(((bf16[64,8,640]{2,1,0:T(8,128)(2,1)}), bf16[64,8,640]{2,1,0:T(8,128)(2,1)S(1)}, u32[]{:S(2)}, u32[]{:S(2)}) %all-to-all-start.1) | async-done | bytes 655392 | tf_op jit(solution)/shard_map/all_to_all | solution.py:242
  153.3 0.1 reduce_sum.52
  153.4 0.6 slice_add_fusion
  154.0 1.0 convolution_convert_fusion.1
  (33 shorter events, 0.4 us)
Async XLA Ops:
  0.6 85.3 %copy-start = (f32[8,384]{1,0:T(8,128)S(1)}, f32[8,384]{1,0:T(8,128)}, u32[]{:S(2)}) copy-start(f32[8,384]{1,0:T(8,128)} %param.13) | copy-start | bytes 36868
  3.8 18.1 %copy-start.3 = (bf16[1,128,4096]{2,1,0:T(8,128)(2,1)S(1)}, bf16[1,128,4096]{2,1,0:T(8,128)(2,1)}, u32[]{:S(2)}) copy-start(bf16[1,128,4096]{2,1,0:T(8,128)(2,1)} %param.11) | copy-start | bytes 3145732
  5.0 16.9 %copy-start.1 = (bf16[1,4096,128]{2,1,0:T(8,128)(2,1)S(1)}, bf16[1,4096,128]{2,1,0:T(8,128)(2,1)}, u32[]{:S(2)}) copy-start(bf16[1,4096,128]{2,1,0:T(8,128)(2,1)} %param.9) | copy-start | bytes 3145732
  5.0 16.9 %copy-start.2 = (bf16[1,4096,128]{2,1,0:T(8,128)(2,1)S(1)}, bf16[1,4096,128]{2,1,0:T(8,128)(2,1)}, u32[]{:S(2)}) copy-start(bf16[1,4096,128]{2,1,0:T(8,128)(2,1)} %param.10) | copy-start | bytes 3145732
  5.0 58.0 %all-to-all-start = ((bf16[64,8,1024]{2,1,0:T(8,128)(2,1)}), bf16[64,8,1024]{2,1,0:T(8,128)(2,1)}, u32[]{:S(2)}, u32[]{:S(2)}) async-start(bf16[64,8,1024]{2,1,0:T(8,128)(2,1)} %bitcast.47), calls=%async_computation | async-start | bytes 2097152 | tf_op jit(solution)/shard_map/all_to_all | solution.py:198
  23.6 24.2 %collective-permute-start = (bf16[1536,256]{1,0:T(8,128)(2,1)}, bf16[1536,256]{1,0:T(8,128)(2,1)}, u32[]{:S(2)}, u32[]{:S(2)}) collective-permute-start(bf16[1536,256]{1,0:T(8,128)(2,1)} %pack_weights.4), channel_id=1, source_target_pairs={{0,4},{2,6},{4,0},{6,2},{1,5},{3,7},{5,1},{7,3},{8,12},{10,14},{12... | collective-permute-start | bytes 2359304 | tf_op jit(solution)/shard_map/ppermute | solution.py:28
  29.4 33.5 %collective-permute-start.1 = (bf16[1536,256]{1,0:T(8,128)(2,1)}, bf16[1536,256]{1,0:T(8,128)(2,1)}, u32[]{:S(2)}, u32[]{:S(2)}) collective-permute-start(bf16[1536,256]{1,0:T(8,128)(2,1)} %pack_weights.5), channel_id=1, source_target_pairs={{0,2},{2,4},{4,6},{6,0},{1,3},{3,5},{5,7},{7,1},{8,10},{10,12},{12... | collective-permute-start | bytes 2359304 | tf_op jit(solution)/shard_map/ppermute | solution.py:28
  33.1 33.6 %collective-permute-start.3 = (bf16[1536,256]{1,0:T(8,128)(2,1)}, bf16[1536,256]{1,0:T(8,128)(2,1)}, u32[]{:S(2)}, u32[]{:S(2)}) collective-permute-start(bf16[1536,256]{1,0:T(8,128)(2,1)} %pack_weights.6), channel_id=1, source_target_pairs={{0,6},{2,0},{4,2},{6,4},{1,7},{3,1},{5,3},{7,5},{8,14},{10,8},{12,... | collective-permute-start | bytes 2359304 | tf_op jit(solution)/shard_map/ppermute | solution.py:28
  64.8 14.4 %copy-start.4 = (bf16[384,1024]{1,0:T(8,128)(2,1)}, bf16[384,1024]{1,0:T(8,128)(2,1)S(1)}, u32[]{:S(2)}) copy-start(bf16[384,1024]{1,0:T(8,128)(2,1)S(1)} %convolution_convert_fusion.own_ref) | copy-start | bytes 2359300
  64.8 4.2 %collective-permute-start.2 = (bf16[384,1024]{1,0:T(8,128)(2,1)S(1)}, bf16[384,1024]{1,0:T(8,128)(2,1)S(1)}, u32[]{:S(2)}, u32[]{:S(2)}) collective-permute-start(bf16[384,1024]{1,0:T(8,128)(2,1)S(1)} %convolution_convert_fusion.own_ref), channel_id=1, source_target_pairs={{0,1},{1,0},{2,3},{3,2},{4,5},{5,4},{6,7},{7,6},{8,9},{9,8},{10,11... | collective-permute-start | bytes 2359304 | tf_op jit(solution)/shard_map/ppermute | solution.py:24
  69.0 10.2 %copy-start.6 = (bf16[384,1024]{1,0:T(8,128)(2,1)}, bf16[384,1024]{1,0:T(8,128)(2,1)S(1)}, u32[]{:S(2)}) copy-start(bf16[384,1024]{1,0:T(8,128)(2,1)S(1)} %collective-permute-done.2.other_ref) | copy-start | bytes 2359300
  71.0 16.2 %collective-permute-start.4 = (bf16[384,384]{1,0:T(8,128)(2,1)S(1)}, bf16[384,384]{1,0:T(8,128)(2,1)}, u32[]{:S(2)}, u32[]{:S(2)}) collective-permute-start(bf16[384,384]{1,0:T(8,128)(2,1)S(1)} %pre_part.4), channel_id=1, source_target_pairs={{0,4},{2,6},{4,0},{6,2},{1,5},{3,7},{5,1},{7,3},{8,12},{10,14},{12... | collective-permute-start | bytes 884744 | tf_op jit(solution)/shard_map/ppermute | solution.py:28
  75.4 14.5 %collective-permute-start.5 = (bf16[384,384]{1,0:T(8,128)(2,1)}, bf16[384,384]{1,0:T(8,128)(2,1)}, u32[]{:S(2)}, u32[]{:S(2)}) collective-permute-start(bf16[384,384]{1,0:T(8,128)(2,1)} %pre_part.5), channel_id=1, source_target_pairs={{0,2},{2,4},{4,6},{6,0},{1,3},{3,5},{5,7},{7,1},{8,10},{10,12},{12... | collective-permute-start | bytes 884744 | tf_op jit(solution)/shard_map/ppermute | solution.py:28
  81.6 11.1 %collective-permute-start.6 = (bf16[384,384]{1,0:T(8,128)(2,1)}, bf16[384,384]{1,0:T(8,128)(2,1)}, u32[]{:S(2)}, u32[]{:S(2)}) collective-permute-start(bf16[384,384]{1,0:T(8,128)(2,1)} %pre_part.6), channel_id=1, source_target_pairs={{0,6},{2,0},{4,2},{6,4},{1,7},{3,1},{5,3},{7,5},{8,14},{10,8},{12,... | collective-permute-start | bytes 884744 | tf_op jit(solution)/shard_map/ppermute | solution.py:28
  85.2 1.1 copy-start.5
  85.2 1.4 copy-start.7
  86.0 1.2 copy-start.8
  94.2 16.1 %copy-start.9 = (bf16[1536,256]{1,0:T(8,128)(2,1)S(1)}, bf16[1536,256]{1,0:T(8,128)(2,1)}, u32[]{:S(2)}) copy-start(bf16[1536,256]{1,0:T(8,128)(2,1)} %copy-done.8) | copy-start | bytes 2359300
  113.0 3.6 %collective-permute-start.7 = (bf16[400,512]{1,0:T(8,128)(2,1)S(1)}, bf16[400,512]{1,0:T(8,128)(2,1)S(1)}, u32[]{:S(2)}, u32[]{:S(2)}) collective-permute-start(bf16[400,512]{1,0:T(8,128)(2,1)S(1)} %get-tuple-element.15), channel_id=1, source_target_pairs={{0,1},{1,0},{2,3},{3,2},{4,5},{5,4},{6,7},{7,6},{8,9},{9,8},{10,11... | collective-permute-start | bytes 1228808 | tf_op jit(solution)/shard_map/ppermute | solution.py:24
  118.0 35.2 %all-to-all-start.1 = ((bf16[64,8,640]{2,1,0:T(8,128)(2,1)}), bf16[64,8,640]{2,1,0:T(8,128)(2,1)S(1)}, u32[]{:S(2)}, u32[]{:S(2)}) async-start(bf16[64,8,640]{2,1,0:T(8,128)(2,1)} %bitcast.17), calls=%async_computation.1 | async-start | bytes 1310720 | tf_op jit(solution)/shard_map/all_to_all | solution.py:242

commit v3 on v2

--- a/solution.py
+++ b/solution.py
@@ -34,43 +34,79 @@
     return hi, lo
 
 
-def pack_kernel(where_ref, gate_ref, up_ref, down_ref, out_ref, sems):
+def prologue_kernel(
+    where_ref, chosen_ref, tokens_ref, grads_ref, gate_ref, up_ref, down_ref,
+    out0, out1, out2, out3, rows_ref, pick_ref, sems,
+):
     hid = gate_ref.shape[1]
-    half = out_ref.shape[0] // 3
-    chunk = out_ref.shape[1]
-    copies = []
-    for h in range(NC):
-        start = pl.multiple_of(where_ref[h], half)
-        rows = pl.ds(h * half, half)
-        copies.append((gate_ref.at[pl.ds(start, half), :], out_ref.at[rows, pl.ds(0, hid)]))
-        copies.append((up_ref.at[pl.ds(start, half), :], out_ref.at[rows, pl.ds(hid, hid)]))
-        for q in range(half // chunk):
-            begin = pl.multiple_of(start + q * chunk, chunk)
-            low = NC * half + (h * (half // chunk) + q) * hid
-            copies.append((down_ref.at[:, pl.ds(begin, chunk)], out_ref.at[pl.ds(low, hid), :]))
+    token_rows, feat = tokens_ref.shape
+    chunk = 2 * hid
+    outs = (out0, out1, out2, out3)
     started = []
-    for i, (src, dst) in enumerate(copies):
-        copy = pltpu.make_async_copy(src, dst, sems.at[i])
-        copy.start()
-        started.append(copy)
+    for k in (1, 3, 2, 0):
+        for h in range(NC):
+            start = pl.multiple_of(where_ref[k * NC + h], feat)
+            rows = pl.ds(h * feat, feat)
+            copies = [
+                (gate_ref.at[pl.ds(start, feat), :], outs[k].at[rows, pl.ds(0, hid)]),
+                (up_ref.at[pl.ds(start, feat), :], outs[k].at[rows, pl.ds(hid, hid)]),
+            ]
+            for q in range(feat // chunk):
+                begin = pl.multiple_of(start + q * chunk, chunk)
+                low = NC * feat + (h * (feat // chunk) + q) * hid
+                copies.append((down_ref.at[:, pl.ds(begin, chunk)], outs[k].at[pl.ds(low, hid), :]))
+            for src, dst in copies:
+                copy = pltpu.make_async_copy(src, dst, sems.at[len(started)])
+                copy.start()
+                started.append(copy)
+    experts, capacity = chosen_ref.shape
+    local = chosen_ref[...] - where_ref[NX * NC]
+    mine = (local >= 0) & (local < token_rows)
+    earlier = lax.broadcasted_iota(jnp.int32, (capacity, capacity), 0) < lax.broadcasted_iota(
+        jnp.int32, (capacity, capacity), 1
+    )
+    earlier = jnp.where(earlier, 1.0, 0.0).astype(BF)
+    rank = jnp.dot(jnp.where(mine, 1.0, 0.0).astype(BF), earlier, preferred_element_type=F32)
+    key = jnp.where(mine, (local + 1).astype(F32), 0.0)
+    slot = lax.broadcasted_iota(jnp.int32, (SLOTS, capacity), 0).astype(F32)
+    token = lax.broadcasted_iota(jnp.int32, (SLOTS, token_rows), 1).astype(F32) + 1.0
+    picks = []
+    for e in range(experts):
+        hit = slot == jnp.broadcast_to(rank[e : e + 1, :], slot.shape)
+        row = jnp.sum(jnp.where(hit, jnp.broadcast_to(key[e : e + 1, :], slot.shape), 0.0), axis=1, keepdims=True)
+        picks.append(jnp.where(row == token, 1.0, 0.0))
+    pick = jnp.concatenate(picks, axis=0).astype(BF)
+    pick_ref[...] = pick
+    for i, ref in enumerate((tokens_ref, grads_ref)):
+        picked = jnp.dot(pick, ref[...], preferred_element_type=F32)
+        picked = picked.reshape(experts, 1, SLOTS, feat)
+        picked = jnp.broadcast_to(picked, (experts, NZ, SLOTS, feat)).reshape(experts * NZ * SLOTS, feat)
+        rows_ref[:, i * feat : (i + 1) * feat] = picked.astype(BF)
     for copy in started:
         copy.wait()
 
 
-def pack(gate, up, down, where, feat):
+def prologue(where, chosen, tokens, grads, gate, up, down):
+    token_rows, feat = tokens.shape
     hid = gate.shape[1]
     chunk = 2 * hid
-    rows = NC * feat + NC * (feat // chunk) * hid
-    n = NC * (2 + feat // chunk)
-    anywhere = pl.BlockSpec(memory_space=pltpu.HBM)
-    return pl.pallas_call(
-        pack_kernel,
-        out_shape=jax.ShapeDtypeStruct((rows, chunk), BF),
-        in_specs=[pl.BlockSpec(memory_space=pltpu.SMEM), anywhere, anywhere, anywhere],
+    packed = jax.ShapeDtypeStruct((NC * feat + NC * (feat // chunk) * hid, chunk), BF)
+    n = NX * NC * (2 + feat // chunk)
+    picks = chosen.shape[0] * SLOTS
+    hbm = pl.BlockSpec(memory_space=pltpu.HBM)
+    vmem = pl.BlockSpec(memory_space=pltpu.VMEM)
+    return pl.pallas_call(
+        prologue_kernel,
+        out_shape=(
+            packed, packed, packed, packed,
+            jax.ShapeDtypeStruct((picks * NZ, 2 * feat), BF),
+            jax.ShapeDtypeStruct((picks, token_rows), BF),
+        ),
+        in_specs=[pl.BlockSpec(memory_space=pltpu.SMEM), vmem, vmem, vmem, hbm, hbm, hbm],
         scratch_shapes=[pltpu.SemaphoreType.DMA((n,))],
-        compiler_params=pltpu.CompilerParams(vmem_limit_bytes=VMEM),
-        name="pack_weights",
-    )(where, gate, up, down)
+        compiler_params=pltpu.CompilerParams(vmem_limit_bytes=60 * 1024 * 1024),
+        name="prologue",
+    )(where, chosen, tokens, grads, gate, up, down)
 
 
 def pre_kernel(own_ref, other_ref, w_ref, out_ref):
@@ -170,34 +206,20 @@
     all_slots = peers * SLOTS
     wide = NC * feat
 
-    packed = {}
-    for k in (2, 1, 3, 0):
-        dest = (x_index + k) % NX
-        where = jnp.stack([dest * wide + c_index * feat, dest * wide + (1 - c_index) * feat])
-        packed[k] = pack(gate_weight[0], up_weight[0], down_weight[0], where, feat)
+    dest = (x_index + jnp.arange(NX, dtype=jnp.int32)) % NX * wide
+    where = jnp.stack([dest + c_index * feat, dest + (1 - c_index) * feat], axis=1).reshape(-1)
+    where = jnp.concatenate([where, (exp_index * token_rows)[None]]).astype(jnp.int32)
+    *packed, outgoing, pick = prologue(
+        where, chosen, tokens, output_grad, gate_weight[0], up_weight[0], down_weight[0]
+    )
     weights = {0: packed[0]}
-    for k in (2, 1, 3):
+    for k in (1, 3, 2):
         weights[k] = shift_x(packed[k], k)
+    got = lax.all_to_all(outgoing, ("y", "z"), split_axis=0, concat_axis=0, tiled=True)
+    got, weights[1] = lax.optimization_barrier((got, weights[1]))
 
     source = chosen // token_rows
-    local_rows = chosen - exp_index * token_rows
-    mine = source == exp_index
     order = jnp.arange(capacity, dtype=jnp.int32)
-    earlier = (order[:, None] < order[None, :]).astype(BF)
-    rank = jnp.dot(mine.astype(BF), earlier, preferred_element_type=F32).astype(jnp.int32)
-    slot_ids = jnp.arange(SLOTS, dtype=jnp.int32)
-    hit = mine[:, None, :] & (rank[:, None, :] == slot_ids[None, :, None])
-    send_row = jnp.sum(jnp.where(hit, local_rows[:, None, :] + 1, 0), axis=2) - 1
-    token_ids = jnp.arange(token_rows, dtype=jnp.int32)
-    pick = (send_row.reshape(-1)[:, None] == token_ids[None, :]).astype(BF)
-    both = jnp.concatenate([tokens, output_grad], axis=1)
-    picked = jnp.dot(pick, both, preferred_element_type=F32).astype(BF)
-    outgoing = jnp.broadcast_to(
-        picked.reshape(expert_count, 1, SLOTS, 2 * feat), (expert_count, NZ, SLOTS, 2 * feat)
-    ).reshape(all_slots, 2 * feat)
-    got = lax.all_to_all(outgoing, ("y", "z"), split_axis=0, concat_axis=0, tiled=True)
-    got, weights[2], weights[1] = lax.optimization_barrier((got, weights[2], weights[1]))
-
     my_source = lax.dynamic_index_in_dim(source, expert, 0, keepdims=False)
     my_gates = lax.dynamic_index_in_dim(gate_values, expert, 0, keepdims=False)
     same = (my_source[:, None] == my_source[None, :]) & (order[None, :] < order[:, None])
@@ -208,10 +230,9 @@
     place_t = (my_slot[None, :] == slot_order[:, None]).astype(BF)
     own = jnp.dot(place, got, preferred_element_type=F32).astype(BF)
     other = swap_cores(own)
-    other, weights[3] = lax.optimization_barrier((other, weights[3]))
-
+    other, weights[3], weights[2] = lax.optimization_barrier((other, weights[3], weights[2]))
     sums = None
-    for k in (2, 1, 3, 0):
+    for k in (1, 3, 0, 2):
         part = pre_part(own, other, weights[(NX - k) % NX])
         part = (shift_x(part, k) if k else part).astype(F32)
         sums = part if sums is None else sums + part

time: 156 us -> 143 us (0.917)
  the two profiles are of different devices: /device:TPU:18 before, /device:TPU:16 now
where the time goes in v3:
time: 143 us; the launch traced here: 142 us
  blocking collectives  50.2 us (35%)
  starting transfers between devices  42.2 us (30%)
  waiting for transfers between devices  32.3 us (23%)
  Pallas kernels  9.5 us (7%)
  other arithmetic  3.02 us (2%)
  matrix products  2.81 us (2%)
  local copies, waits for them, and re-layouts  1.43 us (1%)
    all_to_all x1, blocking collectives, on_device(): lax.all_to_all(spread_out(keep, came, place_t, gate_block), ('y', 'z'), s...  35 us
    ppermute x6, waiting for transfers between devices, shift_x(): return lax.ppermute(a, 'x', [(j, (j + k) % NX) for j in range(NX)])  23.1 us
    ppermute x6, starting transfers between devices, shift_x(): return lax.ppermute(a, 'x', [(j, (j + k) % NX) for j in range(NX)])  21.7 us
    all_to_all x1, starting transfers between devices, on_device(): lax.all_to_all(outgoing, ('y', 'z'), split_axis=0, concat_axis=0, tiled=T...  16.7 us
    all_gather x1, blocking collectives, on_device(): deltas = lax.all_gather(delta, 'x', axis=0, tiled=False)  15.2 us
    all_to_all x1, waiting for transfers between devices, on_device(): lax.all_to_all(outgoing, ('y', 'z'), split_axis=0, concat_axis=0, tiled=T...  7.6 us
    pallas_call x1, Pallas kernels, prologue(): pl.pallas_call(prologue_kernel, out_shape=(packed, packed, packed, packed...  5.23 us
    ppermute x2, starting transfers between devices, swap_cores(): return lax.ppermute(a, 'c', [(0, 1), (1, 0)])  3.84 us
  transfers between devices with their start and end apart: 9, of which 6 were waited for; matrix products, arithmetic and copies ran while one was open for 2% of the time, Pallas kernels for 1%

profile of v3, /device:TPU:16, one launch (start us, length us, event | category | flops | bytes accessed | tf_op | source)
XLA Modules:
  0.0 142.5 jit_solution(11071853549766917199)
XLA Ops:
  0.6 0.0 copy-start
  0.7 0.1 pad_add_fusion
  0.7 0.1 reshape.98
  0.8 0.7 pad_add_fusion.1.where_ref
  1.5 5.2 %prologue.1 = (bf16[1536,256]{1,0:T(8,128)(2,1)}, bf16[1536,256]{1,0:T(8,128)(2,1)}, bf16[1536,256]{1,0:T(8,128)(2,1)}, bf16[1536,256]{1,0:T(8,128)(2,1)}, bf16[...) custom-call(s32[9]{0:T(128)} %pad_add_fusion.1.where_ref, s32[8,384]{1,0:T(8,128)} %chosen_ref.1, ...), custom_call_target="tpu_custom_call" | custom-call | tf_op jit(solution)/shard_map/prologue/pallas_call | solution.py:98
  6.7 16.7 %all-to-all-start = ((bf16[64,8,1024]{2,1,0:T(8,128)(2,1)}), bf16[64,8,1024]{2,1,0:T(8,128)(2,1)}, u32[]{:S(2)}, u32[]{:S(2)}) async-start(bf16[64,8,1024]{2,1,0:T(8,128)(2,1)} %bitcast.30), calls=%async_computation | async-start | bytes 2097152 | tf_op jit(solution)/shard_map/all_to_all | solution.py:218
  23.4 3.4 %collective-permute-start = (bf16[1536,256]{1,0:T(8,128)(2,1)}, bf16[1536,256]{1,0:T(8,128)(2,1)S(1)}, u32[]{:S(2)}, u32[]{:S(2)}) collective-permute-start(bf16[1536,256]{1,0:T(8,128)(2,1)} %get-tuple-element.17), channel_id=1, source_target_pairs={{0,2},{2,4},{4,6},{6,0},{1,3},{3,5},{5,7},{7,1},{8,10},{10,12},{12... | collective-permute-start | bytes 2359304 | tf_op jit(solution)/shard_map/ppermute | solution.py:28
  26.8 3.7 %collective-permute-start.2 = (bf16[1536,256]{1,0:T(8,128)(2,1)}, bf16[1536,256]{1,0:T(8,128)(2,1)S(1)}, u32[]{:S(2)}, u32[]{:S(2)}) collective-permute-start(bf16[1536,256]{1,0:T(8,128)(2,1)} %get-tuple-element.19), channel_id=1, source_target_pairs={{0,6},{2,0},{4,2},{6,4},{1,7},{3,1},{5,3},{7,5},{8,14},{10,8},{12,... | collective-permute-start | bytes 2359304 | tf_op jit(solution)/shard_map/ppermute | solution.py:28
  30.5 3.7 %collective-permute-start.3 = (bf16[1536,256]{1,0:T(8,128)(2,1)}, bf16[1536,256]{1,0:T(8,128)(2,1)S(1)}, u32[]{:S(2)}, u32[]{:S(2)}) collective-permute-start(bf16[1536,256]{1,0:T(8,128)(2,1)} %get-tuple-element.20), channel_id=1, source_target_pairs={{0,4},{2,6},{4,0},{6,2},{1,5},{3,7},{5,1},{7,3},{8,12},{10,14},{12... | collective-permute-start | bytes 2359304 | tf_op jit(solution)/shard_map/ppermute | solution.py:28
  34.2 0.7 fusion.14
  34.9 0.2 convert_reduce_fusion
  35.2 11.0 %collective-permute-done.w_ref.w1 = bf16[1536,256]{1,0:T(8,128)(2,1)S(1)} collective-permute-done((bf16[1536,256]{1,0:T(8,128)(2,1)}, bf16[1536,256]{1,0:T(8,128)(2,1)S(1)}, u32[]{:S(2)}, u32[]{:S(2)}) %collective-permute-start) | collective-permute-done | bytes 786464 | tf_op jit(solution)/shard_map/ppermute | solution.py:28
  46.2 7.6 %all-to-all-done = bf16[64,8,1024]{2,1,0:T(8,128)(2,1)} async-done(((bf16[64,8,1024]{2,1,0:T(8,128)(2,1)}), bf16[64,8,1024]{2,1,0:T(8,128)(2,1)}, u32[]{:S(2)}, u32[]{:S(2)}) %all-to-all-start) | async-done | bytes 1048608 | tf_op jit(solution)/shard_map/all_to_all | solution.py:218
  53.8 1.8 %convolution_convert_fusion.own_ref = bf16[384,1024]{1,0:T(8,128)(2,1)S(1)} fusion(bf16[512,1024]{1,0:T(8,128)(2,1)} %bitcast.7, s32[384]{0:T(512)S(1)} %multiply_add_fusion), kind=kOutput, calls=%fused_computation | convolution fusion | flops 403243008 | bytes 1836544 | tf_op jit(solution)/shard_map/dot_general | solution.py:231
  55.7 1.9 %collective-permute-start.1 = (bf16[384,1024]{1,0:T(8,128)(2,1)S(1)}, bf16[384,1024]{1,0:T(8,128)(2,1)S(1)}, u32[]{:S(2)}, u32[]{:S(2)}) collective-permute-start(bf16[384,1024]{1,0:T(8,128)(2,1)S(1)} %convolution_convert_fusion.own_ref), channel_id=1, source_target_pairs={{0,1},{1,0},{2,3},{3,2},{4,5},{5,4},{6,7},{7,6},{8,9},{9,8},{10,11... | collective-permute-start | bytes 2359304 | tf_op jit(solution)/shard_map/ppermute | solution.py:24
  57.6 6.0 %collective-permute-done.2.w_ref.w3 = bf16[1536,256]{1,0:T(8,128)(2,1)S(1)} collective-permute-done((bf16[1536,256]{1,0:T(8,128)(2,1)}, bf16[1536,256]{1,0:T(8,128)(2,1)S(1)}, u32[]{:S(2)}, u32[]{:S(2)}) %collective-permute-start.2) | collective-permute-done | bytes 786464 | tf_op jit(solution)/shard_map/ppermute | solution.py:28
  63.6 0.0 collective-permute-done.3.w_ref.w2
  63.6 0.0 copy-start.2
  63.6 0.0 collective-permute-done.1.other_ref
  63.6 0.6 pre_part.4
  64.2 4.6 %collective-permute-start.4 = (bf16[384,384]{1,0:T(8,128)(2,1)S(1)}, bf16[384,384]{1,0:T(8,128)(2,1)S(1)}, u32[]{:S(2)}, u32[]{:S(2)}) collective-permute-start(bf16[384,384]{1,0:T(8,128)(2,1)S(1)} %pre_part.4), channel_id=1, source_target_pairs={{0,2},{2,4},{4,6},{6,0},{1,3},{3,5},{5,7},{7,1},{8,10},{10,12},{12... | collective-permute-start | bytes 884744 | tf_op jit(solution)/shard_map/ppermute | solution.py:28
  68.8 0.6 pre_part.5
  69.4 0.0 copy-start.1
  69.4 2.9 %collective-permute-start.5 = (bf16[384,384]{1,0:T(8,128)(2,1)S(1)}, bf16[384,384]{1,0:T(8,128)(2,1)S(1)}, u32[]{:S(2)}, u32[]{:S(2)}) collective-permute-start(bf16[384,384]{1,0:T(8,128)(2,1)S(1)} %pre_part.5), channel_id=1, source_target_pairs={{0,6},{2,0},{4,2},{6,4},{1,7},{3,1},{5,3},{7,5},{8,14},{10,8},{12,... | collective-permute-start | bytes 884744 | tf_op jit(solution)/shard_map/ppermute | solution.py:28
  72.3 0.0 copy-done.2
  72.3 0.6 pre_part.7
  72.9 3.4 %collective-permute-start.6 = (bf16[384,384]{1,0:T(8,128)(2,1)S(1)}, bf16[384,384]{1,0:T(8,128)(2,1)S(1)}, u32[]{:S(2)}, u32[]{:S(2)}) collective-permute-start(bf16[384,384]{1,0:T(8,128)(2,1)S(1)} %pre_part.7), channel_id=1, source_target_pairs={{0,4},{2,6},{4,0},{6,2},{1,5},{3,7},{5,1},{7,3},{8,12},{10,14},{12... | collective-permute-start | bytes 884744 | tf_op jit(solution)/shard_map/ppermute | solution.py:28
  76.3 0.0 copy-done
  76.3 0.0 copy-done.1
  76.3 0.6 pre_part.6
  76.9 0.0 collective-permute-done.4
  76.9 4.0 %collective-permute-done.5 = bf16[384,384]{1,0:T(8,128)(2,1)S(1)} collective-permute-done((bf16[384,384]{1,0:T(8,128)(2,1)S(1)}, bf16[384,384]{1,0:T(8,128)(2,1)S(1)}, u32[]{:S(2)}, u32[]{:S(2)}) %collective-permute-start.5) | collective-permute-done | bytes 294944 | tf_op jit(solution)/shard_map/ppermute | solution.py:28
  80.9 2.1 %collective-permute-done.6 = bf16[384,384]{1,0:T(8,128)(2,1)S(1)} collective-permute-done((bf16[384,384]{1,0:T(8,128)(2,1)S(1)}, bf16[384,384]{1,0:T(8,128)(2,1)S(1)}, u32[]{:S(2)}, u32[]{:S(2)}) %collective-permute-start.6) | collective-permute-done | bytes 294944 | tf_op jit(solution)/shard_map/ppermute | solution.py:28
  83.0 0.1 convert_add_fusion
  83.2 0.2 multiply_convert_fusion.1
  83.5 15.2 %all-gather = bf16[1600,256]{1,0:T(8,128)(2,1)S(1)} all-gather(bf16[400,256]{1,0:T(8,128)(2,1)S(1)} %pad_maximum_fusion), channel_id=2, replica_groups=mesh['y'=8,'z'=8,'x'=4,'c'=2] {'x'}, dimensions={0}, use_global_device_ids=true | all-gather | bytes 1024000 | tf_op jit(solution)/shard_map/all_gather | solution.py:248
  98.9 0.0 copy-start.3
  98.9 1.1 copy-done.3
  100.0 1.5 %input_grads.1 = (bf16[400,512]{1,0:T(8,128)(2,1)S(1)}, f32[384,512]{1,0:T(8,128)S(1)}) custom-call(s32[4]{0:T(128)S(1)} %and_select_fusion.1.from_ref, bf16[4,400,256]{2,1,0:T(8,128)(2,1)S(1)} %bitcast.25, bf16[1536,256]{1,0:T(8,128)(2,1)S(1)} %copy-done.1, bf16[1536,256]{1,0:T(8,128)(2,1)S(1)} %collective-permute-done.w_ref.w1, ...), custom_call_target="tpu_custom_call" | custom-call | tf_op jit(solution)/shard_map/input_grads/pallas_call | solution.py:165
  101.6 1.9 %collective-permute-start.7 = (bf16[400,512]{1,0:T(8,128)(2,1)S(1)}, bf16[400,512]{1,0:T(8,128)(2,1)S(1)}, u32[]{:S(2)}, u32[]{:S(2)}) collective-permute-start(bf16[400,512]{1,0:T(8,128)(2,1)S(1)} %get-tuple-element.27), channel_id=1, source_target_pairs={{0,1},{1,0},{2,3},{3,2},{4,5},{5,4},{6,7},{7,6},{8,9},{9,8},{10,11... | collective-permute-start | bytes 1228808 | tf_op jit(solution)/shard_map/ppermute | solution.py:24
  103.5 0.1 fusion.place_ref
  103.6 1.6 %collective-permute-done.7.came_ref = bf16[400,512]{1,0:T(8,128)(2,1)S(1)} collective-permute-done((bf16[400,512]{1,0:T(8,128)(2,1)S(1)}, bf16[400,512]{1,0:T(8,128)(2,1)S(1)}, u32[]{:S(2)}, u32[]{:S(2)}) %collective-permute-start.7) | collective-permute-done | bytes 409632 | tf_op jit(solution)/shard_map/ppermute | solution.py:24
  105.3 0.5 rows_to_slots.1
  105.7 0.0 copy-start.4
  105.7 35.0 %all_to_all.24 = bf16[64,8,640]{2,1,0:T(8,128)(2,1)S(1)} all-to-all(bf16[64,8,640]{2,1,0:T(8,128)(2,1)S(1)} %bitcast.26), channel_id=1, replica_groups=mesh['y'=8,'z'=8,'x'=4,'c'=2] {'y','z'}, dimensions={0} | all-to-all | bytes 1310720 | tf_op jit(solution)/shard_map/all_to_all | solution.py:263
  140.8 0.1 reduce_sum.42
  140.9 0.6 slice_add_fusion
  141.5 0.0 copy-done.4
  141.5 1.0 convolution_convert_fusion.1
  (25 shorter events, 0.4 us)
Async XLA Ops:
  0.6 75.7 %copy-start = (f32[8,384]{1,0:T(8,128)S(1)}, f32[8,384]{1,0:T(8,128)}, u32[]{:S(2)}) copy-start(f32[8,384]{1,0:T(8,128)} %param.13) | copy-start | bytes 36868
  6.7 47.1 %all-to-all-start = ((bf16[64,8,1024]{2,1,0:T(8,128)(2,1)}), bf16[64,8,1024]{2,1,0:T(8,128)(2,1)}, u32[]{:S(2)}, u32[]{:S(2)}) async-start(bf16[64,8,1024]{2,1,0:T(8,128)(2,1)} %bitcast.30), calls=%async_computation | async-start | bytes 2097152 | tf_op jit(solution)/shard_map/all_to_all | solution.py:218
  23.4 22.8 %collective-permute-start = (bf16[1536,256]{1,0:T(8,128)(2,1)}, bf16[1536,256]{1,0:T(8,128)(2,1)S(1)}, u32[]{:S(2)}, u32[]{:S(2)}) collective-permute-start(bf16[1536,256]{1,0:T(8,128)(2,1)} %get-tuple-element.17), channel_id=1, source_target_pairs={{0,2},{2,4},{4,6},{6,0},{1,3},{3,5},{5,7},{7,1},{8,10},{10,12},{12... | collective-permute-start | bytes 2359304 | tf_op jit(solution)/shard_map/ppermute | solution.py:28
  26.8 36.8 %collective-permute-start.2 = (bf16[1536,256]{1,0:T(8,128)(2,1)}, bf16[1536,256]{1,0:T(8,128)(2,1)S(1)}, u32[]{:S(2)}, u32[]{:S(2)}) collective-permute-start(bf16[1536,256]{1,0:T(8,128)(2,1)} %get-tuple-element.19), channel_id=1, source_target_pairs={{0,6},{2,0},{4,2},{6,4},{1,7},{3,1},{5,3},{7,5},{8,14},{10,8},{12,... | collective-permute-start | bytes 2359304 | tf_op jit(solution)/shard_map/ppermute | solution.py:28
  30.5 33.1 %collective-permute-start.3 = (bf16[1536,256]{1,0:T(8,128)(2,1)}, bf16[1536,256]{1,0:T(8,128)(2,1)S(1)}, u32[]{:S(2)}, u32[]{:S(2)}) collective-permute-start(bf16[1536,256]{1,0:T(8,128)(2,1)} %get-tuple-element.20), channel_id=1, source_target_pairs={{0,4},{2,6},{4,0},{6,2},{1,5},{3,7},{5,1},{7,3},{8,12},{10,14},{12... | collective-permute-start | bytes 2359304 | tf_op jit(solution)/shard_map/ppermute | solution.py:28
  55.7 8.0 %collective-permute-start.1 = (bf16[384,1024]{1,0:T(8,128)(2,1)S(1)}, bf16[384,1024]{1,0:T(8,128)(2,1)S(1)}, u32[]{:S(2)}, u32[]{:S(2)}) collective-permute-start(bf16[384,1024]{1,0:T(8,128)(2,1)S(1)} %convolution_convert_fusion.own_ref), channel_id=1, source_target_pairs={{0,1},{1,0},{2,3},{3,2},{4,5},{5,4},{6,7},{7,6},{8,9},{9,8},{10,11... | collective-permute-start | bytes 2359304 | tf_op jit(solution)/shard_map/ppermute | solution.py:24
  63.6 8.7 %copy-start.2 = (bf16[1536,256]{1,0:T(8,128)(2,1)}, bf16[1536,256]{1,0:T(8,128)(2,1)S(1)}, u32[]{:S(2)}) copy-start(bf16[1536,256]{1,0:T(8,128)(2,1)S(1)} %collective-permute-done.3.w_ref.w2) | copy-start | bytes 2359300
  64.2 12.7 %collective-permute-start.4 = (bf16[384,384]{1,0:T(8,128)(2,1)S(1)}, bf16[384,384]{1,0:T(8,128)(2,1)S(1)}, u32[]{:S(2)}, u32[]{:S(2)}) collective-permute-start(bf16[384,384]{1,0:T(8,128)(2,1)S(1)} %pre_part.4), channel_id=1, source_target_pairs={{0,2},{2,4},{4,6},{6,0},{1,3},{3,5},{5,7},{7,1},{8,10},{10,12},{12... | collective-permute-start | bytes 884744 | tf_op jit(solution)/shard_map/ppermute | solution.py:28
  69.4 6.9 %copy-start.1 = (bf16[1536,256]{1,0:T(8,128)(2,1)S(1)}, bf16[1536,256]{1,0:T(8,128)(2,1)}, u32[]{:S(2)}) copy-start(bf16[1536,256]{1,0:T(8,128)(2,1)} %get-tuple-element.24.w_ref.w0) | copy-start | bytes 2359300
  69.4 11.5 %collective-permute-start.5 = (bf16[384,384]{1,0:T(8,128)(2,1)S(1)}, bf16[384,384]{1,0:T(8,128)(2,1)S(1)}, u32[]{:S(2)}, u32[]{:S(2)}) collective-permute-start(bf16[384,384]{1,0:T(8,128)(2,1)S(1)} %pre_part.5), channel_id=1, source_target_pairs={{0,6},{2,0},{4,2},{6,4},{1,7},{3,1},{5,3},{7,5},{8,14},{10,8},{12,... | collective-permute-start | bytes 884744 | tf_op jit(solution)/shard_map/ppermute | solution.py:28
  72.9 10.1 %collective-permute-start.6 = (bf16[384,384]{1,0:T(8,128)(2,1)S(1)}, bf16[384,384]{1,0:T(8,128)(2,1)S(1)}, u32[]{:S(2)}, u32[]{:S(2)}) collective-permute-start(bf16[384,384]{1,0:T(8,128)(2,1)S(1)} %pre_part.7), channel_id=1, source_target_pairs={{0,4},{2,6},{4,0},{6,2},{1,5},{3,7},{5,1},{7,3},{8,12},{10,14},{12... | collective-permute-start | bytes 884744 | tf_op jit(solution)/shard_map/ppermute | solution.py:28
  98.9 1.1 copy-start.3
  101.6 3.6 %collective-permute-start.7 = (bf16[400,512]{1,0:T(8,128)(2,1)S(1)}, bf16[400,512]{1,0:T(8,128)(2,1)S(1)}, u32[]{:S(2)}, u32[]{:S(2)}) collective-permute-start(bf16[400,512]{1,0:T(8,128)(2,1)S(1)} %get-tuple-element.27), channel_id=1, source_target_pairs={{0,1},{1,0},{2,3},{3,2},{4,5},{5,4},{6,7},{7,6},{8,9},{9,8},{10,11... | collective-permute-start | bytes 1228808 | tf_op jit(solution)/shard_map/ppermute | solution.py:24
  105.7 35.8 %copy-start.4 = (bf16[64,192]{1,0:T(8,128)(2,1)S(1)}, bf16[64,192]{1,0:T(8,128)(2,1)}, u32[]{:S(2)}) copy-start(bf16[64,192]{1,0:T(8,128)(2,1)} %get-tuple-element.15) | copy-start | bytes 73732

commit v4 on v3

--- a/solution.py
+++ b/solution.py
@@ -12,6 +12,7 @@
 BF = jnp.bfloat16
 F32 = jnp.float32
 VMEM = 12 * 1024 * 1024
+BIG_VMEM = 60 * 1024 * 1024
 CONTRACT = (((1,), (1,)), ((), ()))
 
 
@@ -34,33 +35,64 @@
     return hi, lo
 
 
-def prologue_kernel(
-    where_ref, chosen_ref, tokens_ref, grads_ref, gate_ref, up_ref, down_ref,
-    out0, out1, out2, out3, rows_ref, pick_ref, sems,
-):
+def start_packing(start_of, gate_ref, up_ref, down_ref, outs, sems):
     hid = gate_ref.shape[1]
-    token_rows, feat = tokens_ref.shape
     chunk = 2 * hid
-    outs = (out0, out1, out2, out3)
+    feat = outs[0].shape[0] // 3
     started = []
-    for k in (1, 3, 2, 0):
+    for k, out in enumerate(outs):
         for h in range(NC):
-            start = pl.multiple_of(where_ref[k * NC + h], feat)
+            start = pl.multiple_of(start_of[k * NC + h], feat)
             rows = pl.ds(h * feat, feat)
             copies = [
-                (gate_ref.at[pl.ds(start, feat), :], outs[k].at[rows, pl.ds(0, hid)]),
-                (up_ref.at[pl.ds(start, feat), :], outs[k].at[rows, pl.ds(hid, hid)]),
+                (gate_ref.at[pl.ds(start, feat), :], out.at[rows, pl.ds(0, hid)]),
+                (up_ref.at[pl.ds(start, feat), :], out.at[rows, pl.ds(hid, hid)]),
             ]
             for q in range(feat // chunk):
                 begin = pl.multiple_of(start + q * chunk, chunk)
                 low = NC * feat + (h * (feat // chunk) + q) * hid
-                copies.append((down_ref.at[:, pl.ds(begin, chunk)], outs[k].at[pl.ds(low, hid), :]))
+                copies.append((down_ref.at[:, pl.ds(begin, chunk)], out.at[pl.ds(low, hid), :]))
             for src, dst in copies:
                 copy = pltpu.make_async_copy(src, dst, sems.at[len(started)])
                 copy.start()
                 started.append(copy)
+    return started
+
+
+def packed_shape(hid, feat):
+    return jax.ShapeDtypeStruct((NC * feat + feat // 2 // hid * NC * hid, 2 * hid), BF)
+
+
+def pack_copies(hid, feat, count):
+    return pltpu.SemaphoreType.DMA((count * NC * (2 + feat // 2 // hid),))
+
+
+def pack_kernel(where_ref, gate_ref, up_ref, down_ref, *refs):
+    for copy in start_packing(where_ref, gate_ref, up_ref, down_ref, refs[:-1], refs[-1]):
+        copy.wait()
+
+
+def pack_weights(where, gate, up, down, feat, limit):
+    hid = gate.shape[1]
+    count = where.shape[0] // NC
+    hbm = pl.BlockSpec(memory_space=pltpu.HBM)
+    return pl.pallas_call(
+        pack_kernel,
+        out_shape=(packed_shape(hid, feat),) * count,
+        in_specs=[pl.BlockSpec(memory_space=pltpu.SMEM), hbm, hbm, hbm],
+        scratch_shapes=[pack_copies(hid, feat, count)],
+        compiler_params=pltpu.CompilerParams(vmem_limit_bytes=limit),
+        name="pack_weights",
+    )(where, gate, up, down)
+
+
+def pick_kernel(
+    base_ref, chosen_ref, tokens_ref, grads_ref, gate_ref, up_ref, down_ref, rows_ref, pick_ref, out_ref, sems
+):
+    started = start_packing(base_ref, gate_ref, up_ref, down_ref, [out_ref], sems)
+    token_rows, feat = tokens_ref.shape
     experts, capacity = chosen_ref.shape
-    local = chosen_ref[...] - where_ref[NX * NC]
+    local = chosen_ref[...] - base_ref[NC]
     mine = (local >= 0) & (local < token_rows)
     earlier = lax.broadcasted_iota(jnp.int32, (capacity, capacity), 0) < lax.broadcasted_iota(
         jnp.int32, (capacity, capacity), 1
@@ -86,27 +118,24 @@
         copy.wait()
 
 
-def prologue(where, chosen, tokens, grads, gate, up, down):
+def pick_rows(base, chosen, tokens, grads, gate, up, down):
+    hid = gate.shape[1]
+    hbm = pl.BlockSpec(memory_space=pltpu.HBM)
     token_rows, feat = tokens.shape
-    hid = gate.shape[1]
-    chunk = 2 * hid
-    packed = jax.ShapeDtypeStruct((NC * feat + NC * (feat // chunk) * hid, chunk), BF)
-    n = NX * NC * (2 + feat // chunk)
     picks = chosen.shape[0] * SLOTS
-    hbm = pl.BlockSpec(memory_space=pltpu.HBM)
     vmem = pl.BlockSpec(memory_space=pltpu.VMEM)
     return pl.pallas_call(
-        prologue_kernel,
+        pick_kernel,
         out_shape=(
-            packed, packed, packed, packed,
             jax.ShapeDtypeStruct((picks * NZ, 2 * feat), BF),
             jax.ShapeDtypeStruct((picks, token_rows), BF),
+            packed_shape(hid, feat),
         ),
         in_specs=[pl.BlockSpec(memory_space=pltpu.SMEM), vmem, vmem, vmem, hbm, hbm, hbm],
-        scratch_shapes=[pltpu.SemaphoreType.DMA((n,))],
-        compiler_params=pltpu.CompilerParams(vmem_limit_bytes=60 * 1024 * 1024),
-        name="prologue",
-    )(where, chosen, tokens, grads, gate, up, down)
+        scratch_shapes=[pack_copies(hid, feat, 1)],
+        compiler_params=pltpu.CompilerParams(vmem_limit_bytes=BIG_VMEM),
+        name="pick_rows",
+    )(base, chosen, tokens, grads, gate, up, down)
 
 
 def pre_kernel(own_ref, other_ref, w_ref, out_ref):
@@ -206,17 +235,23 @@
     all_slots = peers * SLOTS
     wide = NC * feat
 
-    dest = (x_index + jnp.arange(NX, dtype=jnp.int32)) % NX * wide
-    where = jnp.stack([dest + c_index * feat, dest + (1 - c_index) * feat], axis=1).reshape(-1)
-    where = jnp.concatenate([where, (exp_index * token_rows)[None]]).astype(jnp.int32)
-    *packed, outgoing, pick = prologue(
-        where, chosen, tokens, output_grad, gate_weight[0], up_weight[0], down_weight[0]
-    )
-    weights = {0: packed[0]}
-    for k in (1, 3, 2):
-        weights[k] = shift_x(packed[k], k)
+    own_weights = gate_weight[0], up_weight[0], down_weight[0]
+
+    def starts(k):
+        dest = (x_index + k) % NX * wide
+        return [dest + c_index * feat, dest + (1 - c_index) * feat]
+
+    outgoing, pick, out_2 = pick_rows(
+        jnp.stack(starts(2) + [exp_index * token_rows]), chosen, tokens, output_grad, *own_weights
+    )
     got = lax.all_to_all(outgoing, ("y", "z"), split_axis=0, concat_axis=0, tiled=True)
-    got, weights[1] = lax.optimization_barrier((got, weights[1]))
+    weights = {2: shift_x(out_2, 2)}
+    out_1, out_3, weights[0] = pack_weights(
+        jnp.stack(starts(1) + starts(3) + starts(0)), *own_weights, feat, BIG_VMEM
+    )
+    weights[1] = shift_x(out_1, 1)
+    weights[3] = shift_x(out_3, 3)
+    got, weights[2] = lax.optimization_barrier((got, weights[2]))
 
     source = chosen // token_rows
     order = jnp.arange(capacity, dtype=jnp.int32)
@@ -230,9 +265,9 @@
     place_t = (my_slot[None, :] == slot_order[:, None]).astype(BF)
     own = jnp.dot(place, got, preferred_element_type=F32).astype(BF)
     other = swap_cores(own)
-    other, weights[3], weights[2] = lax.optimization_barrier((other, weights[3], weights[2]))
+    other, weights[1], weights[3] = lax.optimization_barrier((other, weights[1], weights[3]))
     sums = None
-    for k in (1, 3, 0, 2):
+    for k in (2, 1, 3, 0):
         part = pre_part(own, other, weights[(NX - k) % NX])
         part = (shift_x(part, k) if k else part).astype(F32)
         sums = part if sums is None else sums + part

time: 143 us -> 140 us (0.979)
  the two profiles are of different devices: /device:TPU:16 before, /device:TPU:18 now
where the time goes in v4:
time: 140 us; the launch traced here: 139 us
  blocking collectives  50.3 us (36%)
  starting transfers between devices  40.5 us (29%)
  waiting for transfers between devices  28.3 us (20%)
  Pallas kernels  11.8 us (8%)
  other arithmetic  2.84 us (2%)
  matrix products  2.81 us (2%)
  local copies, waits for them, and re-layouts  1.98 us (1%)
    all_to_all x1, blocking collectives, on_device(): lax.all_to_all(spread_out(keep, came, place_t, gate_block), ('y', 'z'), s...  35 us
    ppermute x6, waiting for transfers between devices, shift_x(): return lax.ppermute(a, 'x', [(j, (j + k) % NX) for j in range(NX)])  20.2 us
    ppermute x6, starting transfers between devices, shift_x(): return lax.ppermute(a, 'x', [(j, (j + k) % NX) for j in range(NX)])  19.8 us
    all_to_all x1, starting transfers between devices, on_device(): lax.all_to_all(outgoing, ('y', 'z'), split_axis=0, concat_axis=0, tiled=T...  16.8 us
    all_gather x1, blocking collectives, on_device(): deltas = lax.all_gather(delta, 'x', axis=0, tiled=False)  15.3 us
    all_to_all x1, waiting for transfers between devices, on_device(): lax.all_to_all(outgoing, ('y', 'z'), split_axis=0, concat_axis=0, tiled=T...  6.48 us
    pallas_call x1, Pallas kernels, pack_weights(): pl.pallas_call(pack_kernel, out_shape=(packed_shape(hid, feat),) * count,...  3.91 us
    ppermute x2, starting transfers between devices, swap_cores(): return lax.ppermute(a, 'c', [(0, 1), (1, 0)])  3.84 us
  transfers between devices with their start and end apart: 9, of which 6 were waited for; matrix products, arithmetic and copies ran while one was open for 3% of the time, Pallas kernels for 4%

profile of v4, /device:TPU:18, one launch (start us, length us, event | category | flops | bytes accessed | tf_op | source)
XLA Modules:
  0.0 139.4 jit_solution(15864596404603000790)
XLA Ops:
  0.6 0.0 copy-start
  0.7 0.6 pad_add_fusion.base_ref
  1.2 3.5 %pick_rows.1 = (bf16[512,1024]{1,0:T(8,128)(2,1)}, bf16[64,192]{1,0:T(8,128)(2,1)}, bf16[1536,256]{1,0:T(8,128)(2,1)}) custom-call(s32[3]{0:T(128)} %pad_add_fusion.base_ref, s32[8,384]{1,0:T(8,128)} %chosen_ref.1, bf16[192,512]{1,0:T(8,128)(2,1)} %tokens_ref.1, bf16[192,512]{1,0:T(8,128)(2,1)} %grads_ref.1, bf16[4096,128]{1,0:T(8,128)(2,1)} %bitcast.35, ...), custom_call_target="tpu_custom_call" | custom-call | tf_op jit(solution)/shard_map/pick_rows/pallas_call | solution.py:127
  4.8 0.0 copy-start.5
  4.8 16.8 %all-to-all-start = ((bf16[64,8,1024]{2,1,0:T(8,128)(2,1)}), bf16[64,8,1024]{2,1,0:T(8,128)(2,1)}, u32[]{:S(2)}, u32[]{:S(2)}) async-start(bf16[64,8,1024]{2,1,0:T(8,128)(2,1)} %bitcast.41), calls=%async_computation | async-start | bytes 2097152 | tf_op jit(solution)/shard_map/all_to_all | solution.py:247
  21.6 0.0 copy-done.5
  21.6 4.0 %collective-permute-start = (bf16[1536,256]{1,0:T(8,128)(2,1)S(1)}, bf16[1536,256]{1,0:T(8,128)(2,1)S(1)}, u32[]{:S(2)}, u32[]{:S(2)}) collective-permute-start(bf16[1536,256]{1,0:T(8,128)(2,1)S(1)} %copy-done.5), channel_id=1, source_target_pairs={{0,4},{2,6},{4,0},{6,2},{1,5},{3,7},{5,1},{7,3},{8,12},{10,14},{12... | collective-permute-start | bytes 2359304 | tf_op jit(solution)/shard_map/ppermute | solution.py:29
  25.7 0.6 stack.43.where_ref
  26.3 3.9 %pack_weights.1 = (bf16[1536,256]{1,0:T(8,128)(2,1)}, bf16[1536,256]{1,0:T(8,128)(2,1)}, bf16[1536,256]{1,0:T(8,128)(2,1)}) custom-call(s32[6]{0:T(128)} %stack.43.where_ref, bf16[4096,128]{1,0:T(8,128)(2,1)} %bitcast.36, bf16[4096,128]{1,0:T(8,128)(2,1)} %bitcast.38, bf16[128,4096]{1,0:T(8,128)(2,1)} %bitcast.40), custom_call_target="tpu_custom_call" | custom-call | tf_op jit(solution)/shard_map/pack_weights/pallas_call | solution.py:79
  30.2 1.9 %collective-permute-start.2 = (bf16[1536,256]{1,0:T(8,128)(2,1)}, bf16[1536,256]{1,0:T(8,128)(2,1)S(1)}, u32[]{:S(2)}, u32[]{:S(2)}) collective-permute-start(bf16[1536,256]{1,0:T(8,128)(2,1)} %get-tuple-element.19), channel_id=1, source_target_pairs={{0,2},{2,4},{4,6},{6,0},{1,3},{3,5},{5,7},{7,1},{8,10},{10,12},{12... | collective-permute-start | bytes 2359304 | tf_op jit(solution)/shard_map/ppermute | solution.py:29
  32.2 3.9 %collective-permute-start.3 = (bf16[1536,256]{1,0:T(8,128)(2,1)}, bf16[1536,256]{1,0:T(8,128)(2,1)S(1)}, u32[]{:S(2)}, u32[]{:S(2)}) collective-permute-start(bf16[1536,256]{1,0:T(8,128)(2,1)} %get-tuple-element.20), channel_id=1, source_target_pairs={{0,6},{2,0},{4,2},{6,4},{1,7},{3,1},{5,3},{7,5},{8,14},{10,8},{12,... | collective-permute-start | bytes 2359304 | tf_op jit(solution)/shard_map/ppermute | solution.py:29
  36.1 0.7 fusion.12
  36.8 0.2 convert_reduce_fusion
  37.1 8.5 %collective-permute-done.w_ref.w2 = bf16[1536,256]{1,0:T(8,128)(2,1)S(1)} collective-permute-done((bf16[1536,256]{1,0:T(8,128)(2,1)S(1)}, bf16[1536,256]{1,0:T(8,128)(2,1)S(1)}, u32[]{:S(2)}, u32[]{:S(2)}) %collective-permute-start) | collective-permute-done | bytes 786464 | tf_op jit(solution)/shard_map/ppermute | solution.py:29
  45.5 6.5 %all-to-all-done = bf16[64,8,1024]{2,1,0:T(8,128)(2,1)} async-done(((bf16[64,8,1024]{2,1,0:T(8,128)(2,1)}), bf16[64,8,1024]{2,1,0:T(8,128)(2,1)}, u32[]{:S(2)}, u32[]{:S(2)}) %all-to-all-start) | async-done | bytes 1048608 | tf_op jit(solution)/shard_map/all_to_all | solution.py:247
  52.0 1.8 %convolution_convert_fusion.own_ref = bf16[384,1024]{1,0:T(8,128)(2,1)S(1)} fusion(bf16[512,1024]{1,0:T(8,128)(2,1)} %bitcast.9, s32[384]{0:T(512)S(1)} %multiply_add_fusion), kind=kOutput, calls=%fused_computation | convolution fusion | flops 403243008 | bytes 1836544 | tf_op jit(solution)/shard_map/dot_general | solution.py:266
  53.9 1.9 %collective-permute-start.1 = (bf16[384,1024]{1,0:T(8,128)(2,1)S(1)}, bf16[384,1024]{1,0:T(8,128)(2,1)S(1)}, u32[]{:S(2)}, u32[]{:S(2)}) collective-permute-start(bf16[384,1024]{1,0:T(8,128)(2,1)S(1)} %convolution_convert_fusion.own_ref), channel_id=1, source_target_pairs={{0,1},{1,0},{2,3},{3,2},{4,5},{5,4},{6,7},{7,6},{8,9},{9,8},{10,11... | collective-permute-start | bytes 2359304 | tf_op jit(solution)/shard_map/ppermute | solution.py:25
  55.8 4.9 %collective-permute-done.2.w_ref.w1 = bf16[1536,256]{1,0:T(8,128)(2,1)S(1)} collective-permute-done((bf16[1536,256]{1,0:T(8,128)(2,1)}, bf16[1536,256]{1,0:T(8,128)(2,1)S(1)}, u32[]{:S(2)}, u32[]{:S(2)}) %collective-permute-start.2) | collective-permute-done | bytes 786464 | tf_op jit(solution)/shard_map/ppermute | solution.py:29
  60.7 0.0 collective-permute-done.3.w_ref.w3
  60.7 0.0 copy-start.2
  60.7 0.0 collective-permute-done.1.other_ref
  60.7 0.6 pre_part.4
  61.3 4.0 %collective-permute-start.4 = (bf16[384,384]{1,0:T(8,128)(2,1)S(1)}, bf16[384,384]{1,0:T(8,128)(2,1)S(1)}, u32[]{:S(2)}, u32[]{:S(2)}) collective-permute-start(bf16[384,384]{1,0:T(8,128)(2,1)S(1)} %pre_part.4), channel_id=1, source_target_pairs={{0,4},{2,6},{4,0},{6,2},{1,5},{3,7},{5,1},{7,3},{8,12},{10,14},{12... | collective-permute-start | bytes 884744 | tf_op jit(solution)/shard_map/ppermute | solution.py:29
  65.2 0.0 copy-done.2
  65.2 0.6 pre_part.5
  65.8 0.0 copy-start.1
  65.8 2.1 %collective-permute-start.5 = (bf16[384,384]{1,0:T(8,128)(2,1)S(1)}, bf16[384,384]{1,0:T(8,128)(2,1)S(1)}, u32[]{:S(2)}, u32[]{:S(2)}) collective-permute-start(bf16[384,384]{1,0:T(8,128)(2,1)S(1)} %pre_part.5), channel_id=1, source_target_pairs={{0,2},{2,4},{4,6},{6,0},{1,3},{3,5},{5,7},{7,1},{8,10},{10,12},{12... | collective-permute-start | bytes 884744 | tf_op jit(solution)/shard_map/ppermute | solution.py:29
  67.9 0.6 pre_part.6
  68.5 3.9 %collective-permute-start.6 = (bf16[384,384]{1,0:T(8,128)(2,1)S(1)}, bf16[384,384]{1,0:T(8,128)(2,1)S(1)}, u32[]{:S(2)}, u32[]{:S(2)}) collective-permute-start(bf16[384,384]{1,0:T(8,128)(2,1)S(1)} %pre_part.6), channel_id=1, source_target_pairs={{0,6},{2,0},{4,2},{6,4},{1,7},{3,1},{5,3},{7,5},{8,14},{10,8},{12,... | collective-permute-start | bytes 884744 | tf_op jit(solution)/shard_map/ppermute | solution.py:29
  72.4 0.0 copy-done
  72.4 0.0 copy-done.1
  72.5 0.6 pre_part.7
  73.0 0.6 collective-permute-done.4
  73.6 6.3 %collective-permute-done.5 = bf16[384,384]{1,0:T(8,128)(2,1)S(1)} collective-permute-done((bf16[384,384]{1,0:T(8,128)(2,1)S(1)}, bf16[384,384]{1,0:T(8,128)(2,1)S(1)}, u32[]{:S(2)}, u32[]{:S(2)}) %collective-permute-start.5) | collective-permute-done | bytes 294944 | tf_op jit(solution)/shard_map/ppermute | solution.py:29
  79.9 0.0 collective-permute-done.6
  79.9 0.1 convert_add_fusion
  80.0 0.2 multiply_convert_fusion.1
  80.4 15.3 %all-gather = bf16[1600,256]{1,0:T(8,128)(2,1)S(1)} all-gather(bf16[400,256]{1,0:T(8,128)(2,1)S(1)} %pad_maximum_fusion), channel_id=2, replica_groups=mesh['y'=8,'z'=8,'x'=4,'c'=2] {'x'}, dimensions={0}, use_global_device_ids=true | all-gather | bytes 1024000 | tf_op jit(solution)/shard_map/all_gather | solution.py:283
  95.8 0.0 copy-start.3
  95.8 1.1 copy-done.3
  96.9 1.5 %input_grads.1 = (bf16[400,512]{1,0:T(8,128)(2,1)S(1)}, f32[384,512]{1,0:T(8,128)S(1)}) custom-call(s32[4]{0:T(128)S(1)} %and_select_fusion.1.from_ref, bf16[4,400,256]{2,1,0:T(8,128)(2,1)S(1)} %bitcast.33, bf16[1536,256]{1,0:T(8,128)(2,1)S(1)} %copy-done.1, bf16[1536,256]{1,0:T(8,128)(2,1)S(1)} %collective-permute-done.2.w_ref.w1, ...), custom_call_target="tpu_custom_call" | custom-call | tf_op jit(solution)/shard_map/input_grads/pallas_call | solution.py:194
  98.5 1.9 %collective-permute-start.7 = (bf16[400,512]{1,0:T(8,128)(2,1)S(1)}, bf16[400,512]{1,0:T(8,128)(2,1)S(1)}, u32[]{:S(2)}, u32[]{:S(2)}) collective-permute-start(bf16[400,512]{1,0:T(8,128)(2,1)S(1)} %get-tuple-element.27), channel_id=1, source_target_pairs={{0,1},{1,0},{2,3},{3,2},{4,5},{5,4},{6,7},{7,6},{8,9},{9,8},{10,11... | collective-permute-start | bytes 1228808 | tf_op jit(solution)/shard_map/ppermute | solution.py:25
  100.4 0.1 fusion.place_ref
  100.5 1.6 %collective-permute-done.7.came_ref = bf16[400,512]{1,0:T(8,128)(2,1)S(1)} collective-permute-done((bf16[400,512]{1,0:T(8,128)(2,1)S(1)}, bf16[400,512]{1,0:T(8,128)(2,1)S(1)}, u32[]{:S(2)}, u32[]{:S(2)}) %collective-permute-start.7) | collective-permute-done | bytes 409632 | tf_op jit(solution)/shard_map/ppermute | solution.py:25
  102.2 0.5 rows_to_slots.1
  102.7 0.0 copy-start.4
  102.7 35.0 %all_to_all.24 = bf16[64,8,640]{2,1,0:T(8,128)(2,1)S(1)} all-to-all(bf16[64,8,640]{2,1,0:T(8,128)(2,1)S(1)} %bitcast.34), channel_id=1, replica_groups=mesh['y'=8,'z'=8,'x'=4,'c'=2] {'y','z'}, dimensions={0} | all-to-all | bytes 1310720 | tf_op jit(solution)/shard_map/all_to_all | solution.py:298
  137.7 0.1 reduce_sum.42
  137.8 0.6 slice_add_fusion
  138.4 0.0 copy-done.4
  138.4 1.0 convolution_convert_fusion.1
  (24 shorter events, 0.4 us)
Async XLA Ops:
  0.6 71.8 %copy-start = (f32[8,384]{1,0:T(8,128)S(1)}, f32[8,384]{1,0:T(8,128)}, u32[]{:S(2)}) copy-start(f32[8,384]{1,0:T(8,128)} %param.13) | copy-start | bytes 36868
  4.8 16.8 %copy-start.5 = (bf16[1536,256]{1,0:T(8,128)(2,1)S(1)}, bf16[1536,256]{1,0:T(8,128)(2,1)}, u32[]{:S(2)}) copy-start(bf16[1536,256]{1,0:T(8,128)(2,1)} %get-tuple-element.17) | copy-start | bytes 2359300
  4.8 47.2 %all-to-all-start = ((bf16[64,8,1024]{2,1,0:T(8,128)(2,1)}), bf16[64,8,1024]{2,1,0:T(8,128)(2,1)}, u32[]{:S(2)}, u32[]{:S(2)}) async-start(bf16[64,8,1024]{2,1,0:T(8,128)(2,1)} %bitcast.41), calls=%async_computation | async-start | bytes 2097152 | tf_op jit(solution)/shard_map/all_to_all | solution.py:247
  21.6 23.9 %collective-permute-start = (bf16[1536,256]{1,0:T(8,128)(2,1)S(1)}, bf16[1536,256]{1,0:T(8,128)(2,1)S(1)}, u32[]{:S(2)}, u32[]{:S(2)}) collective-permute-start(bf16[1536,256]{1,0:T(8,128)(2,1)S(1)} %copy-done.5), channel_id=1, source_target_pairs={{0,4},{2,6},{4,0},{6,2},{1,5},{3,7},{5,1},{7,3},{8,12},{10,14},{12... | collective-permute-start | bytes 2359304 | tf_op jit(solution)/shard_map/ppermute | solution.py:29
  30.2 30.4 %collective-permute-start.2 = (bf16[1536,256]{1,0:T(8,128)(2,1)}, bf16[1536,256]{1,0:T(8,128)(2,1)S(1)}, u32[]{:S(2)}, u32[]{:S(2)}) collective-permute-start(bf16[1536,256]{1,0:T(8,128)(2,1)} %get-tuple-element.19), channel_id=1, source_target_pairs={{0,2},{2,4},{4,6},{6,0},{1,3},{3,5},{5,7},{7,1},{8,10},{10,12},{12... | collective-permute-start | bytes 2359304 | tf_op jit(solution)/shard_map/ppermute | solution.py:29
  32.2 28.5 %collective-permute-start.3 = (bf16[1536,256]{1,0:T(8,128)(2,1)}, bf16[1536,256]{1,0:T(8,128)(2,1)S(1)}, u32[]{:S(2)}, u32[]{:S(2)}) collective-permute-start(bf16[1536,256]{1,0:T(8,128)(2,1)} %get-tuple-element.20), channel_id=1, source_target_pairs={{0,6},{2,0},{4,2},{6,4},{1,7},{3,1},{5,3},{7,5},{8,14},{10,8},{12,... | collective-permute-start | bytes 2359304 | tf_op jit(solution)/shard_map/ppermute | solution.py:29
  53.9 6.8 %collective-permute-start.1 = (bf16[384,1024]{1,0:T(8,128)(2,1)S(1)}, bf16[384,1024]{1,0:T(8,128)(2,1)S(1)}, u32[]{:S(2)}, u32[]{:S(2)}) collective-permute-start(bf16[384,1024]{1,0:T(8,128)(2,1)S(1)} %convolution_convert_fusion.own_ref), channel_id=1, source_target_pairs={{0,1},{1,0},{2,3},{3,2},{4,5},{5,4},{6,7},{7,6},{8,9},{9,8},{10,11... | collective-permute-start | bytes 2359304 | tf_op jit(solution)/shard_map/ppermute | solution.py:25
  60.7 4.6 %copy-start.2 = (bf16[1536,256]{1,0:T(8,128)(2,1)}, bf16[1536,256]{1,0:T(8,128)(2,1)S(1)}, u32[]{:S(2)}) copy-start(bf16[1536,256]{1,0:T(8,128)(2,1)S(1)} %collective-permute-done.3.w_ref.w3) | copy-start | bytes 2359300
  61.3 12.3 %collective-permute-start.4 = (bf16[384,384]{1,0:T(8,128)(2,1)S(1)}, bf16[384,384]{1,0:T(8,128)(2,1)S(1)}, u32[]{:S(2)}, u32[]{:S(2)}) collective-permute-start(bf16[384,384]{1,0:T(8,128)(2,1)S(1)} %pre_part.4), channel_id=1, source_target_pairs={{0,4},{2,6},{4,0},{6,2},{1,5},{3,7},{5,1},{7,3},{8,12},{10,14},{12... | collective-permute-start | bytes 884744 | tf_op jit(solution)/shard_map/ppermute | solution.py:29
  65.8 6.6 %copy-start.1 = (bf16[1536,256]{1,0:T(8,128)(2,1)S(1)}, bf16[1536,256]{1,0:T(8,128)(2,1)}, u32[]{:S(2)}) copy-start(bf16[1536,256]{1,0:T(8,128)(2,1)} %get-tuple-element.25.w_ref.w0) | copy-start | bytes 2359300
  65.8 14.1 %collective-permute-start.5 = (bf16[384,384]{1,0:T(8,128)(2,1)S(1)}, bf16[384,384]{1,0:T(8,128)(2,1)S(1)}, u32[]{:S(2)}, u32[]{:S(2)}) collective-permute-start(bf16[384,384]{1,0:T(8,128)(2,1)S(1)} %pre_part.5), channel_id=1, source_target_pairs={{0,2},{2,4},{4,6},{6,0},{1,3},{3,5},{5,7},{7,1},{8,10},{10,12},{12... | collective-permute-start | bytes 884744 | tf_op jit(solution)/shard_map/ppermute | solution.py:29
  68.5 11.4 %collective-permute-start.6 = (bf16[384,384]{1,0:T(8,128)(2,1)S(1)}, bf16[384,384]{1,0:T(8,128)(2,1)S(1)}, u32[]{:S(2)}, u32[]{:S(2)}) collective-permute-start(bf16[384,384]{1,0:T(8,128)(2,1)S(1)} %pre_part.6), channel_id=1, source_target_pairs={{0,6},{2,0},{4,2},{6,4},{1,7},{3,1},{5,3},{7,5},{8,14},{10,8},{12,... | collective-permute-start | bytes 884744 | tf_op jit(solution)/shard_map/ppermute | solution.py:29
  95.8 1.1 copy-start.3
  98.5 3.6 %collective-permute-start.7 = (bf16[400,512]{1,0:T(8,128)(2,1)S(1)}, bf16[400,512]{1,0:T(8,128)(2,1)S(1)}, u32[]{:S(2)}, u32[]{:S(2)}) collective-permute-start(bf16[400,512]{1,0:T(8,128)(2,1)S(1)} %get-tuple-element.27), channel_id=1, source_target_pairs={{0,1},{1,0},{2,3},{3,2},{4,5},{5,4},{6,7},{7,6},{8,9},{9,8},{10,11... | collective-permute-start | bytes 1228808 | tf_op jit(solution)/shard_map/ppermute | solution.py:25
  102.7 35.7 %copy-start.4 = (bf16[64,192]{1,0:T(8,128)(2,1)S(1)}, bf16[64,192]{1,0:T(8,128)(2,1)}, u32[]{:S(2)}) copy-start(bf16[64,192]{1,0:T(8,128)(2,1)} %get-tuple-element.15) | copy-start | bytes 73732

commit v5 on v4

--- a/solution.py
+++ b/solution.py
@@ -42,7 +42,7 @@
     started = []
     for k, out in enumerate(outs):
         for h in range(NC):
-            start = pl.multiple_of(start_of[k * NC + h], feat)
+            start = pl.multiple_of(start_of(k, h, feat), feat)
             rows = pl.ds(h * feat, feat)
             copies = [
                 (gate_ref.at[pl.ds(start, feat), :], out.at[rows, pl.ds(0, hid)]),
@@ -68,7 +68,7 @@
 
 
 def pack_kernel(where_ref, gate_ref, up_ref, down_ref, *refs):
-    for copy in start_packing(where_ref, gate_ref, up_ref, down_ref, refs[:-1], refs[-1]):
+    for copy in start_packing(lambda k, h, feat: where_ref[k * NC + h], gate_ref, up_ref, down_ref, refs[:-1], refs[-1]):
         copy.wait()
 
 
@@ -87,12 +87,14 @@
 
 
 def pick_kernel(
-    base_ref, chosen_ref, tokens_ref, grads_ref, gate_ref, up_ref, down_ref, rows_ref, pick_ref, out_ref, sems
+    chosen_ref, tokens_ref, grads_ref, gate_ref, up_ref, down_ref, rows_ref, pick_ref, out_ref, sems
 ):
-    started = start_packing(base_ref, gate_ref, up_ref, down_ref, [out_ref], sems)
+    c_index = lax.axis_index("c")
+    dest = lax.rem(lax.axis_index("x") + 2, NX)
+    started = start_packing(lambda k, h, feat: (dest * NC + (1 - c_index if h else c_index)) * feat, gate_ref, up_ref, down_ref, [out_ref], sems)
     token_rows, feat = tokens_ref.shape
     experts, capacity = chosen_ref.shape
-    local = chosen_ref[...] - base_ref[NC]
+    local = chosen_ref[...] - (lax.axis_index("y") * NZ + lax.axis_index("z")) * token_rows
     mine = (local >= 0) & (local < token_rows)
     earlier = lax.broadcasted_iota(jnp.int32, (capacity, capacity), 0) < lax.broadcasted_iota(
         jnp.int32, (capacity, capacity), 1
@@ -118,7 +120,7 @@
         copy.wait()
 
 
-def pick_rows(base, chosen, tokens, grads, gate, up, down):
+def pick_rows(chosen, tokens, grads, gate, up, down):
     hid = gate.shape[1]
     hbm = pl.BlockSpec(memory_space=pltpu.HBM)
     token_rows, feat = tokens.shape
@@ -131,11 +133,11 @@
             jax.ShapeDtypeStruct((picks, token_rows), BF),
             packed_shape(hid, feat),
         ),
-        in_specs=[pl.BlockSpec(memory_space=pltpu.SMEM), vmem, vmem, vmem, hbm, hbm, hbm],
+        in_specs=[vmem, vmem, vmem, hbm, hbm, hbm],
         scratch_shapes=[pack_copies(hid, feat, 1)],
         compiler_params=pltpu.CompilerParams(vmem_limit_bytes=BIG_VMEM),
         name="pick_rows",
-    )(base, chosen, tokens, grads, gate, up, down)
+    )(chosen, tokens, grads, gate, up, down)
 
 
 def pre_kernel(own_ref, other_ref, w_ref, out_ref):
@@ -170,37 +172,49 @@
     )(own, other, w)
 
 
-def give_kernel(from_ref, d_ref, w0, w1, w2, w3, extra_ref, give_ref, keep_ref):
+def half_term(h, from_ref, d_ref, weights, rows, feat):
+    total = None
+    for k, w in enumerate(weights):
+        term = lax.dot_general(
+            d_ref[from_ref[k], :rows, :],
+            w[h * feat : (h + 1) * feat, :],
+            CONTRACT,
+            preferred_element_type=F32,
+        )
+        total = term if total is None else total + term
+    return total
+
+
+def give_kernel(from_ref, d_ref, w0, w1, w2, w3, extra_ref, give_ref):
+    rows = give_ref.shape[0] - extra_ref.shape[0]
+    total = half_term(1, from_ref, d_ref, (w0, w1, w2, w3), rows, give_ref.shape[1])
+    give_ref[:rows, :] = total.astype(BF)
+    give_ref[rows:, :] = extra_ref[...]
+
+
+def keep_kernel(from_ref, d_ref, w0, w1, w2, w3, keep_ref):
     rows, feat = keep_ref.shape
-    for h in (1, 0):
-        total = None
-        for k, w in enumerate((w0, w1, w2, w3)):
-            term = lax.dot_general(
-                d_ref[from_ref[k], :rows, :],
-                w[h * feat : (h + 1) * feat, :],
-                CONTRACT,
-                preferred_element_type=F32,
-            )
-            total = term if total is None else total + term
-        if h:
-            give_ref[:rows, :] = total.astype(BF)
-            give_ref[rows:, :] = extra_ref[...]
-        else:
-            keep_ref[...] = total
+    keep_ref[...] = half_term(0, from_ref, d_ref, (w0, w1, w2, w3), rows, feat)
 
 
 def give_keep(origin, deltas, weights, extra, rows, feat):
     vmem = pl.BlockSpec(memory_space=pltpu.VMEM)
-    return pl.pallas_call(
+    smem = pl.BlockSpec(memory_space=pltpu.SMEM)
+    give = pl.pallas_call(
         give_kernel,
-        out_shape=(
-            jax.ShapeDtypeStruct((rows + extra.shape[0], feat), BF),
-            jax.ShapeDtypeStruct((rows, feat), F32),
-        ),
-        in_specs=[pl.BlockSpec(memory_space=pltpu.SMEM)] + [vmem] * 6,
+        out_shape=jax.ShapeDtypeStruct((rows + extra.shape[0], feat), BF),
+        in_specs=[smem] + [vmem] * 6,
         compiler_params=pltpu.CompilerParams(vmem_limit_bytes=VMEM),
-        name="input_grads",
+        name="input_grads_give",
     )(origin, deltas, *weights, extra)
+    keep = pl.pallas_call(
+        keep_kernel,
+        out_shape=jax.ShapeDtypeStruct((rows, feat), F32),
+        in_specs=[smem] + [vmem] * 5,
+        compiler_params=pltpu.CompilerParams(vmem_limit_bytes=VMEM),
+        name="input_grads_keep",
+    )(origin, deltas, *weights)
+    return give, keep
 
 
 def spread_kernel(keep_ref, came_ref, place_ref, gate_ref, out_ref):
@@ -241,9 +255,7 @@
         dest = (x_index + k) % NX * wide
         return [dest + c_index * feat, dest + (1 - c_index) * feat]
 
-    outgoing, pick, out_2 = pick_rows(
-        jnp.stack(starts(2) + [exp_index * token_rows]), chosen, tokens, output_grad, *own_weights
-    )
+    outgoing, pick, out_2 = pick_rows(chosen, tokens, output_grad, *own_weights)
     got = lax.all_to_all(outgoing, ("y", "z"), split_axis=0, concat_axis=0, tiled=True)
     weights = {2: shift_x(out_2, 2)}
     out_1, out_3, weights[0] = pack_weights(

time: 140 us -> 139 us (level)
  transfers between devices with their start and end apart: 9 -> 9, of which waited for: 6 -> 6; matrix products, arithmetic and copies ran while one was open for 3% -> 3% of each run, Pallas kernels for 4% -> 5%
where the time goes in v5:
time: 139 us; the launch traced here: 138 us
  blocking collectives  50.3 us (36%)
  starting transfers between devices  40.5 us (29%)
  waiting for transfers between devices  27.1 us (19%)
  Pallas kernels  12.5 us (9%)
  matrix products  2.82 us (2%)
  other arithmetic  2.27 us (2%)
  local copies, waits for them, and re-layouts  1.96 us (1%)
    all_to_all x1, blocking collectives, on_device(): lax.all_to_all(spread_out(keep, came, place_t, gate_block), ('y', 'z'), s...  35 us
    ppermute x6, waiting for transfers between devices, shift_x(): return lax.ppermute(a, 'x', [(j, (j + k) % NX) for j in range(NX)])  20.2 us
    ppermute x6, starting transfers between devices, shift_x(): return lax.ppermute(a, 'x', [(j, (j + k) % NX) for j in range(NX)])  19.8 us
    all_to_all x1, starting transfers between devices, on_device(): lax.all_to_all(outgoing, ('y', 'z'), split_axis=0, concat_axis=0, tiled=T...  16.8 us
    all_gather x1, blocking collectives, on_device(): deltas = lax.all_gather(delta, 'x', axis=0, tiled=False)  15.3 us
    all_to_all x1, waiting for transfers between devices, on_device(): lax.all_to_all(outgoing, ('y', 'z'), split_axis=0, concat_axis=0, tiled=T...  6.48 us
    pallas_call x1, Pallas kernels, pack_weights(): pl.pallas_call(pack_kernel, out_shape=(packed_shape(hid, feat),) * count,...  3.9 us
    ppermute x2, starting transfers between devices, swap_cores(): return lax.ppermute(a, 'c', [(0, 1), (1, 0)])  3.84 us
  transfers between devices with their start and end apart: 9, of which 6 were waited for; matrix products, arithmetic and copies ran while one was open for 3% of the time, Pallas kernels for 5%

profile of v5, /device:TPU:18, one launch (start us, length us, event | category | flops | bytes accessed | tf_op | source)
XLA Modules:
  0.0 138.4 jit_solution(14203171741828078921)
XLA Ops:
  0.6 0.0 copy-start
  0.6 3.6 %pick_rows.1 = (bf16[512,1024]{1,0:T(8,128)(2,1)}, bf16[64,192]{1,0:T(8,128)(2,1)}, bf16[1536,256]{1,0:T(8,128)(2,1)}) custom-call(s32[8,384]{1,0:T(8,128)} %chosen_ref.1, bf16[192,512]{1,0:T(8,128)(2,1)} %tokens_ref.1, bf16[192,512]{1,0:T(8,128)(2,1)} %grads_ref.1, bf16[4096,128]{1,0:T(8,128)(2,1)} %bitcast.33, bf16[4096,128]{1,0:T(8,128)(2,1)} %bitcast.35, ...), custom_call_target="tpu_custom_call" | custom-call | tf_op jit(solution)/shard_map/pick_rows/pallas_call | solution.py:129
  4.2 0.0 copy-start.5
  4.2 16.8 %all-to-all-start = ((bf16[64,8,1024]{2,1,0:T(8,128)(2,1)}), bf16[64,8,1024]{2,1,0:T(8,128)(2,1)}, u32[]{:S(2)}, u32[]{:S(2)}) async-start(bf16[64,8,1024]{2,1,0:T(8,128)(2,1)} %bitcast.39), calls=%async_computation | async-start | bytes 2097152 | tf_op jit(solution)/shard_map/all_to_all | solution.py:259
  21.0 0.0 copy-done.5
  21.1 4.0 %collective-permute-start = (bf16[1536,256]{1,0:T(8,128)(2,1)S(1)}, bf16[1536,256]{1,0:T(8,128)(2,1)S(1)}, u32[]{:S(2)}, u32[]{:S(2)}) collective-permute-start(bf16[1536,256]{1,0:T(8,128)(2,1)S(1)} %copy-done.5), channel_id=1, source_target_pairs={{0,4},{2,6},{4,0},{6,2},{1,5},{3,7},{5,1},{7,3},{8,12},{10,14},{12... | collective-permute-start | bytes 2359304 | tf_op jit(solution)/shard_map/ppermute | solution.py:29
  25.1 0.6 stack.27.where_ref
  25.7 3.9 %pack_weights.1 = (bf16[1536,256]{1,0:T(8,128)(2,1)}, bf16[1536,256]{1,0:T(8,128)(2,1)}, bf16[1536,256]{1,0:T(8,128)(2,1)}) custom-call(s32[6]{0:T(128)} %stack.27.where_ref, bf16[4096,128]{1,0:T(8,128)(2,1)} %bitcast.34, bf16[4096,128]{1,0:T(8,128)(2,1)} %bitcast.36, bf16[128,4096]{1,0:T(8,128)(2,1)} %bitcast.38), custom_call_target="tpu_custom_call" | custom-call | tf_op jit(solution)/shard_map/pack_weights/pallas_call | solution.py:79
  29.7 1.9 %collective-permute-start.2 = (bf16[1536,256]{1,0:T(8,128)(2,1)}, bf16[1536,256]{1,0:T(8,128)(2,1)S(1)}, u32[]{:S(2)}, u32[]{:S(2)}) collective-permute-start(bf16[1536,256]{1,0:T(8,128)(2,1)} %get-tuple-element.17), channel_id=1, source_target_pairs={{0,2},{2,4},{4,6},{6,0},{1,3},{3,5},{5,7},{7,1},{8,10},{10,12},{12... | collective-permute-start | bytes 2359304 | tf_op jit(solution)/shard_map/ppermute | solution.py:29
  31.6 3.9 %collective-permute-start.3 = (bf16[1536,256]{1,0:T(8,128)(2,1)}, bf16[1536,256]{1,0:T(8,128)(2,1)S(1)}, u32[]{:S(2)}, u32[]{:S(2)}) collective-permute-start(bf16[1536,256]{1,0:T(8,128)(2,1)} %get-tuple-element.18), channel_id=1, source_target_pairs={{0,6},{2,0},{4,2},{6,4},{1,7},{3,1},{5,3},{7,5},{8,14},{10,8},{12,... | collective-permute-start | bytes 2359304 | tf_op jit(solution)/shard_map/ppermute | solution.py:29
  35.5 0.7 fusion.12
  36.3 0.2 convert_reduce_fusion
  36.5 8.5 %collective-permute-done.w_ref.w2 = bf16[1536,256]{1,0:T(8,128)(2,1)S(1)} collective-permute-done((bf16[1536,256]{1,0:T(8,128)(2,1)S(1)}, bf16[1536,256]{1,0:T(8,128)(2,1)S(1)}, u32[]{:S(2)}, u32[]{:S(2)}) %collective-permute-start) | collective-permute-done | bytes 786464 | tf_op jit(solution)/shard_map/ppermute | solution.py:29
  45.0 6.5 %all-to-all-done = bf16[64,8,1024]{2,1,0:T(8,128)(2,1)} async-done(((bf16[64,8,1024]{2,1,0:T(8,128)(2,1)}), bf16[64,8,1024]{2,1,0:T(8,128)(2,1)}, u32[]{:S(2)}, u32[]{:S(2)}) %all-to-all-start) | async-done | bytes 1048608 | tf_op jit(solution)/shard_map/all_to_all | solution.py:259
  51.5 1.8 %convolution_convert_fusion.own_ref = bf16[384,1024]{1,0:T(8,128)(2,1)S(1)} fusion(bf16[512,1024]{1,0:T(8,128)(2,1)} %bitcast.6, s32[384]{0:T(512)S(1)} %multiply_add_fusion), kind=kOutput, calls=%fused_computation | convolution fusion | flops 403243008 | bytes 1836544 | tf_op jit(solution)/shard_map/dot_general | solution.py:278
  53.3 1.9 %collective-permute-start.1 = (bf16[384,1024]{1,0:T(8,128)(2,1)S(1)}, bf16[384,1024]{1,0:T(8,128)(2,1)S(1)}, u32[]{:S(2)}, u32[]{:S(2)}) collective-permute-start(bf16[384,1024]{1,0:T(8,128)(2,1)S(1)} %convolution_convert_fusion.own_ref), channel_id=1, source_target_pairs={{0,1},{1,0},{2,3},{3,2},{4,5},{5,4},{6,7},{7,6},{8,9},{9,8},{10,11... | collective-permute-start | bytes 2359304 | tf_op jit(solution)/shard_map/ppermute | solution.py:25
  55.2 4.9 %collective-permute-done.2.w_ref.w1 = bf16[1536,256]{1,0:T(8,128)(2,1)S(1)} collective-permute-done((bf16[1536,256]{1,0:T(8,128)(2,1)}, bf16[1536,256]{1,0:T(8,128)(2,1)S(1)}, u32[]{:S(2)}, u32[]{:S(2)}) %collective-permute-start.2) | collective-permute-done | bytes 786464 | tf_op jit(solution)/shard_map/ppermute | solution.py:29
  60.1 0.0 collective-permute-done.3.w_ref.w3
  60.1 0.0 copy-start.2
  60.1 0.0 collective-permute-done.1.other_ref
  60.1 0.6 pre_part.4
  60.7 4.0 %collective-permute-start.4 = (bf16[384,384]{1,0:T(8,128)(2,1)S(1)}, bf16[384,384]{1,0:T(8,128)(2,1)S(1)}, u32[]{:S(2)}, u32[]{:S(2)}) collective-permute-start(bf16[384,384]{1,0:T(8,128)(2,1)S(1)} %pre_part.4), channel_id=1, source_target_pairs={{0,4},{2,6},{4,0},{6,2},{1,5},{3,7},{5,1},{7,3},{8,12},{10,14},{12... | collective-permute-start | bytes 884744 | tf_op jit(solution)/shard_map/ppermute | solution.py:29
  64.6 0.0 copy-done.2
  64.7 0.6 pre_part.5
  65.2 0.0 copy-start.1
  65.3 2.1 %collective-permute-start.5 = (bf16[384,384]{1,0:T(8,128)(2,1)S(1)}, bf16[384,384]{1,0:T(8,128)(2,1)S(1)}, u32[]{:S(2)}, u32[]{:S(2)}) collective-permute-start(bf16[384,384]{1,0:T(8,128)(2,1)S(1)} %pre_part.5), channel_id=1, source_target_pairs={{0,2},{2,4},{4,6},{6,0},{1,3},{3,5},{5,7},{7,1},{8,10},{10,12},{12... | collective-permute-start | bytes 884744 | tf_op jit(solution)/shard_map/ppermute | solution.py:29
  67.3 0.6 pre_part.6
  67.9 3.9 %collective-permute-start.6 = (bf16[384,384]{1,0:T(8,128)(2,1)S(1)}, bf16[384,384]{1,0:T(8,128)(2,1)S(1)}, u32[]{:S(2)}, u32[]{:S(2)}) collective-permute-start(bf16[384,384]{1,0:T(8,128)(2,1)S(1)} %pre_part.6), channel_id=1, source_target_pairs={{0,6},{2,0},{4,2},{6,4},{1,7},{3,1},{5,3},{7,5},{8,14},{10,8},{12,... | collective-permute-start | bytes 884744 | tf_op jit(solution)/shard_map/ppermute | solution.py:29
  71.8 0.0 copy-done
  71.9 0.0 copy-done.1
  71.9 0.6 pre_part.7
  72.5 0.6 collective-permute-done.4
  73.0 6.3 %collective-permute-done.5 = bf16[384,384]{1,0:T(8,128)(2,1)S(1)} collective-permute-done((bf16[384,384]{1,0:T(8,128)(2,1)S(1)}, bf16[384,384]{1,0:T(8,128)(2,1)S(1)}, u32[]{:S(2)}, u32[]{:S(2)}) %collective-permute-start.5) | collective-permute-done | bytes 294944 | tf_op jit(solution)/shard_map/ppermute | solution.py:29
  79.3 0.0 collective-permute-done.6
  79.3 0.1 convert_add_fusion
  79.5 0.2 multiply_convert_fusion.1
  79.8 15.3 %all-gather = bf16[1600,256]{1,0:T(8,128)(2,1)S(1)} all-gather(bf16[400,256]{1,0:T(8,128)(2,1)S(1)} %pad_maximum_fusion), channel_id=2, replica_groups=mesh['y'=8,'z'=8,'x'=4,'c'=2] {'x'}, dimensions={0}, use_global_device_ids=true | all-gather | bytes 1024000 | tf_op jit(solution)/shard_map/all_gather | solution.py:295
  95.2 0.0 copy-start.3
  95.2 1.1 copy-done.3
  96.4 1.1 input_grads_give.1
  97.5 1.9 %collective-permute-start.7 = (bf16[400,512]{1,0:T(8,128)(2,1)S(1)}, bf16[400,512]{1,0:T(8,128)(2,1)S(1)}, u32[]{:S(2)}, u32[]{:S(2)}) collective-permute-start(bf16[400,512]{1,0:T(8,128)(2,1)S(1)} %input_grads_give.1), channel_id=1, source_target_pairs={{0,1},{1,0},{2,3},{3,2},{4,5},{5,4},{6,7},{7,6},{8,9},{9,8},{10,11... | collective-permute-start | bytes 1228808 | tf_op jit(solution)/shard_map/ppermute | solution.py:25
  99.5 0.1 fusion.place_ref
  99.6 1.1 input_grads_keep.1.keep_ref
  100.7 0.4 collective-permute-done.7.came_ref
  101.2 0.5 rows_to_slots.1
  101.7 0.0 copy-start.4
  101.7 35.0 %all_to_all.24 = bf16[64,8,640]{2,1,0:T(8,128)(2,1)S(1)} all-to-all(bf16[64,8,640]{2,1,0:T(8,128)(2,1)S(1)} %bitcast.32), channel_id=1, replica_groups=mesh['y'=8,'z'=8,'x'=4,'c'=2] {'y','z'}, dimensions={0} | all-to-all | bytes 1310720 | tf_op jit(solution)/shard_map/all_to_all | solution.py:310
  136.7 0.1 reduce_sum.42
  136.8 0.6 slice_add_fusion
  137.4 0.0 copy-done.4
  137.4 1.0 convolution_convert_fusion.1
  (24 shorter events, 0.4 us)
Async XLA Ops:
  0.6 71.2 %copy-start = (f32[8,384]{1,0:T(8,128)S(1)}, f32[8,384]{1,0:T(8,128)}, u32[]{:S(2)}) copy-start(f32[8,384]{1,0:T(8,128)} %param.13) | copy-start | bytes 36868
  4.2 16.8 %copy-start.5 = (bf16[1536,256]{1,0:T(8,128)(2,1)S(1)}, bf16[1536,256]{1,0:T(8,128)(2,1)}, u32[]{:S(2)}) copy-start(bf16[1536,256]{1,0:T(8,128)(2,1)} %get-tuple-element.15) | copy-start | bytes 2359300
  4.2 47.2 %all-to-all-start = ((bf16[64,8,1024]{2,1,0:T(8,128)(2,1)}), bf16[64,8,1024]{2,1,0:T(8,128)(2,1)}, u32[]{:S(2)}, u32[]{:S(2)}) async-start(bf16[64,8,1024]{2,1,0:T(8,128)(2,1)} %bitcast.39), calls=%async_computation | async-start | bytes 2097152 | tf_op jit(solution)/shard_map/all_to_all | solution.py:259
  21.1 23.9 %collective-permute-start = (bf16[1536,256]{1,0:T(8,128)(2,1)S(1)}, bf16[1536,256]{1,0:T(8,128)(2,1)S(1)}, u32[]{:S(2)}, u32[]{:S(2)}) collective-permute-start(bf16[1536,256]{1,0:T(8,128)(2,1)S(1)} %copy-done.5), channel_id=1, source_target_pairs={{0,4},{2,6},{4,0},{6,2},{1,5},{3,7},{5,1},{7,3},{8,12},{10,14},{12... | collective-permute-start | bytes 2359304 | tf_op jit(solution)/shard_map/ppermute | solution.py:29
  29.7 30.4 %collective-permute-start.2 = (bf16[1536,256]{1,0:T(8,128)(2,1)}, bf16[1536,256]{1,0:T(8,128)(2,1)S(1)}, u32[]{:S(2)}, u32[]{:S(2)}) collective-permute-start(bf16[1536,256]{1,0:T(8,128)(2,1)} %get-tuple-element.17), channel_id=1, source_target_pairs={{0,2},{2,4},{4,6},{6,0},{1,3},{3,5},{5,7},{7,1},{8,10},{10,12},{12... | collective-permute-start | bytes 2359304 | tf_op jit(solution)/shard_map/ppermute | solution.py:29
  31.6 28.5 %collective-permute-start.3 = (bf16[1536,256]{1,0:T(8,128)(2,1)}, bf16[1536,256]{1,0:T(8,128)(2,1)S(1)}, u32[]{:S(2)}, u32[]{:S(2)}) collective-permute-start(bf16[1536,256]{1,0:T(8,128)(2,1)} %get-tuple-element.18), channel_id=1, source_target_pairs={{0,6},{2,0},{4,2},{6,4},{1,7},{3,1},{5,3},{7,5},{8,14},{10,8},{12,... | collective-permute-start | bytes 2359304 | tf_op jit(solution)/shard_map/ppermute | solution.py:29
  53.3 6.8 %collective-permute-start.1 = (bf16[384,1024]{1,0:T(8,128)(2,1)S(1)}, bf16[384,1024]{1,0:T(8,128)(2,1)S(1)}, u32[]{:S(2)}, u32[]{:S(2)}) collective-permute-start(bf16[384,1024]{1,0:T(8,128)(2,1)S(1)} %convolution_convert_fusion.own_ref), channel_id=1, source_target_pairs={{0,1},{1,0},{2,3},{3,2},{4,5},{5,4},{6,7},{7,6},{8,9},{9,8},{10,11... | collective-permute-start | bytes 2359304 | tf_op jit(solution)/shard_map/ppermute | solution.py:25
  60.1 4.6 %copy-start.2 = (bf16[1536,256]{1,0:T(8,128)(2,1)}, bf16[1536,256]{1,0:T(8,128)(2,1)S(1)}, u32[]{:S(2)}) copy-start(bf16[1536,256]{1,0:T(8,128)(2,1)S(1)} %collective-permute-done.3.w_ref.w3) | copy-start | bytes 2359300
  60.7 12.3 %collective-permute-start.4 = (bf16[384,384]{1,0:T(8,128)(2,1)S(1)}, bf16[384,384]{1,0:T(8,128)(2,1)S(1)}, u32[]{:S(2)}, u32[]{:S(2)}) collective-permute-start(bf16[384,384]{1,0:T(8,128)(2,1)S(1)} %pre_part.4), channel_id=1, source_target_pairs={{0,4},{2,6},{4,0},{6,2},{1,5},{3,7},{5,1},{7,3},{8,12},{10,14},{12... | collective-permute-start | bytes 884744 | tf_op jit(solution)/shard_map/ppermute | solution.py:29
  65.2 6.6 %copy-start.1 = (bf16[1536,256]{1,0:T(8,128)(2,1)S(1)}, bf16[1536,256]{1,0:T(8,128)(2,1)}, u32[]{:S(2)}) copy-start(bf16[1536,256]{1,0:T(8,128)(2,1)} %get-tuple-element.23.w_ref.w0) | copy-start | bytes 2359300
  65.3 14.1 %collective-permute-start.5 = (bf16[384,384]{1,0:T(8,128)(2,1)S(1)}, bf16[384,384]{1,0:T(8,128)(2,1)S(1)}, u32[]{:S(2)}, u32[]{:S(2)}) collective-permute-start(bf16[384,384]{1,0:T(8,128)(2,1)S(1)} %pre_part.5), channel_id=1, source_target_pairs={{0,2},{2,4},{4,6},{6,0},{1,3},{3,5},{5,7},{7,1},{8,10},{10,12},{12... | collective-permute-start | bytes 884744 | tf_op jit(solution)/shard_map/ppermute | solution.py:29
  67.9 11.4 %collective-permute-start.6 = (bf16[384,384]{1,0:T(8,128)(2,1)S(1)}, bf16[384,384]{1,0:T(8,128)(2,1)S(1)}, u32[]{:S(2)}, u32[]{:S(2)}) collective-permute-start(bf16[384,384]{1,0:T(8,128)(2,1)S(1)} %pre_part.6), channel_id=1, source_target_pairs={{0,6},{2,0},{4,2},{6,4},{1,7},{3,1},{5,3},{7,5},{8,14},{10,8},{12,... | collective-permute-start | bytes 884744 | tf_op jit(solution)/shard_map/ppermute | solution.py:29
  95.2 1.1 copy-start.3
  97.5 3.6 %collective-permute-start.7 = (bf16[400,512]{1,0:T(8,128)(2,1)S(1)}, bf16[400,512]{1,0:T(8,128)(2,1)S(1)}, u32[]{:S(2)}, u32[]{:S(2)}) collective-permute-start(bf16[400,512]{1,0:T(8,128)(2,1)S(1)} %input_grads_give.1), channel_id=1, source_target_pairs={{0,1},{1,0},{2,3},{3,2},{4,5},{5,4},{6,7},{7,6},{8,9},{9,8},{10,11... | collective-permute-start | bytes 1228808 | tf_op jit(solution)/shard_map/ppermute | solution.py:25
  101.7 35.8 %copy-start.4 = (bf16[64,192]{1,0:T(8,128)(2,1)S(1)}, bf16[64,192]{1,0:T(8,128)(2,1)}, u32[]{:S(2)}) copy-start(bf16[64,192]{1,0:T(8,128)(2,1)} %get-tuple-element.13) | copy-start | bytes 73732

commit v6 on v5

--- a/solution.py
+++ b/solution.py
@@ -11,7 +11,7 @@
 SLOTS = 8
 BF = jnp.bfloat16
 F32 = jnp.float32
-VMEM = 12 * 1024 * 1024
+VMEM = 6 * 1024 * 1024
 BIG_VMEM = 60 * 1024 * 1024
 CONTRACT = (((1,), (1,)), ((), ()))
 

time: 139 us -> 139 us (level)
  no operation moved by 1% of the time
where the time goes in v6:
time: 139 us; the launch traced here: 138 us
  blocking collectives  50.3 us (36%)
  starting transfers between devices  40.5 us (29%)
  waiting for transfers between devices  27.1 us (19%)
  Pallas kernels  12.5 us (9%)
  matrix products  2.81 us (2%)
  other arithmetic  2.27 us (2%)
  local copies, waits for them, and re-layouts  1.98 us (1%)
    all_to_all x1, blocking collectives, on_device(): lax.all_to_all(spread_out(keep, came, place_t, gate_block), ('y', 'z'), s...  35 us
    ppermute x6, waiting for transfers between devices, shift_x(): return lax.ppermute(a, 'x', [(j, (j + k) % NX) for j in range(NX)])  20.2 us
    ppermute x6, starting transfers between devices, shift_x(): return lax.ppermute(a, 'x', [(j, (j + k) % NX) for j in range(NX)])  19.8 us
    all_to_all x1, starting transfers between devices, on_device(): lax.all_to_all(outgoing, ('y', 'z'), split_axis=0, concat_axis=0, tiled=T...  16.8 us
    all_gather x1, blocking collectives, on_device(): deltas = lax.all_gather(delta, 'x', axis=0, tiled=False)  15.3 us
    all_to_all x1, waiting for transfers between devices, on_device(): lax.all_to_all(outgoing, ('y', 'z'), split_axis=0, concat_axis=0, tiled=T...  6.48 us
    pallas_call x1, Pallas kernels, pack_weights(): pl.pallas_call(pack_kernel, out_shape=(packed_shape(hid, feat),) * count,...  3.91 us
    ppermute x2, starting transfers between devices, swap_cores(): return lax.ppermute(a, 'c', [(0, 1), (1, 0)])  3.84 us
  transfers between devices with their start and end apart: 9, of which 6 were waited for; matrix products, arithmetic and copies ran while one was open for 3% of the time, Pallas kernels for 5%

profile of v6, /device:TPU:18, one launch (start us, length us, event | category | flops | bytes accessed | tf_op | source)
XLA Modules:
  0.0 138.4 jit_solution(238950140093188982)
XLA Ops:
  0.6 0.0 copy-start
  0.6 3.6 %pick_rows.1 = (bf16[512,1024]{1,0:T(8,128)(2,1)}, bf16[64,192]{1,0:T(8,128)(2,1)}, bf16[1536,256]{1,0:T(8,128)(2,1)}) custom-call(s32[8,384]{1,0:T(8,128)} %chosen_ref.1, bf16[192,512]{1,0:T(8,128)(2,1)} %tokens_ref.1, bf16[192,512]{1,0:T(8,128)(2,1)} %grads_ref.1, bf16[4096,128]{1,0:T(8,128)(2,1)} %bitcast.33, bf16[4096,128]{1,0:T(8,128)(2,1)} %bitcast.35, ...), custom_call_target="tpu_custom_call" | custom-call | tf_op jit(solution)/shard_map/pick_rows/pallas_call | solution.py:129
  4.2 0.0 copy-start.6
  4.2 16.8 %all-to-all-start = ((bf16[64,8,1024]{2,1,0:T(8,128)(2,1)}), bf16[64,8,1024]{2,1,0:T(8,128)(2,1)}, u32[]{:S(2)}, u32[]{:S(2)}) async-start(bf16[64,8,1024]{2,1,0:T(8,128)(2,1)} %bitcast.39), calls=%async_computation | async-start | bytes 2097152 | tf_op jit(solution)/shard_map/all_to_all | solution.py:259
  21.0 0.0 copy-done.6
  21.0 4.0 %collective-permute-start = (bf16[1536,256]{1,0:T(8,128)(2,1)S(1)}, bf16[1536,256]{1,0:T(8,128)(2,1)S(1)}, u32[]{:S(2)}, u32[]{:S(2)}) collective-permute-start(bf16[1536,256]{1,0:T(8,128)(2,1)S(1)} %copy-done.6), channel_id=1, source_target_pairs={{0,4},{2,6},{4,0},{6,2},{1,5},{3,7},{5,1},{7,3},{8,12},{10,14},{12... | collective-permute-start | bytes 2359304 | tf_op jit(solution)/shard_map/ppermute | solution.py:29
  25.1 0.6 stack.27.where_ref
  25.8 3.9 %pack_weights.1 = (bf16[1536,256]{1,0:T(8,128)(2,1)}, bf16[1536,256]{1,0:T(8,128)(2,1)}, bf16[1536,256]{1,0:T(8,128)(2,1)}) custom-call(s32[6]{0:T(128)} %stack.27.where_ref, bf16[4096,128]{1,0:T(8,128)(2,1)} %bitcast.34, bf16[4096,128]{1,0:T(8,128)(2,1)} %bitcast.36, bf16[128,4096]{1,0:T(8,128)(2,1)} %bitcast.38), custom_call_target="tpu_custom_call" | custom-call | tf_op jit(solution)/shard_map/pack_weights/pallas_call | solution.py:79
  29.7 1.9 %collective-permute-start.2 = (bf16[1536,256]{1,0:T(8,128)(2,1)}, bf16[1536,256]{1,0:T(8,128)(2,1)S(1)}, u32[]{:S(2)}, u32[]{:S(2)}) collective-permute-start(bf16[1536,256]{1,0:T(8,128)(2,1)} %get-tuple-element.17), channel_id=1, source_target_pairs={{0,2},{2,4},{4,6},{6,0},{1,3},{3,5},{5,7},{7,1},{8,10},{10,12},{12... | collective-permute-start | bytes 2359304 | tf_op jit(solution)/shard_map/ppermute | solution.py:29
  31.6 3.9 %collective-permute-start.3 = (bf16[1536,256]{1,0:T(8,128)(2,1)}, bf16[1536,256]{1,0:T(8,128)(2,1)S(1)}, u32[]{:S(2)}, u32[]{:S(2)}) collective-permute-start(bf16[1536,256]{1,0:T(8,128)(2,1)} %get-tuple-element.18), channel_id=1, source_target_pairs={{0,6},{2,0},{4,2},{6,4},{1,7},{3,1},{5,3},{7,5},{8,14},{10,8},{12,... | collective-permute-start | bytes 2359304 | tf_op jit(solution)/shard_map/ppermute | solution.py:29
  35.5 0.7 fusion.12
  36.3 0.2 convert_reduce_fusion
  36.5 8.5 %collective-permute-done.w_ref.w2 = bf16[1536,256]{1,0:T(8,128)(2,1)S(1)} collective-permute-done((bf16[1536,256]{1,0:T(8,128)(2,1)S(1)}, bf16[1536,256]{1,0:T(8,128)(2,1)S(1)}, u32[]{:S(2)}, u32[]{:S(2)}) %collective-permute-start) | collective-permute-done | bytes 786464 | tf_op jit(solution)/shard_map/ppermute | solution.py:29
  45.0 6.5 %all-to-all-done = bf16[64,8,1024]{2,1,0:T(8,128)(2,1)} async-done(((bf16[64,8,1024]{2,1,0:T(8,128)(2,1)}), bf16[64,8,1024]{2,1,0:T(8,128)(2,1)}, u32[]{:S(2)}, u32[]{:S(2)}) %all-to-all-start) | async-done | bytes 1048608 | tf_op jit(solution)/shard_map/all_to_all | solution.py:259
  51.4 1.8 %convolution_convert_fusion.own_ref = bf16[384,1024]{1,0:T(8,128)(2,1)S(1)} fusion(bf16[512,1024]{1,0:T(8,128)(2,1)} %bitcast.6, s32[384]{0:T(512)S(1)} %multiply_add_fusion), kind=kOutput, calls=%fused_computation | convolution fusion | flops 403243008 | bytes 1836544 | tf_op jit(solution)/shard_map/dot_general | solution.py:278
  53.3 1.9 %collective-permute-start.1 = (bf16[384,1024]{1,0:T(8,128)(2,1)S(1)}, bf16[384,1024]{1,0:T(8,128)(2,1)S(1)}, u32[]{:S(2)}, u32[]{:S(2)}) collective-permute-start(bf16[384,1024]{1,0:T(8,128)(2,1)S(1)} %convolution_convert_fusion.own_ref), channel_id=1, source_target_pairs={{0,1},{1,0},{2,3},{3,2},{4,5},{5,4},{6,7},{7,6},{8,9},{9,8},{10,11... | collective-permute-start | bytes 2359304 | tf_op jit(solution)/shard_map/ppermute | solution.py:25
  55.2 4.9 %collective-permute-done.2.w_ref.w1 = bf16[1536,256]{1,0:T(8,128)(2,1)S(1)} collective-permute-done((bf16[1536,256]{1,0:T(8,128)(2,1)}, bf16[1536,256]{1,0:T(8,128)(2,1)S(1)}, u32[]{:S(2)}, u32[]{:S(2)}) %collective-permute-start.2) | collective-permute-done | bytes 786464 | tf_op jit(solution)/shard_map/ppermute | solution.py:29
  60.1 0.0 collective-permute-done.3.w_ref.w3
  60.1 0.0 copy-start.2
  60.1 0.0 collective-permute-done.1.other_ref
  60.1 0.6 pre_part.4
  60.7 4.0 %collective-permute-start.4 = (bf16[384,384]{1,0:T(8,128)(2,1)S(1)}, bf16[384,384]{1,0:T(8,128)(2,1)S(1)}, u32[]{:S(2)}, u32[]{:S(2)}) collective-permute-start(bf16[384,384]{1,0:T(8,128)(2,1)S(1)} %pre_part.4), channel_id=1, source_target_pairs={{0,4},{2,6},{4,0},{6,2},{1,5},{3,7},{5,1},{7,3},{8,12},{10,14},{12... | collective-permute-start | bytes 884744 | tf_op jit(solution)/shard_map/ppermute | solution.py:29
  64.7 0.0 copy-done.2
  64.7 0.6 pre_part.5
  65.3 0.0 copy-start.1
  65.3 2.1 %collective-permute-start.5 = (bf16[384,384]{1,0:T(8,128)(2,1)S(1)}, bf16[384,384]{1,0:T(8,128)(2,1)S(1)}, u32[]{:S(2)}, u32[]{:S(2)}) collective-permute-start(bf16[384,384]{1,0:T(8,128)(2,1)S(1)} %pre_part.5), channel_id=1, source_target_pairs={{0,2},{2,4},{4,6},{6,0},{1,3},{3,5},{5,7},{7,1},{8,10},{10,12},{12... | collective-permute-start | bytes 884744 | tf_op jit(solution)/shard_map/ppermute | solution.py:29
  67.3 0.6 pre_part.6
  67.9 3.9 %collective-permute-start.6 = (bf16[384,384]{1,0:T(8,128)(2,1)S(1)}, bf16[384,384]{1,0:T(8,128)(2,1)S(1)}, u32[]{:S(2)}, u32[]{:S(2)}) collective-permute-start(bf16[384,384]{1,0:T(8,128)(2,1)S(1)} %pre_part.6), channel_id=1, source_target_pairs={{0,6},{2,0},{4,2},{6,4},{1,7},{3,1},{5,3},{7,5},{8,14},{10,8},{12,... | collective-permute-start | bytes 884744 | tf_op jit(solution)/shard_map/ppermute | solution.py:29
  71.9 0.0 copy-done
  71.9 0.0 copy-done.1
  71.9 0.6 pre_part.7
  72.5 0.5 collective-permute-done.4
  73.0 6.3 %collective-permute-done.5 = bf16[384,384]{1,0:T(8,128)(2,1)S(1)} collective-permute-done((bf16[384,384]{1,0:T(8,128)(2,1)S(1)}, bf16[384,384]{1,0:T(8,128)(2,1)S(1)}, u32[]{:S(2)}, u32[]{:S(2)}) %collective-permute-start.5) | collective-permute-done | bytes 294944 | tf_op jit(solution)/shard_map/ppermute | solution.py:29
  79.3 0.0 collective-permute-done.6
  79.3 0.1 convert_add_fusion
  79.5 0.2 multiply_convert_fusion.1
  79.8 15.3 %all-gather = bf16[1600,256]{1,0:T(8,128)(2,1)S(1)} all-gather(bf16[400,256]{1,0:T(8,128)(2,1)S(1)} %pad_maximum_fusion), channel_id=2, replica_groups=mesh['y'=8,'z'=8,'x'=4,'c'=2] {'x'}, dimensions={0}, use_global_device_ids=true | all-gather | bytes 1024000 | tf_op jit(solution)/shard_map/all_gather | solution.py:295
  95.2 0.0 copy-start.3
  95.2 1.1 copy-done.3
  96.4 0.0 copy-start.4
  96.4 1.1 input_grads_give.1
  97.5 1.9 %collective-permute-start.7 = (bf16[400,512]{1,0:T(8,128)(2,1)S(1)}, bf16[400,512]{1,0:T(8,128)(2,1)S(1)}, u32[]{:S(2)}, u32[]{:S(2)}) collective-permute-start(bf16[400,512]{1,0:T(8,128)(2,1)S(1)} %input_grads_give.1), channel_id=1, source_target_pairs={{0,1},{1,0},{2,3},{3,2},{4,5},{5,4},{6,7},{7,6},{8,9},{9,8},{10,11... | collective-permute-start | bytes 1228808 | tf_op jit(solution)/shard_map/ppermute | solution.py:25
  99.5 0.1 fusion.place_ref
  99.6 0.0 copy-done.4
  99.6 1.1 input_grads_keep.1.keep_ref
  100.7 0.4 collective-permute-done.7.came_ref
  101.2 0.5 rows_to_slots.1
  101.7 0.0 copy-start.5
  101.7 35.0 %all_to_all.24 = bf16[64,8,640]{2,1,0:T(8,128)(2,1)S(1)} all-to-all(bf16[64,8,640]{2,1,0:T(8,128)(2,1)S(1)} %bitcast.32), channel_id=1, replica_groups=mesh['y'=8,'z'=8,'x'=4,'c'=2] {'y','z'}, dimensions={0} | all-to-all | bytes 1310720 | tf_op jit(solution)/shard_map/all_to_all | solution.py:310
  136.8 0.1 reduce_sum.42
  136.8 0.6 slice_add_fusion
  137.4 0.0 copy-done.5
  137.5 1.0 convolution_convert_fusion.1
  (24 shorter events, 0.4 us)
Async XLA Ops:
  0.6 71.2 %copy-start = (f32[8,384]{1,0:T(8,128)S(1)}, f32[8,384]{1,0:T(8,128)}, u32[]{:S(2)}) copy-start(f32[8,384]{1,0:T(8,128)} %param.13) | copy-start | bytes 36868
  4.2 16.8 %copy-start.6 = (bf16[1536,256]{1,0:T(8,128)(2,1)S(1)}, bf16[1536,256]{1,0:T(8,128)(2,1)}, u32[]{:S(2)}) copy-start(bf16[1536,256]{1,0:T(8,128)(2,1)} %get-tuple-element.15) | copy-start | bytes 2359300
  4.2 47.2 %all-to-all-start = ((bf16[64,8,1024]{2,1,0:T(8,128)(2,1)}), bf16[64,8,1024]{2,1,0:T(8,128)(2,1)}, u32[]{:S(2)}, u32[]{:S(2)}) async-start(bf16[64,8,1024]{2,1,0:T(8,128)(2,1)} %bitcast.39), calls=%async_computation | async-start | bytes 2097152 | tf_op jit(solution)/shard_map/all_to_all | solution.py:259
  21.0 23.9 %collective-permute-start = (bf16[1536,256]{1,0:T(8,128)(2,1)S(1)}, bf16[1536,256]{1,0:T(8,128)(2,1)S(1)}, u32[]{:S(2)}, u32[]{:S(2)}) collective-permute-start(bf16[1536,256]{1,0:T(8,128)(2,1)S(1)} %copy-done.6), channel_id=1, source_target_pairs={{0,4},{2,6},{4,0},{6,2},{1,5},{3,7},{5,1},{7,3},{8,12},{10,14},{12... | collective-permute-start | bytes 2359304 | tf_op jit(solution)/shard_map/ppermute | solution.py:29
  29.7 30.4 %collective-permute-start.2 = (bf16[1536,256]{1,0:T(8,128)(2,1)}, bf16[1536,256]{1,0:T(8,128)(2,1)S(1)}, u32[]{:S(2)}, u32[]{:S(2)}) collective-permute-start(bf16[1536,256]{1,0:T(8,128)(2,1)} %get-tuple-element.17), channel_id=1, source_target_pairs={{0,2},{2,4},{4,6},{6,0},{1,3},{3,5},{5,7},{7,1},{8,10},{10,12},{12... | collective-permute-start | bytes 2359304 | tf_op jit(solution)/shard_map/ppermute | solution.py:29
  31.6 28.5 %collective-permute-start.3 = (bf16[1536,256]{1,0:T(8,128)(2,1)}, bf16[1536,256]{1,0:T(8,128)(2,1)S(1)}, u32[]{:S(2)}, u32[]{:S(2)}) collective-permute-start(bf16[1536,256]{1,0:T(8,128)(2,1)} %get-tuple-element.18), channel_id=1, source_target_pairs={{0,6},{2,0},{4,2},{6,4},{1,7},{3,1},{5,3},{7,5},{8,14},{10,8},{12,... | collective-permute-start | bytes 2359304 | tf_op jit(solution)/shard_map/ppermute | solution.py:29
  53.3 6.8 %collective-permute-start.1 = (bf16[384,1024]{1,0:T(8,128)(2,1)S(1)}, bf16[384,1024]{1,0:T(8,128)(2,1)S(1)}, u32[]{:S(2)}, u32[]{:S(2)}) collective-permute-start(bf16[384,1024]{1,0:T(8,128)(2,1)S(1)} %convolution_convert_fusion.own_ref), channel_id=1, source_target_pairs={{0,1},{1,0},{2,3},{3,2},{4,5},{5,4},{6,7},{7,6},{8,9},{9,8},{10,11... | collective-permute-start | bytes 2359304 | tf_op jit(solution)/shard_map/ppermute | solution.py:25
  60.1 4.6 %copy-start.2 = (bf16[1536,256]{1,0:T(8,128)(2,1)}, bf16[1536,256]{1,0:T(8,128)(2,1)S(1)}, u32[]{:S(2)}) copy-start(bf16[1536,256]{1,0:T(8,128)(2,1)S(1)} %collective-permute-done.3.w_ref.w3) | copy-start | bytes 2359300
  60.7 12.3 %collective-permute-start.4 = (bf16[384,384]{1,0:T(8,128)(2,1)S(1)}, bf16[384,384]{1,0:T(8,128)(2,1)S(1)}, u32[]{:S(2)}, u32[]{:S(2)}) collective-permute-start(bf16[384,384]{1,0:T(8,128)(2,1)S(1)} %pre_part.4), channel_id=1, source_target_pairs={{0,4},{2,6},{4,0},{6,2},{1,5},{3,7},{5,1},{7,3},{8,12},{10,14},{12... | collective-permute-start | bytes 884744 | tf_op jit(solution)/shard_map/ppermute | solution.py:29
  65.3 6.6 %copy-start.1 = (bf16[1536,256]{1,0:T(8,128)(2,1)S(1)}, bf16[1536,256]{1,0:T(8,128)(2,1)}, u32[]{:S(2)}) copy-start(bf16[1536,256]{1,0:T(8,128)(2,1)} %get-tuple-element.23.w_ref.w0) | copy-start | bytes 2359300
  65.3 14.1 %collective-permute-start.5 = (bf16[384,384]{1,0:T(8,128)(2,1)S(1)}, bf16[384,384]{1,0:T(8,128)(2,1)S(1)}, u32[]{:S(2)}, u32[]{:S(2)}) collective-permute-start(bf16[384,384]{1,0:T(8,128)(2,1)S(1)} %pre_part.5), channel_id=1, source_target_pairs={{0,2},{2,4},{4,6},{6,0},{1,3},{3,5},{5,7},{7,1},{8,10},{10,12},{12... | collective-permute-start | bytes 884744 | tf_op jit(solution)/shard_map/ppermute | solution.py:29
  67.9 11.4 %collective-permute-start.6 = (bf16[384,384]{1,0:T(8,128)(2,1)S(1)}, bf16[384,384]{1,0:T(8,128)(2,1)S(1)}, u32[]{:S(2)}, u32[]{:S(2)}) collective-permute-start(bf16[384,384]{1,0:T(8,128)(2,1)S(1)} %pre_part.6), channel_id=1, source_target_pairs={{0,6},{2,0},{4,2},{6,4},{1,7},{3,1},{5,3},{7,5},{8,14},{10,8},{12,... | collective-permute-start | bytes 884744 | tf_op jit(solution)/shard_map/ppermute | solution.py:29
  95.2 1.1 copy-start.3
  96.4 3.2 %copy-start.4 = (bf16[1536,256]{1,0:T(8,128)(2,1)S(1)}, bf16[1536,256]{1,0:T(8,128)(2,1)}, u32[]{:S(2)}) copy-start(bf16[1536,256]{1,0:T(8,128)(2,1)} %copy-done.2) | copy-start | bytes 2359300
  97.5 3.6 %collective-permute-start.7 = (bf16[400,512]{1,0:T(8,128)(2,1)S(1)}, bf16[400,512]{1,0:T(8,128)(2,1)S(1)}, u32[]{:S(2)}, u32[]{:S(2)}) collective-permute-start(bf16[400,512]{1,0:T(8,128)(2,1)S(1)} %input_grads_give.1), channel_id=1, source_target_pairs={{0,1},{1,0},{2,3},{3,2},{4,5},{5,4},{6,7},{7,6},{8,9},{9,8},{10,11... | collective-permute-start | bytes 1228808 | tf_op jit(solution)/shard_map/ppermute | solution.py:25
  101.7 35.7 %copy-start.5 = (bf16[64,192]{1,0:T(8,128)(2,1)S(1)}, bf16[64,192]{1,0:T(8,128)(2,1)}, u32[]{:S(2)}) copy-start(bf16[64,192]{1,0:T(8,128)(2,1)} %get-tuple-element.13) | copy-start | bytes 73732
